TPU v7x, 128 devices: a whole 4x4x4 slice. The times are simulated.
128 devices in a mesh: dp: 8 (over y, z_lo), seq: 16 (over x, z_hi, core).
Axes of the slice: x: 4, y: 4, z: 4 (z_hi: 2, z_lo: 2; z = z_hi * 2 + z_lo), core: 2. Of those that a mesh axis runs over, the one named last changes fastest.
Arguments:
- normed: bfloat16 [8, 4096, 1536], P('dp', 'seq'), may hold values from -12 to 12
- w_query: bfloat16 [1536, 768], replicated, may hold values from -0.15309311 to 0.15309311
- w_key: bfloat16 [1536, 768], replicated, may hold values from -0.15309311 to 0.15309311
- w_value: bfloat16 [1536, 768], replicated, may hold values from -0.15625 to 0.15625
- grad_context: bfloat16 [8, 4096, 768], P('dp', 'seq'), may hold values from -6 to 6
Outputs:
- d_normed: bfloat16 [8, 4096, 1536], P('dp', 'seq')
- grad_query: float32 [1536, 768], P(('dp', 'seq'))
- grad_key: float32 [1536, 768], P(('dp', 'seq'))
- grad_value: float32 [1536, 768], P(('dp', 'seq'))
All inputs are finite; a program needn't handle non-finite values.
Results may differ from a plain program's by a relative error of at most 0.017.
Values may be sent and summed in bfloat16 or wider, within the bound.
No kernel may reach another device: no remote copies, remote signals or barrier semaphores. Data moves between devices by JAX's collectives and lax.ppermute only.
A program may use at most 192 MiB of HBM per device.

v0:
```python
import math

import jax
import jax.numpy as jnp
from jax import lax
from jax.sharding import PartitionSpec as P

H = 4
E = 192


def project(rows, weight):
    return jnp.dot(rows, weight, preferred_element_type=jnp.float32).astype(jnp.bfloat16)


def rounded_sum(partials):
    return jnp.sum(partials.astype(jnp.bfloat16).astype(jnp.float32), axis=0).astype(jnp.bfloat16)


def shards(normed, w_query, w_key, w_value, grad_context):
    scale = 1.0 / math.sqrt(E)
    rows = normed[0]
    cot_rows = grad_context[0]
    local = rows.shape[0]
    parts = lax.axis_size("seq")
    total = local * parts
    width = H * E
    query = project(rows, w_query)
    key = project(rows, w_key)
    value = project(rows, w_value)
    key_all, value_all = (
        lax.all_gather(key, "seq", axis=0, tiled=True),
        lax.all_gather(value, "seq", axis=0, tiled=True),
    )
    query3 = query.reshape(local, H, E)
    cotan3 = cot_rows.reshape(local, H, E)
    key3 = key_all.reshape(total, H, E)
    value3 = value_all.reshape(total, H, E)
    scores = jnp.einsum("qhe,khe->hqk", query3, key3, preferred_element_type=jnp.float32) * scale
    probs = jax.nn.softmax(scores, axis=-1)
    dprob = jnp.einsum("qhe,khe->hqk", cotan3, value3, preferred_element_type=jnp.float32)
    delta = jnp.sum(probs * dprob, axis=-1, keepdims=True)
    dscore = (probs * (dprob - delta) * scale).astype(jnp.bfloat16)
    prob_b = probs.astype(jnp.bfloat16)
    dq_parts = jnp.einsum(
        "hqnk,nkhe->nqhe",
        dscore.reshape(H, local, parts, local),
        key3.reshape(parts, local, H, E),
        preferred_element_type=jnp.float32,
    )
    dq = rounded_sum(dq_parts).reshape(local, width)
    dk_term = jnp.einsum(
        "hqk,qhe->khe", dscore, query3, preferred_element_type=jnp.float32
    ).reshape(total, width)
    dv_term = jnp.einsum(
        "hqk,qhe->khe", prob_b, cotan3, preferred_element_type=jnp.float32
    ).reshape(total, width)
    dk_sum, dv_sum = (
        lax.psum_scatter(
            dk_term.astype(jnp.bfloat16), "seq", scatter_dimension=0, tiled=True
        ).astype(jnp.float32),
        lax.psum_scatter(
            dv_term.astype(jnp.bfloat16), "seq", scatter_dimension=0, tiled=True
        ).astype(jnp.float32),
    )
    dk = dk_sum.astype(jnp.bfloat16)
    dv = dv_sum.astype(jnp.bfloat16)
    back = jnp.einsum("qc,dc->qd", dq, w_query, preferred_element_type=jnp.float32)
    back = back + jnp.einsum("qc,dc->qd", dk, w_key, preferred_element_type=jnp.float32)
    back = back + jnp.einsum("qc,dc->qd", dv, w_value, preferred_element_type=jnp.float32)
    d_normed = back.astype(jnp.bfloat16).reshape(normed.shape)
    term_q = jnp.einsum("qd,qc->dc", rows, dq, preferred_element_type=jnp.float32)
    term_k = jnp.einsum("qd,qc->dc", rows, dk, preferred_element_type=jnp.float32)
    term_v = jnp.einsum("qd,qc->dc", rows, dv, preferred_element_type=jnp.float32)
    grad_q, grad_k, grad_v = (
        lax.psum_scatter(term_q, ("dp", "seq"), scatter_dimension=0, tiled=True),
        lax.psum_scatter(term_k, ("dp", "seq"), scatter_dimension=0, tiled=True),
        lax.psum_scatter(term_v, ("dp", "seq"), scatter_dimension=0, tiled=True),
    )
    return (d_normed, grad_q, grad_k, grad_v)


def solution(mesh):
    in_specs = (P("dp", "seq", None), P(), P(), P(), P("dp", "seq", None))
    out_specs = (
        P("dp", "seq", None),
        P(("dp", "seq"), None),
        P(("dp", "seq"), None),
        P(("dp", "seq"), None),
    )
    return jax.shard_map(shards, mesh=mesh, in_specs=in_specs, out_specs=out_specs, check_vma=False)
```

profile of v0, /device:TPU:1, one launch (start us, length us, event | category | flops | bytes accessed | tf_op | source)
XLA Modules:
  0.0 550.9 jit_solution(5175505379654169001)
XLA Ops:
  7.2 0.0 copy-start
  7.2 0.0 copy-start.1
  7.2 0.0 all-gather.3.cloned.1.call-start
  7.2 3.6 convolution_convert_fusion.3
  10.8 0.0 all-gather.3.cloned.1.call-update
  10.9 0.0 all-gather.5.cloned.1.call-start
  10.9 3.4 convolution_convert_fusion.1
  14.3 0.0 all-gather.5.cloned.1.call-update
  14.4 0.0 reduce-scatter.6.cloned.1.call-start
  14.4 0.0 copy-done
  14.4 0.0 copy-done.1
  14.4 1.5 convolution_convert_fusion.2
  16.0 1.2 copy.33
  17.1 1.9 copy.36
  19.1 59.8 %all-gather.3.cloned.1.call-done = bf16[4096,768]{1,0:T(8,128)(2,1)} async-done(((bf16[256,768]{1,0:T(8,128)(2,1)}), bf16[4096,768]{1,0:T(8,128)(2,1)}) %all-gather.3.cloned.1.call-update) | async-done | bytes 6291472 | tf_op jit(solution)/shard_map/all_gather | solution.py:32
  78.9 8.8 %copy.34 = bf16[4096,768]{0,1:T(8,128)(2,1)} copy(bf16[4096,768]{1,0:T(8,128)(2,1)} %all-gather.3.cloned.1.call-done) | data formatting | bytes 12582912 | tf_op jit(solution)/shard_map/all_gather | solution.py:32
  87.7 11.0 %fusion.36 = (f32[4,256]{1,0:T(4,128)S(1)}, f32[4,256,4096]{2,1,0:T(8,128)}) fusion(bf16[256,4,192]{0,2,1:T(8,128)(2,1)S(1)} %bitcast.88, bf16[4096,4,192]{0,2,1:T(8,128)(2,1)} %bitcast.84), kind=kOutput, calls=%fused_computation.44 | convolution fusion | flops 1623199744 | bytes 23465984 | tf_op jit(solution)/shard_map/sub | solution.py:40
  98.7 45.7 %all-gather.5.cloned.1.call-done = bf16[4096,768]{1,0:T(8,128)(2,1)} async-done(((bf16[256,768]{1,0:T(8,128)(2,1)}), bf16[4096,768]{1,0:T(8,128)(2,1)}) %all-gather.5.cloned.1.call-update) | async-done | bytes 6291472 | tf_op jit(solution)/shard_map/all_gather | solution.py:33
  144.3 8.8 %copy.35 = bf16[4096,768]{0,1:T(8,128)(2,1)} copy(bf16[4096,768]{1,0:T(8,128)(2,1)} %all-gather.5.cloned.1.call-done) | data formatting | bytes 12582912 | tf_op jit(solution)/shard_map/all_gather | solution.py:33
  153.1 21.9 %fusion.4 = bf16[4,256,4096]{2,1,0:T(8,128)(2,1)} fusion(bf16[4096,4,192]{0,2,1:T(8,128)(2,1)} %bitcast.85, bf16[256,4,192]{0,2,1:T(8,128)(2,1)} %bitcast.90, f32[4,256,4096]{2,1,0:T(8,128)} %get-tuple-element.20, f32[4,256]{1,0:T(4,128)S(1)} %get-tuple-element.19), kind=kOutput, calls=%fused_computation.6 | convolution fusion | flops 3250590720 | bytes 31854592 | tf_op jit(solution)/shard_map/sub | solution.py:43
  175.0 7.9 %convolution_convert_fusion = bf16[4,192,4096]{2,1,0:T(8,128)(2,1)} fusion(bf16[256,4,192]{0,2,1:T(8,128)(2,1)S(1)} %bitcast.89, bf16[4,256,4096]{2,1,0:T(8,128)(2,1)} %fusion.4), kind=kOutput, calls=%fused_computation.20 | convolution fusion | flops 1613758464 | bytes 15073280 | tf_op jit(solution)/shard_map/hqk,qhe->khe/dot_general | solution.py:52
  182.9 0.0 reduce-scatter.6.cloned.1.call-update
  182.9 0.0 reduce-scatter.8.cloned.1.call-start
  183.0 0.9 copy-done.5
  183.9 10.5 %fusion.16 = bf16[4,4096,192]{1,2,0:T(8,128)(2,1)} fusion(bf16[256,4,192]{0,2,1:T(8,128)(2,1)S(1)} %bitcast.91, f32[4,256,4096]{2,1,0:T(8,128)} %get-tuple-element.20, f32[4,256]{1,0:T(4,128)S(1)} %get-tuple-element.19), kind=kOutput, calls=%fused_computation.19 | convolution fusion | flops 1622147072 | bytes 23465984 | tf_op jit(solution)/shard_map/hqk,qhe->khe/dot_general | solution.py:55
  194.5 0.0 reduce-scatter.8.cloned.1.call-update
  194.5 0.2 all-reduce.6.cloned.1.call-start
  194.7 17.0 %reshape.39 = bf16[16,256,4,192]{3,2,1,0:T(4,128)(2,1)} reshape(bf16[4096,768]{1,0:T(8,128)(2,1)} %all-gather.3.cloned.1.call-done) | data formatting | bytes 12582912 | tf_op jit(solution)/shard_map/reshape;reshape | solution.py:48
  211.7 10.3 %convert_reduce_fusion = bf16[4,192,256]{2,1,0:T(8,128)(2,1)S(1)} fusion(bf16[4,32,16,8,256]{4,3,2,1,0:T(8,128)(2,1)} %bitcast.82, bf16[16,256,4,192]{3,2,1,0:T(4,128)(2,1)} %reshape.39), kind=kOutput, calls=%fused_computation.21 | convolution fusion | flops 1616707584 | bytes 15073280 | tf_op jit(solution)/shard_map/hqnk,nkhe->nqhe/dot_general | solution.py:45
  222.0 2.9 convolution_bitcast_fusion.2
  224.9 44.3 %reduce-scatter.6.cloned.1.call-done = bf16[256,768]{0,1:T(8,128)(2,1)} async-done(((bf16[4096,768]{0,1:T(8,128)(2,1)}), bf16[256,768]{0,1:T(8,128)(2,1)}) %reduce-scatter.6.cloned.1.call-update) | async-done | bytes 393232 | tf_op jit(solution)/shard_map/reduce_scatter | solution.py:59
  269.3 3.9 convolution_bitcast_fusion.1
  273.2 88.3 %reduce-scatter.8.cloned.1.call-done = bf16[256,768]{0,1:T(8,128)(2,1)} async-done(((bf16[4096,768]{0,1:T(8,128)(2,1)}), bf16[256,768]{0,1:T(8,128)(2,1)}) %reduce-scatter.8.cloned.1.call-update) | async-done | bytes 393232 | tf_op jit(solution)/shard_map/reduce_scatter | solution.py:62
  361.5 4.0 convolution_bitcast_fusion
  365.5 0.0 all-reduce.6.cloned.1.call-update
  365.6 0.0 copy-start.3
  365.6 0.0 copy-start.4
  365.6 0.8 fusion.37
  366.4 0.1 copy-done.2
  366.5 2.5 convolution_add_fusion.1
  369.1 0.0 copy-done.3
  369.1 1.7 fusion.24
  370.8 168.2 %all-reduce.6.cloned.1.call-done = (f32[1536,768]{0,1:T(8,128)}, f32[1536,768]{0,1:T(8,128)}, f32[1536,768]{0,1:T(8,128)}) async-done(((f32[1536,768]{0,1:T(8,128)}, f32[1536,768]{0,1:T(8,128)}, f32[1536,768]{0,1:T(8,128)}), (f32[1536,768]{0,1:T(8,128)}, f32[1536,768]{0,1:T(8,128)}, f32[1536,768]{0,1:T(8,128)})) %all-reduce.6.cloned.1.call-update) | async-done | bytes 14155792
  539.1 1.6 constant_dynamic-slice_fusion
  540.7 0.8 copy.41
  541.5 0.8 copy.42
  542.3 1.3 constant_dynamic-slice_fusion.2
  543.6 0.8 copy.40
  (3 shorter events, 0.0 us)
Async XLA Ops:
  7.2 7.3 %copy-start = (bf16[1536,768]{1,0:T(8,128)(2,1)S(1)}, bf16[1536,768]{1,0:T(8,128)(2,1)}, u32[]{:S(2)}) copy-start(bf16[1536,768]{1,0:T(8,128)(2,1)} %param.6) | copy-start | bytes 7077892
  7.2 7.3 %copy-start.1 = (bf16[1,256,1536]{2,1,0:T(8,128)(2,1)S(1)}, bf16[1,256,1536]{2,1,0:T(8,128)(2,1)}, u32[]{:S(2)}) copy-start(bf16[1,256,1536]{2,1,0:T(8,128)(2,1)} %param.5) | copy-start | bytes 2359300
  7.2 71.7 %all-gather.3.cloned.1.call-start = ((), (), s32[]{:S(2)}) async-start(), calls=%async_computation.2 | async-start | bytes 6684672 | tf_op jit(solution)/shard_map/all_gather | solution.py:32
  10.9 133.5 %all-gather.5.cloned.1.call-start = ((), (), s32[]{:S(2)}) async-start(), calls=%async_computation.3 | async-start | bytes 6684672 | tf_op jit(solution)/shard_map/all_gather | solution.py:33
  14.4 254.9 %reduce-scatter.6.cloned.1.call-start = ((), (), s32[]{:S(2)}) async-start(), calls=%async_computation.4 | async-start | bytes 6684672 | tf_op jit(solution)/shard_map/reduce_scatter | solution.py:59
  182.9 1.0 copy-start.5
  182.9 178.6 %reduce-scatter.8.cloned.1.call-start = ((), (), s32[]{:S(2)}) async-start(), calls=%async_computation.5 | async-start | bytes 6684672 | tf_op jit(solution)/shard_map/reduce_scatter | solution.py:62
  194.5 344.6 %all-reduce.6.cloned.1.call-start = ((), (), s32[]{:S(2)}) async-start(), calls=%async_computation.6 | async-start | bytes 28311552
  365.5 1.0 copy-start.2
  365.6 3.5 copy-start.3
  365.6 3.5 copy-start.4
Sparse Core Ops, SparseCore 0:
  11.0 67.8 all-gather.2
  81.8 62.4 all-gather.4
  183.1 86.1 reduce-scatter.5
  273.3 88.2 reduce-scatter.7
  366.8 172.2 all-reduce.5
where the time goes:
time: 552 us; the launch traced here: 551 us
  waiting for transfers between devices  406 us (74%)
  matrix products  86.1 us (16%)
  local copies, waits for them, and re-layouts  44 us (8%)
  between operations  13.9 us (3%)
    unnamed x6, waiting for transfers between devices  168 us
    reduce_scatter x1, waiting for transfers between devices, shards(): lax.psum_scatter(dv_term.astype(jnp.bfloat16), 'seq', scatter_dimension=0...  88.3 us
    all_gather x1, waiting for transfers between devices, shards(): lax.all_gather(key, 'seq', axis=0, tiled=True)  59.8 us
    all_gather x1, waiting for transfers between devices, shards(): lax.all_gather(value, 'seq', axis=0, tiled=True)  45.7 us
    reduce_scatter x1, waiting for transfers between devices, shards(): lax.psum_scatter(dk_term.astype(jnp.bfloat16), 'seq', scatter_dimension=0...  44.3 us
    sub x1, matrix products, shards(): dscore = (probs * (dprob - delta) * scale).astype(jnp.bfloat16)  21.9 us
    another operation x1, local copies, waits for them, and re-layouts, shards(): key3.reshape(parts, local, H, E)  17 us
  transfers between devices with their start and end apart: 5, of which 5 were waited for; matrix products, arithmetic and copies ran while one was open for 14% of the time, Pallas kernels for 0%

commit v1 on v0

v1 whole, which is shorter than its diff:
```python
import functools
import math

import jax
import jax.numpy as jnp
from jax import lax
from jax.experimental import pallas as pl
from jax.experimental.pallas import tpu as pltpu
from jax.sharding import Mesh, PartitionSpec as P

F32, BF16 = jnp.float32, jnp.bfloat16
D = 1536
H = 4
E = 192
HD = H * E
NB = 256
NQ = 4 * NB
NK = 16 * NB
KC = 512
SCALE = 1.0 / math.sqrt(E)
C2 = SCALE * math.log2(math.e)
ANY = pl.BlockSpec(memory_space=pl.ANY)
VM = pl.BlockSpec(memory_space=pltpu.VMEM)
SM = pl.BlockSpec(memory_space=pltpu.SMEM)
PARAMS = pltpu.CompilerParams(vmem_limit_bytes=56 * 2**20)
sds = jax.ShapeDtypeStruct


def dot(a, b, dims=(((1,), (0,)), ((), ()))):
    return lax.dot_general(a, b, dims, preferred_element_type=F32)


def nt(a, b):
    return dot(a, b, (((1,), (1,)), ((), ())))


def joined(a, b):
    return jnp.concatenate([a[:, :128], a[:, 128:] + b[:, :128], b[:, 128:]], 1)


def scatter_heads(me, a, b, outs):
    for h in range(H):
        piece = jnp.concatenate([a[:, h * E:(h + 1) * E], b[:, h * E:(h + 1) * E]], 1)
        slot = lax.rem(h - me + H, H)
        for j in range(H):
            @pl.when(slot == j)
            def _(j=j, piece=piece):
                outs[j][...] = piece


KP = D // 4


def projkv_body(me, x, wk, wv, o0, o1, o2, o3, wks, wvs, sem):
    cps = []
    for i in range(4):
        r = pl.ds(i * KP, KP)
        cps.append((pltpu.make_async_copy(wk.at[r], wks.at[r], sem.at[i]),
                    pltpu.make_async_copy(wv.at[r], wvs.at[r], sem.at[4 + i])))
    for a, b in cps:
        a.start()
        b.start()
    k = v = None
    for i in range(4):
        for c in cps[i]:
            c.wait()
        r = pl.ds(i * KP, KP)
        xi = x[:, r]
        dk, dv = dot(xi, wks[r, :]), dot(xi, wvs[r, :])
        k, v = (dk, dv) if i == 0 else (k + dk, v + dv)
    scatter_heads(me[0], k.astype(BF16), v.astype(BF16), (o0, o1, o2, o3))


def projkv(me, x, wk, wv):
    return pl.pallas_call(
        projkv_body, in_specs=[SM, VM, ANY, ANY], out_specs=[VM] * 4,
        out_shape=[sds((NB, 2 * E), BF16)] * 4,
        scratch_shapes=[pltpu.VMEM((D, HD), BF16), pltpu.VMEM((D, HD), BF16),
                        pltpu.SemaphoreType.DMA((8,))],
        compiler_params=PARAMS, name="projkv",
        cost_estimate=pl.CostEstimate(flops=4 * NB * D * HD, bytes_accessed=6 * 2**20, transcendentals=0),
    )(me, x, wk, wv)


def projq_body(me, x, wq, do, o0, o1, o2, o3, wqs, sem):
    cps = []
    for i in range(4):
        r = pl.ds(i * KP, KP)
        cps.append(pltpu.make_async_copy(wq.at[r], wqs.at[r], sem.at[i]))
        cps[i].start()
    q = None
    for i in range(4):
        cps[i].wait()
        r = pl.ds(i * KP, KP)
        dq = dot(x[:, r], wqs[r, :])
        q = dq if i == 0 else q + dq
    scatter_heads(me[0], q.astype(BF16), do[...], (o0, o1, o2, o3))


def projq(me, x, wq, do):
    return pl.pallas_call(
        projq_body, in_specs=[SM, VM, ANY, VM], out_specs=[VM] * 4,
        out_shape=[sds((NB, 2 * E), BF16)] * 4,
        scratch_shapes=[pltpu.VMEM((D, HD), BF16), pltpu.SemaphoreType.DMA((4,))],
        compiler_params=PARAMS, name="projq",
        cost_estimate=pl.CostEstimate(flops=2 * NB * D * HD, bytes_accessed=4 * 2**20, transcendentals=0),
    )(me, x, wq, do)

def attn1_body(*refs):
    kv_in=refs[:16]; qdo_in=refs[16:20]
    rsame, rother, p_out, ds_out, qs_out, dos_out, cq_out, kv_out = refs[20:28]
    kv, qdo, qT, doT, s_scr, dp_scr, p_scr, ds_scr, qs, dos, sem, osem = refs[28:]
    cps=[]
    for i in range(4):
        cps.append(pltpu.make_async_copy(qdo_in[i], qdo.at[pl.ds(256*i,256)], sem.at[i]))
    for i in range(16):
        cps.append(pltpu.make_async_copy(kv_in[i], kv.at[pl.ds(256*i,256)], sem.at[4+i]))
    for c in cps: c.start()
    for c in cps: c.wait()
    kvo=pltpu.make_async_copy(kv, kv_out, osem.at[9]); kvo.start()
    lane=lax.broadcasted_iota(jnp.int32,(256,NQ),0)
    x=qdo[...]
    xT=x.T
    qT[...]=jnp.concatenate([xT[:192], jnp.zeros((64,NQ),BF16)],0)
    doT[...]=jnp.concatenate([jnp.zeros((64,NQ),BF16), xT[192:]],0)
    outs=[]
    NC=NK//KC
    for t in range(4):
        qcol=pl.ds(256*t,256)
        qTt=qT[:,qcol]; doTt=doT[:,qcol]
        def pa(i,m):
            r=pl.ds(pl.multiple_of(i*KC,KC),KC)
            s=dot(kv[r,0:256],qTt)
            s_scr[r,:]=s
            return jnp.maximum(m, jnp.max(s.reshape(KC//8,8,256),axis=0))
        m8=lax.fori_loop(0,NC,pa,jnp.full((8,256),-jnp.inf,F32))
        mc=jnp.max(m8,axis=0,keepdims=True)*C2
        def pb(i,lr):
            l,r_=lr
            r=pl.ds(pl.multiple_of(i*KC,KC),KC)
            dp=dot(kv[r,128:384],doTt)
            p=jnp.exp2(s_scr[r,:]*C2-mc)
            dp_scr[r,:]=dp
            s_scr[r,:]=p
            p_scr[r,qcol]=p.astype(BF16)
            l=l+jnp.sum(p.reshape(KC//8,8,256),axis=0)
            r_=r_+jnp.sum((p*dp).reshape(KC//8,8,256),axis=0)
            return l,r_
        z=jnp.zeros((8,256),F32)
        l8,r8=lax.fori_loop(0,NC,pb,(z,z))
        l=jnp.sum(l8,axis=0,keepdims=True); rr=jnp.sum(r8,axis=0,keepdims=True)
        inv=1.0/l
        delta=rr*inv
        def pc(i,_):
            r=pl.ds(pl.multiple_of(i*KC,KC),KC)
            ds_scr[r,qcol]=(s_scr[r,:]*(dp_scr[r,:]-delta)).astype(BF16)
            return 0
        lax.fori_loop(0,NC,pc,0)
        cq=inv*SCALE
        cq_out[:,qcol]=jnp.broadcast_to(cq,(8,256))
        invc=jnp.broadcast_to(inv,(8,256)).T[:,0:1]
        rows=pl.ds(256*t,256)
        qt=qdo[rows,0:192].astype(F32)*(invc*SCALE)
        dt=qdo[rows,192:384].astype(F32)*invc
        zz=jnp.zeros((256,64),BF16)
        qs[rows,:]=jnp.concatenate([qt.astype(BF16),zz],1)
        dos[rows,:]=jnp.concatenate([zz,dt.astype(BF16)],1)
        o1=pltpu.make_async_copy(ds_scr.at[:,qcol], ds_out.at[:,qcol], osem.at[t]); o1.start()
        o2=pltpu.make_async_copy(p_scr.at[pl.ds(0,2048),qcol], p_out.at[:,qcol], osem.at[4+t]); o2.start()
        outs+= [o1,o2]
    qs_out[...]=qs[...]; dos_out[...]=dos[...]
    for i in range(4):
        r=pl.ds(2048+i*512,512)
        a=dot(ds_scr[r,:],qs[...]); b=dot(p_scr[r,:],dos[...])
        o=jnp.concatenate([a[:,:128],a[:,128:]+b[:,:128],b[:,128:]],1)
        if i<2: rsame[pl.ds(i*512,512),:]=o
        else: rother[pl.ds((i-2)*512,512),:]=o.astype(BF16)
    for o in outs: o.wait()
    kvo.wait()

def attn1(kvp,qdop):
    A, V = ANY, VM
    return pl.pallas_call(attn1_body,
      in_specs=[A]*20,
      out_specs=[V,V,A,A,V,V,V,A],
      out_shape=[sds((1024,384),F32),sds((1024,384),BF16),sds((2048,NQ),BF16),sds((NK,NQ),BF16),sds((NQ,256),BF16),sds((NQ,256),BF16),sds((8,NQ),F32),sds((NK,384),BF16)],
      scratch_shapes=[pltpu.VMEM((NK,384),BF16),pltpu.VMEM((NQ,384),BF16),pltpu.VMEM((256,NQ),BF16),pltpu.VMEM((256,NQ),BF16),
        pltpu.VMEM((NK,256),F32),pltpu.VMEM((NK,256),F32),pltpu.VMEM((NK,NQ),BF16),pltpu.VMEM((NK,NQ),BF16),pltpu.VMEM((NQ,256),BF16),pltpu.VMEM((NQ,256),BF16),
        pltpu.SemaphoreType.DMA((20,)),pltpu.SemaphoreType.DMA((10,))],
      compiler_params=PARAMS,
      name="attn1", cost_estimate=pl.CostEstimate(flops=20*2**30, bytes_accessed=20*2**20, transcendentals=4*2**20),
    )(*kvp,*qdop)

def attn2_body(p_in, ds_in, qs, dos, cq, kv_in, lsame, lother, d0, d1, d2, d3, kv, p, ds, sem):
    cps=[pltpu.make_async_copy(p_in.at[pl.ds(512*i,512)],p.at[pl.ds(512*i,512)],sem.at[i]) for i in range(4)]
    cds=[pltpu.make_async_copy(ds_in.at[pl.ds(512*i,512)],ds.at[pl.ds(512*i,512)],sem.at[4+i]) for i in range(8)]
    ck=pltpu.make_async_copy(kv_in,kv,sem.at[12])
    for i in range(4): cds[i].start(); cps[i].start()
    ck.start()
    for i in range(4,8): cds[i].start()
    for i in (2,3,0,1):
        cds[i].wait(); cps[i].wait()
        r=pl.ds(i*512,512)
        a=dot(ds[r,:],qs[...]); b=dot(p[r,:],dos[...])
        o=jnp.concatenate([a[:,:128],a[:,128:]+b[:,:128],b[:,128:]],1)
        if i<2: lsame[pl.ds(i*512,512),:]=o
        else: lother[pl.ds((i-2)*512,512),:]=o.astype(BF16)
    ck.wait()
    for i in range(4,8): cds[i].wait()
    acc=jnp.zeros((256,NQ),F32)
    for i in range(4):
        r=pl.ds(i*1024,1024)
        kT=kv[r,0:256].T
        acc=acc+dot(kT,ds[r,:])
    dqT=(acc*cq[0:1,:]).astype(BF16)[:192]
    for j, o in enumerate((d0, d1, d2, d3)):
        o[...]=dqT[:, j*NB:(j+1)*NB]

def attn2(p,ds,qs,dos,cq,kv):
    A, V = ANY, VM
    return pl.pallas_call(attn2_body,
      in_specs=[A,A,V,V,V,A], out_specs=[V]*6,
      out_shape=[sds((1024,384),F32),sds((1024,384),BF16),*[sds((E,NB),BF16)]*4],
      scratch_shapes=[pltpu.VMEM((NK,384),BF16),pltpu.VMEM((2048,NQ),BF16),pltpu.VMEM((NK,NQ),BF16),pltpu.SemaphoreType.DMA((13,))],
      compiler_params=PARAMS,
      name="attn2", cost_estimate=pl.CostEstimate(flops=8*2**30, bytes_accessed=16*2**20, transcendentals=0),
    )(p,ds,qs,dos,cq,kv)


def gq_body(core, d0, d1, d2, d3, x0, x1, x2, x3, mine, other):
    acc = None
    c = core[0]
    for d, x in ((d0, x0), (d1, x1), (d2, x2), (d3, x3)):
        g = dot(d[...], x[...])
        acc = g if acc is None else acc + g
    half = E // 2
    for k in range(2):
        @pl.when(c == k)
        def _(k=k):
            mine[...] = acc[k * half:(k + 1) * half]
            other[...] = acc[(1 - k) * half:(2 - k) * half].astype(BF16)


def gq(core, ds, xs):
    return pl.pallas_call(
        gq_body, in_specs=[SM] + [VM] * 8, out_specs=[VM] * 2,
        out_shape=[sds((E // 2, D), F32), sds((E // 2, D), BF16)],
        compiler_params=PARAMS, name="gq",
        cost_estimate=pl.CostEstimate(flops=2 * NQ * D * E, bytes_accessed=5 * 2**20, transcendentals=0),
    )(core, *ds, *xs)


def comb_body(a, t, u, o0, o1, o2, o3):
    for j, o in enumerate((o0, o1, o2, o3)):
        r = pl.ds(j * NB, NB)
        o[...] = (a[r, :] + t[r, :].astype(F32) + u[r, :].astype(F32)).astype(BF16)


def comb(a, t, u):
    return pl.pallas_call(
        comb_body, in_specs=[VM] * 3, out_specs=[VM] * 4, out_shape=[sds((NB, 2 * E), BF16)] * 4,
        compiler_params=PARAMS, name="comb",
        cost_estimate=pl.CostEstimate(flops=2**20, bytes_accessed=4 * 2**20, transcendentals=0),
    )(a, t, u)


def gkv_body(core, d0, d1, d2, d3, x0, x1, x2, x3, mine, other):
    acc = None
    c = core[0]
    for d, x in ((d0, x0), (d1, x1), (d2, x2), (d3, x3)):
        g = dot(d[...].T, x[...])
        acc = g if acc is None else acc + g
    for k in range(2):
        @pl.when(c == k)
        def _(k=k):
            mine[...] = acc[k * E:(k + 1) * E]
            other[...] = acc[(1 - k) * E:(2 - k) * E].astype(BF16)


def gkv(core, ds, xs):
    return pl.pallas_call(
        gkv_body, in_specs=[SM] + [VM] * 8, out_specs=[VM] * 2,
        out_shape=[sds((E, D), F32), sds((E, D), BF16)],
        compiler_params=PARAMS, name="gkv",
        cost_estimate=pl.CostEstimate(flops=4 * NQ * D * E, bytes_accessed=6 * 2**20, transcendentals=0),
    )(core, *ds, *xs)


def split_body(me, a, t, o0, o1, o2, o3):
    w = D // 4
    for j, o in enumerate((o0, o1, o2, o3)):
        at = pl.multiple_of(lax.rem(me[0] + j, 4) * w, 128)
        o[...] = (a[:, pl.ds(at, w)] + t[:, pl.ds(at, w)].astype(F32)).astype(BF16)


def split(me, a, t):
    n = a.shape[0]
    return pl.pallas_call(
        split_body, in_specs=[SM, VM, VM], out_specs=[VM] * 4, out_shape=[sds((n, D // 4), BF16)] * 4,
        compiler_params=PARAMS, name="split",
        cost_estimate=pl.CostEstimate(flops=2**20, bytes_accessed=2 * 2**20, transcendentals=0),
    )(me, a, t)


def back_body(me, q0, q1, q2, q3, p0, p1, p2, p3, wq, wk, wv, out, dqT, dk, dv, wqs, wks, wvs, sem):
    cps = [pltpu.make_async_copy(a, b, sem.at[i]) for i, (a, b) in enumerate(((wq, wqs), (wk, wks), (wv, wvs)))]
    for c in cps:
        c.start()
    m = me[0]
    for j, (q, p) in enumerate(((q0, p0), (q1, p1), (q2, p2), (q3, p3))):
        h = lax.rem(m + j, H)
        dqT[pl.ds(pl.multiple_of(h * E, E), E), :] = q[...]
        for k in range(H):
            @pl.when(h == k)
            def _(k=k, p=p):
                dk[:, k * E:(k + 1) * E] = p[:, :E]
                dv[:, k * E:(k + 1) * E] = p[:, E:]
    cps[0].wait()
    acc = nt(dqT[...].T, wqs[...])
    cps[1].wait()
    acc = acc + nt(dk[...], wks[...])
    cps[2].wait()
    acc = acc + nt(dv[...], wvs[...])
    out[...] = acc.astype(BF16)


def back(me, qs, ps, wq, wk, wv):
    return pl.pallas_call(
        back_body, in_specs=[SM] + [VM] * 8 + [ANY] * 3, out_specs=VM, out_shape=sds((NB, D), BF16),
        scratch_shapes=[pltpu.VMEM((HD, NB), BF16), pltpu.VMEM((NB, HD), BF16), pltpu.VMEM((NB, HD), BF16)]
        + [pltpu.VMEM((D, HD), BF16)] * 3 + [pltpu.SemaphoreType.DMA((3,))],
        compiler_params=PARAMS, name="back",
        cost_estimate=pl.CostEstimate(flops=6 * NB * D * HD, bytes_accessed=9 * 2**20, transcendentals=0),
    )(me, *qs, *ps, wq, wk, wv)


def ahead(x, axis, j, n):
    return lax.ppermute(x, axis, [(i, (i + j) % n) for i in range(n)])


def shards(normed, w_query, w_key, w_value, grad_context):
    rows = normed[0]
    cot = grad_context[0]
    mx = lax.axis_index("x").reshape(1)
    my = lax.axis_index("y").reshape(1)
    mc = lax.axis_index("c").reshape(1)
    kv = projkv(mx, rows, w_key, w_value)
    kv = [kv[0]] + [ahead(kv[j], "x", j, 4) for j in (1, 2, 3)]
    qdo = projq(mx, rows, w_query, cot)
    qdo = [qdo[0]] + [ahead(qdo[j], "x", j, 4) for j in (1, 2, 3)]
    rows2, _ = lax.optimization_barrier((rows, tuple(qdo[1:])))
    xs = [rows] + [ahead(rows2, "x", j, 4) for j in (1, 2, 3)]
    far = [ahead(p, "zh", 1, 2) for p in kv]
    near = [ahead(p, "c", 1, 2) for p in kv]
    diag = [ahead(p, "c", 1, 2) for p in far]
    rsame, rother, p, ds, qs, dos, cq, kvh = attn1(kv + near + far + diag, qdo)
    t = ahead(rother, "c", 1, 2)
    u = ahead((rsame + t.astype(F32)).astype(BF16), "zh", 1, 2)
    lsame, lother, *dqT = attn2(p, ds, qs, dos, cq, kvh)
    t2 = ahead(lother, "c", 1, 2)
    backq = [dqT[0]] + [ahead(dqT[j], "x", 4 - j, 4) for j in (1, 2, 3)]
    gqm, gqo = gq(mc, dqT, xs)
    q4 = split(my, gqm, ahead(gqo, "c", 1, 2))
    q4 = [q4[0]] + [ahead(q4[j], "y", j, 4) for j in (1, 2, 3)]
    dkv = comb(lsame, t2, u)
    backp = [dkv[0]] + [ahead(dkv[j], "x", 4 - j, 4) for j in (1, 2, 3)]
    gm, go = gkv(mc, dkv, xs)
    s4 = split(my, gm, ahead(go, "c", 1, 2))
    s4 = [s4[0]] + [ahead(s4[j], "y", j, 4) for j in (1, 2, 3)]
    d_normed = back(mx, backq, backp, w_query, w_key, w_value).reshape(normed.shape)
    sq = (q4[0].astype(F32) + q4[1].astype(F32)) + (q4[2].astype(F32) + q4[3].astype(F32))
    skv = (s4[0].astype(F32) + s4[1].astype(F32)) + (s4[2].astype(F32) + s4[3].astype(F32))
    s = jnp.concatenate([skv, sq], 0).astype(BF16)
    s = s.T.reshape(32, 12, 288)
    s = lax.all_to_all(s, ("zl", "x", "zh", "c"), 0, 0, tiled=True)
    s = s.astype(F32).reshape(2, 4, 2, 2, 12, 288).sum(axis=(0, 2))
    g = s.transpose(2, 0, 1, 3)
    grad_q = g[..., E:].reshape(12, HD)
    grad_k = g[:, :, 0, :E].reshape(12, HD)
    grad_v = g[:, :, 1, :E].reshape(12, HD)
    return d_normed, grad_q, grad_k, grad_v


def solution(mesh):
    split_mesh = Mesh(mesh.devices.reshape(4, 2, 4, 2, 2), ("y", "zl", "x", "zh", "c"))
    dp, seq = ("y", "zl"), ("x", "zh", "c")
    rows = P(dp, seq, None)
    grads = P(dp + seq, None)
    return jax.shard_map(
        shards, mesh=split_mesh, in_specs=(rows, P(), P(), P(), rows),
        out_specs=(rows, grads, grads, grads), check_vma=False,
    )
```

time: 552 us -> 184 us (0.33)
  waiting for transfers between devices: 406 us -> 51.2 us
  matrix products: 86.1 us -> 0 us
  Pallas kernels: 0 us -> 69.3 us
  starting transfers between devices: 0.39 us -> 51 us
  local copies, waits for them, and re-layouts: 44 us -> 8.26 us
  between operations: 13.9 us -> 1.09 us
    unnamed x6 -> x0, waiting for transfers between devices: 168 us -> none
    reduce_scatter x2 -> x0, waiting for transfers between devices: 133 us -> none  [the longest x1 88.3 us: shards(): lax.psum_scatter(dv_term.astype(jnp.bfloat16), 'seq', scatter_dimension=0...]
    all_gather x2 -> x0, waiting for transfers between devices: 105 us -> none  [the longest x1 59.8 us: shards(): lax.all_gather(key, 'seq', axis=0, tiled=True)]
    pallas_call x0 -> x10, Pallas kernels: none -> 69.3 us  [the longest x1 25.7 us: attn1(): pl.pallas_call(attn1_body, in_specs=[A] * 20, out_specs=[V, V, A, A, V, V...]
    dot_general x12 -> x0, matrix products: 53.2 us -> none  [the longest x1 10.5 us: shards(): jnp.einsum('hqk,qhe->khe', prob_b, cotan3, preferred_element_type=jnp.flo...]
    ppermute x0 -> x38, waiting for transfers between devices: none -> 49.2 us  [ahead(): return lax.ppermute(x, axis, [(i, (i + j) % n) for i in range(n)])]
    ppermute x0 -> x38, starting transfers between devices: none -> 41 us  [ahead(): return lax.ppermute(x, axis, [(i, (i + j) % n) for i in range(n)])]
    sub x2 -> x0, matrix products: 32.9 us -> none  [the longest x1 21.9 us: shards(): dscore = (probs * (dprob - delta) * scale).astype(jnp.bfloat16)]
  transfers between devices with their start and end apart: 5 -> 39, of which waited for: 5 -> 12; matrix products, arithmetic and copies ran while one was open for 14% -> 2% of each run, Pallas kernels for 0% -> 18%
where the time goes in v1:
time: 184 us; the launch traced here: 183 us
  Pallas kernels  69.3 us (38%)
  waiting for transfers between devices  51.2 us (28%)
  starting transfers between devices  51 us (28%)
  local copies, waits for them, and re-layouts  8.26 us (4%)
  other arithmetic  2.17 us (1%)
    ppermute x38, waiting for transfers between devices, ahead(): return lax.ppermute(x, axis, [(i, (i + j) % n) for i in range(n)])  49.2 us
    ppermute x38, starting transfers between devices, ahead(): return lax.ppermute(x, axis, [(i, (i + j) % n) for i in range(n)])  41 us
    pallas_call x1, Pallas kernels, attn1(): pl.pallas_call(attn1_body, in_specs=[A] * 20, out_specs=[V, V, A, A, V, V...  25.7 us
    pallas_call x1, Pallas kernels, attn2(): pl.pallas_call(attn2_body, in_specs=[A, A, V, V, V, A], out_specs=[V] * 6...  10.1 us
    all_to_all x1, starting transfers between devices, shards(): s = lax.all_to_all(s, ('zl', 'x', 'zh', 'c'), 0, 0, tiled=True)  9.96 us
    pallas_call x1, Pallas kernels, back(): pl.pallas_call(back_body, in_specs=[SM] + [VM] * 8 + [ANY] * 3, out_specs...  6.72 us
    pallas_call x1, Pallas kernels, projkv(): pl.pallas_call(projkv_body, in_specs=[SM, VM, ANY, ANY], out_specs=[VM] *...  5.94 us
    pallas_call x1, Pallas kernels, projq(): pl.pallas_call(projq_body, in_specs=[SM, VM, ANY, VM], out_specs=[VM] * 4...  5.02 us
  transfers between devices with their start and end apart: 39, of which 12 were waited for; matrix products, arithmetic and copies ran while one was open for 2% of the time, Pallas kernels for 18%

profile of v1, /device:TPU:1, one launch (start us, length us, event | category | flops | bytes accessed | tf_op | source)
XLA Modules:
  0.0 183.0 jit_solution(10569893255344406250)
XLA Ops:
  0.6 5.9 %projkv.1 = (bf16[256,384]{1,0:T(8,128)(2,1)}, bf16[256,384]{1,0:T(8,128)(2,1)}, bf16[256,384]{1,0:T(8,128)(2,1)}, bf16[256,384]{1,0:T(8,128)(2,1)}) custom-call(s32[1]{0:T(128)} %bitcast.me, bf16[256,1536]{1,0:T(8,128)(2,1)} %bitcast.15, bf16[1536,768]{1,0:T(8,128)(2,1)} %wk.3, bf16[1536,768]{1,0:T(8,128)(2,1)} %wv.3), custom_call_target="tpu_custom_call" | custom-call | flops 1207959552 | bytes 6291456 | tf_op jit(solution)/shard_map/projkv/pallas_call | solution.py:75
  6.6 2.1 %collective-permute-start = (bf16[256,384]{1,0:T(8,128)(2,1)}, bf16[256,384]{1,0:T(8,128)(2,1)S(1)}, u32[]{:S(2)}, u32[]{:S(2)}) collective-permute-start(bf16[256,384]{1,0:T(8,128)(2,1)} %get-tuple-element.44), channel_id=1, source_target_pairs={{0,4},{4,8},{8,12},{12,0},{1,5},{5,9},{9,13},{13,1},{2,6},{6,10},{... | collective-permute-start | bytes 589832 | tf_op jit(solution)/shard_map/ppermute | solution.py:338
  8.7 2.4 %collective-permute-start.1 = (bf16[256,384]{1,0:T(8,128)(2,1)}, bf16[256,384]{1,0:T(8,128)(2,1)S(1)}, u32[]{:S(2)}, u32[]{:S(2)}) collective-permute-start(bf16[256,384]{1,0:T(8,128)(2,1)} %get-tuple-element.45), channel_id=1, source_target_pairs={{0,8},{4,12},{8,0},{12,4},{1,9},{5,13},{9,1},{13,5},{2,10},{6,14},... | collective-permute-start | bytes 589832 | tf_op jit(solution)/shard_map/ppermute | solution.py:338
  11.1 1.2 collective-permute-start.2
  12.3 3.6 %collective-permute-start.7 = (bf16[256,384]{1,0:T(8,128)(2,1)}, bf16[256,384]{1,0:T(8,128)(2,1)S(1)}, u32[]{:S(2)}, u32[]{:S(2)}) collective-permute-start(bf16[256,384]{1,0:T(8,128)(2,1)} %get-tuple-element.43.refs_0_), channel_id=1, source_target_pairs={{0,2},{2,0},{1,3},{3,1},{4,6},{6,4},{5,7},{7,5},{8,10},{10,8},{9,1... | collective-permute-start | bytes 589832 | tf_op jit(solution)/shard_map/ppermute | solution.py:338
  15.9 1.8 collective-permute-start.3
  17.7 5.0 %projq.1 = (bf16[256,384]{1,0:T(8,128)(2,1)}, bf16[256,384]{1,0:T(8,128)(2,1)}, bf16[256,384]{1,0:T(8,128)(2,1)}, bf16[256,384]{1,0:T(8,128)(2,1)}) custom-call(s32[1]{0:T(128)} %bitcast.me, bf16[256,1536]{1,0:T(8,128)(2,1)} %bitcast.16, bf16[1536,768]{1,0:T(8,128)(2,1)} %wq.3, bf16[256,768]{1,0:T(8,128)(2,1)} %bitcast.26), custom_call_target="tpu_custom_call" | custom-call | flops 603979776 | bytes 4194304 | tf_op jit(solution)/shard_map/projq/pallas_call | solution.py:101
  23.7 1.9 %collective-permute-start.17 = (bf16[256,384]{1,0:T(8,128)(2,1)}, bf16[256,384]{1,0:T(8,128)(2,1)S(1)}, u32[]{:S(2)}, u32[]{:S(2)}) collective-permute-start(bf16[256,384]{1,0:T(8,128)(2,1)} %get-tuple-element.50), channel_id=1, source_target_pairs={{0,12},{4,0},{8,4},{12,8},{1,13},{5,1},{9,5},{13,9},{2,14},{6,2},{... | collective-permute-start | bytes 589832 | tf_op jit(solution)/shard_map/ppermute | solution.py:338
  26.2 2.5 %collective-permute-start.9 = (bf16[256,384]{1,0:T(8,128)(2,1)S(1)}, bf16[256,384]{1,0:T(8,128)(2,1)S(1)}, u32[]{:S(2)}, u32[]{:S(2)}) collective-permute-start(bf16[256,384]{1,0:T(8,128)(2,1)S(1)} %collective-permute-done.1.refs_2_), channel_id=1, source_target_pairs={{0,2},{2,0},{1,3},{3,1},{4,6},{6,4},{5,7},{7,5},{8,10},{10,8},{9,1... | collective-permute-start | bytes 589832 | tf_op jit(solution)/shard_map/ppermute | solution.py:338
  28.6 6.4 %collective-permute-done.15.refs_17_ = bf16[256,384]{1,0:T(8,128)(2,1)S(1)} collective-permute-done((bf16[256,384]{1,0:T(8,128)(2,1)}, bf16[256,384]{1,0:T(8,128)(2,1)S(1)}, u32[]{:S(2)}, u32[]{:S(2)}) %collective-permute-start.15) | collective-permute-done | bytes 196640 | tf_op jit(solution)/shard_map/ppermute | solution.py:338
  35.0 0.9 collective-permute-start.11
  36.5 0.8 collective-permute-done.9.refs_10_
  37.3 1.4 collective-permute-start.6
  38.7 3.5 %collective-permute-done.10.refs_11_ = bf16[256,384]{1,0:T(8,128)(2,1)S(1)} collective-permute-done((bf16[256,384]{1,0:T(8,128)(2,1)S(1)}, bf16[256,384]{1,0:T(8,128)(2,1)S(1)}, u32[]{:S(2)}, u32[]{:S(2)}) %collective-permute-start.10) | collective-permute-done | bytes 196640 | tf_op jit(solution)/shard_map/ppermute | solution.py:338
  42.1 1.7 collective-permute-start.12
  46.2 25.7 %attn1.1 = (f32[1024,384]{1,0:T(8,128)}, bf16[1024,384]{1,0:T(8,128)(2,1)}, bf16[2048,1024]{1,0:T(8,128)(2,1)}, bf16[4096,1024]{1,0:T(8,128)(2,1)}, bf16[1024,25...) custom-call(bf16[256,384]{1,0:T(8,128)(2,1)} %get-tuple-element.43.refs_0_, ...), custom_call_target="tpu_custom_call" | custom-call | flops 21474836480 | bytes 20971520 | tf_op jit(solution)/shard_map/attn1/pallas_call | solution.py:183
  72.3 10.1 %attn2.1 = (f32[1024,384]{1,0:T(8,128)}, bf16[1024,384]{1,0:T(8,128)(2,1)}, bf16[192,256]{1,0:T(8,128)(2,1)}, bf16[192,256]{1,0:T(8,128)(2,1)}, bf16[192,256]{1,0:T(8,128)(2,1)}, /*index=5*/bf16[192,256]{1,0:T(8,128)(2,1)}) custom-call(bf16[2048,1024]{1,0:T(8,128)(2,1)} %get-tuple-element.51.p_in, bf16[4096,1024]{1,0:T(8,128)(2,1)} %get-tuple-element.52.ds_in, ...), custom_call_target="tpu_custom_call" | custom-call | flops 8589934592 | bytes 16777216 | tf_op jit(solution)/shard_map/attn2/pallas_call | solution.py:221
  83.6 1.3 collective-permute-start.28
  84.9 2.1 %collective-permute-start.29 = (bf16[256,1536]{1,0:T(8,128)(2,1)S(1)}, bf16[256,1536]{1,0:T(8,128)(2,1)}, u32[]{:S(2)}, u32[]{:S(2)}) collective-permute-start(bf16[256,1536]{1,0:T(8,128)(2,1)S(1)} %bitcast.21), channel_id=1, source_target_pairs={{0,12},{4,0},{8,4},{12,8},{1,13},{5,1},{9,5},{13,9},{2,14},{6,2},{... | collective-permute-start | bytes 2359304 | tf_op jit(solution)/shard_map/ppermute | solution.py:338
  87.0 16.4 %collective-permute-done.23.u = bf16[1024,384]{1,0:T(8,128)(2,1)S(1)} collective-permute-done((bf16[1024,384]{1,0:T(8,128)(2,1)S(1)}, bf16[1024,384]{1,0:T(8,128)(2,1)S(1)}, u32[]{:S(2)}, u32[]{:S(2)}) %collective-permute-start.23) | collective-permute-done | bytes 786464 | tf_op jit(solution)/shard_map/ppermute | solution.py:338
  103.4 0.9 copy-done.3
  104.3 2.8 %comb.1 = (bf16[256,384]{1,0:T(8,128)(2,1)}, bf16[256,384]{1,0:T(8,128)(2,1)}, bf16[256,384]{1,0:T(8,128)(2,1)}, bf16[256,384]{1,0:T(8,128)(2,1)}) custom-call(f32[1024,384]{1,0:T(8,128)} %get-tuple-element.61.a, bf16[1024,384]{1,0:T(8,128)(2,1)} %copy-done.2, bf16[1024,384]{1,0:T(8,128)(2,1)} %copy-done.3), custom_call_target="tpu_custom_call" | custom-call | flops 1048576 | bytes 4194304 | tf_op jit(solution)/shard_map/comb/pallas_call | solution.py:260
  107.1 13.5 %collective-permute-done.27.x1 = bf16[256,1536]{1,0:T(8,128)(2,1)} collective-permute-done((bf16[256,1536]{1,0:T(8,128)(2,1)S(1)}, bf16[256,1536]{1,0:T(8,128)(2,1)}, u32[]{:S(2)}, u32[]{:S(2)}) %collective-permute-start.27) | collective-permute-done | bytes 786464 | tf_op jit(solution)/shard_map/ppermute | solution.py:338
  121.0 4.9 %gkv.1 = (f32[192,1536]{1,0:T(8,128)}, bf16[192,1536]{1,0:T(8,128)(2,1)}) custom-call(s32[1]{0:T(128)} %bitcast.5.core, bf16[256,384]{1,0:T(8,128)(2,1)} %get-tuple-element.65.p0.d0, bf16[256,384]{1,0:T(8,128)(2,1)} %get-tuple-element.66.d1, bf16[256,384]{1,0:T(8,128)(2,1)} %get-tuple-element.67.d2, bf16[256,384]{1,0:T(8,128)(2,1)} %get-tuple-element.68.d3, ...), custom_call_target="tpu_custom_call" | custom-call | flops 1207959552 | bytes 6291456 | tf_op jit(solution)/shard_map/gkv/pallas_call | solution.py:281
  125.9 1.6 collective-permute-start.30
  127.5 3.8 %gq.1 = (f32[96,1536]{1,0:T(8,128)}, bf16[96,1536]{1,0:T(8,128)(2,1)}) custom-call(s32[1]{0:T(128)} %bitcast.5.core, bf16[192,256]{1,0:T(8,128)(2,1)} %get-tuple-element.57.q0.d0, bf16[192,256]{1,0:T(8,128)(2,1)} %get-tuple-element.58.d1, bf16[192,256]{1,0:T(8,128)(2,1)} %get-tuple-element.59.d2, bf16[192,256]{1,0:T(8,128)(2,1)} %get-tuple-element.60.d3, ...), custom_call_target="tpu_custom_call" | custom-call | flops 603979776 | bytes 5242880 | tf_op jit(solution)/shard_map/gq/pallas_call | solution.py:245
  131.4 1.8 collective-permute-done.34.t
  133.1 0.7 copy-done.5
  133.8 1.9 %split.3 = (bf16[96,384]{1,0:T(8,128)(2,1)}, bf16[96,384]{1,0:T(8,128)(2,1)}, bf16[96,384]{1,0:T(8,128)(2,1)}, bf16[96,384]{1,0:T(8,128)(2,1)}) custom-call(s32[1]{0:T(128)} %bitcast.4.me, f32[96,1536]{1,0:T(8,128)} %get-tuple-element.76.a, bf16[96,1536]{1,0:T(8,128)(2,1)} %copy-done.5), custom_call_target="tpu_custom_call" | custom-call | flops 1048576 | bytes 2097152 | tf_op jit(solution)/shard_map/split/pallas_call | solution.py:298
  135.8 1.3 collective-permute-start.35
  137.0 2.6 %collective-permute-start.36 = (bf16[96,384]{1,0:T(8,128)(2,1)}, bf16[96,384]{1,0:T(8,128)(2,1)S(1)}, u32[]{:S(2)}, u32[]{:S(2)}) collective-permute-start(bf16[96,384]{1,0:T(8,128)(2,1)} %get-tuple-element.80), channel_id=1, source_target_pairs={{0,64},{32,96},{64,0},{96,32},{1,65},{33,97},{65,1},{97,33},{2,66}... | collective-permute-start | bytes 221192 | tf_op jit(solution)/shard_map/ppermute | solution.py:338
  139.7 1.1 collective-permute-start.37
  140.7 2.4 %collective-permute-start.18 = (bf16[192,256]{1,0:T(8,128)(2,1)S(1)}, bf16[192,256]{1,0:T(8,128)(2,1)S(1)}, u32[]{:S(2)}, u32[]{:S(2)}) collective-permute-start(bf16[192,256]{1,0:T(8,128)(2,1)S(1)} %copy-done.14), channel_id=1, source_target_pairs={{0,12},{4,0},{8,4},{12,8},{1,13},{5,1},{9,5},{13,9},{2,14},{6,2},{... | collective-permute-start | bytes 294920 | tf_op jit(solution)/shard_map/ppermute | solution.py:338
  143.9 2.3 %split.2 = (bf16[192,384]{1,0:T(8,128)(2,1)}, bf16[192,384]{1,0:T(8,128)(2,1)}, bf16[192,384]{1,0:T(8,128)(2,1)}, bf16[192,384]{1,0:T(8,128)(2,1)}) custom-call(s32[1]{0:T(128)} %bitcast.4.me, f32[192,1536]{1,0:T(8,128)} %get-tuple-element.70.a, bf16[192,1536]{1,0:T(8,128)(2,1)} %copy-done.4), custom_call_target="tpu_custom_call" | custom-call | flops 1048576 | bytes 2097152 | tf_op jit(solution)/shard_map/split/pallas_call | solution.py:298
  146.7 0.8 collective-permute-start.32
  147.4 1.7 collective-permute-start.33
  149.1 0.9 add_convert_fusion.2
  150.1 5.3 %collective-permute-done.31 = bf16[192,384]{1,0:T(8,128)(2,1)S(1)} collective-permute-done((bf16[192,384]{1,0:T(8,128)(2,1)}, bf16[192,384]{1,0:T(8,128)(2,1)S(1)}, u32[]{:S(2)}, u32[]{:S(2)}) %collective-permute-start.31) | collective-permute-done | bytes 147488 | tf_op jit(solution)/shard_map/ppermute | solution.py:338
  155.4 1.6 collective-permute-start.25
  157.1 1.0 add_convert_fusion.1
  158.1 1.1 collective-permute-start.20
  159.5 0.9 reshape.36
  160.4 10.0 %all-to-all-start = ((bf16[32,12,288]{2,1,0:T(8,128)(2,1)}), bf16[32,12,288]{2,1,0:T(8,128)(2,1)S(1)}, u32[]{:S(2)}, u32[]{:S(2)}) async-start(bf16[32,12,288]{2,1,0:T(8,128)(2,1)} %reshape.36), calls=%async_computation | async-start | bytes 786432 | tf_op jit(solution)/shard_map/all_to_all | solution.py:375
  171.9 6.7 %back.1 = bf16[256,1536]{1,0:T(8,128)(2,1)} custom-call(s32[1]{0:T(128)} %bitcast.me, bf16[192,256]{1,0:T(8,128)(2,1)} %get-tuple-element.57.q0.d0, bf16[192,256]{1,0:T(8,128)(2,1)} %copy-done.9, bf16[192,256]{1,0:T(8,128)(2,1)} %copy-done.10, bf16[192,256]{1,0:T(8,128)(2,1)} %copy-done.11, bf16[256,384]{1,0:T(8,128)(2,1)} %get-tuple-element.65.p0.d0, ...), custom_call_target="tpu_custom_call" | custom-call | flops 1811939328 | bytes 9437184 | tf_op jit(solution)/shard_map/back/pallas_call | solution.py:328
  178.6 1.9 %all-to-all-done = bf16[32,12,288]{2,1,0:T(8,128)(2,1)S(1)} async-done(((bf16[32,12,288]{2,1,0:T(8,128)(2,1)}), bf16[32,12,288]{2,1,0:T(8,128)(2,1)S(1)}, u32[]{:S(2)}, u32[]{:S(2)}) %all-to-all-start) | async-done | bytes 221216 | tf_op jit(solution)/shard_map/all_to_all | solution.py:375
  180.7 0.7 reshape_squeeze.6
  181.5 0.7 reshape_squeeze.7
  182.2 0.7 reshape.39
  (127 shorter events, 9.5 us)
Async XLA Ops:
  6.6 16.1 %collective-permute-start = (bf16[256,384]{1,0:T(8,128)(2,1)}, bf16[256,384]{1,0:T(8,128)(2,1)S(1)}, u32[]{:S(2)}, u32[]{:S(2)}) collective-permute-start(bf16[256,384]{1,0:T(8,128)(2,1)} %get-tuple-element.44), channel_id=1, source_target_pairs={{0,4},{4,8},{8,12},{12,0},{1,5},{5,9},{9,13},{13,1},{2,6},{6,10},{... | collective-permute-start | bytes 589832 | tf_op jit(solution)/shard_map/ppermute | solution.py:338
  8.7 14.4 %collective-permute-start.1 = (bf16[256,384]{1,0:T(8,128)(2,1)}, bf16[256,384]{1,0:T(8,128)(2,1)S(1)}, u32[]{:S(2)}, u32[]{:S(2)}) collective-permute-start(bf16[256,384]{1,0:T(8,128)(2,1)} %get-tuple-element.45), channel_id=1, source_target_pairs={{0,8},{4,12},{8,0},{12,4},{1,9},{5,13},{9,1},{13,5},{2,10},{6,14},... | collective-permute-start | bytes 589832 | tf_op jit(solution)/shard_map/ppermute | solution.py:338
  11.1 12.6 %collective-permute-start.2 = (bf16[256,384]{1,0:T(8,128)(2,1)}, bf16[256,384]{1,0:T(8,128)(2,1)S(1)}, u32[]{:S(2)}, u32[]{:S(2)}) collective-permute-start(bf16[256,384]{1,0:T(8,128)(2,1)} %get-tuple-element.46), channel_id=1, source_target_pairs={{0,12},{4,0},{8,4},{12,8},{1,13},{5,1},{9,5},{13,9},{2,14},{6,2},{... | collective-permute-start | bytes 589832 | tf_op jit(solution)/shard_map/ppermute | solution.py:338
  12.3 13.3 %collective-permute-start.7 = (bf16[256,384]{1,0:T(8,128)(2,1)}, bf16[256,384]{1,0:T(8,128)(2,1)S(1)}, u32[]{:S(2)}, u32[]{:S(2)}) collective-permute-start(bf16[256,384]{1,0:T(8,128)(2,1)} %get-tuple-element.43.refs_0_), channel_id=1, source_target_pairs={{0,2},{2,0},{1,3},{3,1},{4,6},{6,4},{5,7},{7,5},{8,10},{10,8},{9,1... | collective-permute-start | bytes 589832 | tf_op jit(solution)/shard_map/ppermute | solution.py:338
  15.9 10.3 %collective-permute-start.3 = (bf16[256,384]{1,0:T(8,128)(2,1)}, bf16[256,384]{1,0:T(8,128)(2,1)S(1)}, u32[]{:S(2)}, u32[]{:S(2)}) collective-permute-start(bf16[256,384]{1,0:T(8,128)(2,1)} %get-tuple-element.43.refs_0_), channel_id=1, source_target_pairs={{0,1},{1,0},{2,3},{3,2},{4,5},{5,4},{6,7},{7,6},{8,9},{9,8},{10,11... | collective-permute-start | bytes 589832 | tf_op jit(solution)/shard_map/ppermute | solution.py:338
  22.7 22.8 %copy-start.18 = (bf16[256,384]{1,0:T(8,128)(2,1)}, bf16[256,384]{1,0:T(8,128)(2,1)S(1)}, u32[]{:S(2)}) copy-start(bf16[256,384]{1,0:T(8,128)(2,1)S(1)} %collective-permute-done.refs_1_) | copy-start | bytes 589828
  22.7 12.2 %collective-permute-start.15 = (bf16[256,384]{1,0:T(8,128)(2,1)}, bf16[256,384]{1,0:T(8,128)(2,1)S(1)}, u32[]{:S(2)}, u32[]{:S(2)}) collective-permute-start(bf16[256,384]{1,0:T(8,128)(2,1)} %get-tuple-element.48), channel_id=1, source_target_pairs={{0,4},{4,8},{8,12},{12,0},{1,5},{5,9},{9,13},{13,1},{2,6},{6,10},{... | collective-permute-start | bytes 589832 | tf_op jit(solution)/shard_map/ppermute | solution.py:338
  23.1 22.4 %copy-start.19 = (bf16[256,384]{1,0:T(8,128)(2,1)}, bf16[256,384]{1,0:T(8,128)(2,1)S(1)}, u32[]{:S(2)}) copy-start(bf16[256,384]{1,0:T(8,128)(2,1)S(1)} %collective-permute-done.1.refs_2_) | copy-start | bytes 589828
  23.1 11.9 %collective-permute-start.16 = (bf16[256,384]{1,0:T(8,128)(2,1)}, bf16[256,384]{1,0:T(8,128)(2,1)S(1)}, u32[]{:S(2)}, u32[]{:S(2)}) collective-permute-start(bf16[256,384]{1,0:T(8,128)(2,1)} %get-tuple-element.49), channel_id=1, source_target_pairs={{0,8},{4,12},{8,0},{12,4},{1,9},{5,13},{9,1},{13,5},{2,10},{6,14},... | collective-permute-start | bytes 589832 | tf_op jit(solution)/shard_map/ppermute | solution.py:338
  23.7 21.8 %copy-start.20 = (bf16[256,384]{1,0:T(8,128)(2,1)}, bf16[256,384]{1,0:T(8,128)(2,1)S(1)}, u32[]{:S(2)}) copy-start(bf16[256,384]{1,0:T(8,128)(2,1)S(1)} %collective-permute-done.2.refs_3_) | copy-start | bytes 589828
  23.7 12.1 %collective-permute-start.17 = (bf16[256,384]{1,0:T(8,128)(2,1)}, bf16[256,384]{1,0:T(8,128)(2,1)S(1)}, u32[]{:S(2)}, u32[]{:S(2)}) collective-permute-start(bf16[256,384]{1,0:T(8,128)(2,1)} %get-tuple-element.50), channel_id=1, source_target_pairs={{0,12},{4,0},{8,4},{12,8},{1,13},{5,1},{9,5},{13,9},{2,14},{6,2},{... | collective-permute-start | bytes 589832 | tf_op jit(solution)/shard_map/ppermute | solution.py:338
  25.6 19.9 %copy-start.21 = (bf16[256,384]{1,0:T(8,128)(2,1)}, bf16[256,384]{1,0:T(8,128)(2,1)S(1)}, u32[]{:S(2)}) copy-start(bf16[256,384]{1,0:T(8,128)(2,1)S(1)} %collective-permute-done.7.refs_8_) | copy-start | bytes 589828
  25.6 10.8 %collective-permute-start.8 = (bf16[256,384]{1,0:T(8,128)(2,1)S(1)}, bf16[256,384]{1,0:T(8,128)(2,1)S(1)}, u32[]{:S(2)}, u32[]{:S(2)}) collective-permute-start(bf16[256,384]{1,0:T(8,128)(2,1)S(1)} %collective-permute-done.refs_1_), channel_id=1, source_target_pairs={{0,2},{2,0},{1,3},{3,1},{4,6},{6,4},{5,7},{7,5},{8,10},{10,8},{9,1... | collective-permute-start | bytes 589832 | tf_op jit(solution)/shard_map/ppermute | solution.py:338
  26.2 19.4 %copy-start.22 = (bf16[256,384]{1,0:T(8,128)(2,1)}, bf16[256,384]{1,0:T(8,128)(2,1)S(1)}, u32[]{:S(2)}) copy-start(bf16[256,384]{1,0:T(8,128)(2,1)S(1)} %collective-permute-done.3.refs_4_) | copy-start | bytes 589828
  26.2 11.1 %collective-permute-start.9 = (bf16[256,384]{1,0:T(8,128)(2,1)S(1)}, bf16[256,384]{1,0:T(8,128)(2,1)S(1)}, u32[]{:S(2)}, u32[]{:S(2)}) collective-permute-start(bf16[256,384]{1,0:T(8,128)(2,1)S(1)} %collective-permute-done.1.refs_2_), channel_id=1, source_target_pairs={{0,2},{2,0},{1,3},{3,1},{4,6},{6,4},{5,7},{7,5},{8,10},{10,8},{9,1... | collective-permute-start | bytes 589832 | tf_op jit(solution)/shard_map/ppermute | solution.py:338
  35.0 7.2 %collective-permute-start.10 = (bf16[256,384]{1,0:T(8,128)(2,1)S(1)}, bf16[256,384]{1,0:T(8,128)(2,1)S(1)}, u32[]{:S(2)}, u32[]{:S(2)}) collective-permute-start(bf16[256,384]{1,0:T(8,128)(2,1)S(1)} %collective-permute-done.2.refs_3_), channel_id=1, source_target_pairs={{0,2},{2,0},{1,3},{3,1},{4,6},{6,4},{5,7},{7,5},{8,10},{10,8},{9,1... | collective-permute-start | bytes 589832 | tf_op jit(solution)/shard_map/ppermute | solution.py:338
  35.0 8.8 %collective-permute-start.11 = (bf16[256,384]{1,0:T(8,128)(2,1)S(1)}, bf16[256,384]{1,0:T(8,128)(2,1)S(1)}, u32[]{:S(2)}, u32[]{:S(2)}) collective-permute-start(bf16[256,384]{1,0:T(8,128)(2,1)S(1)} %collective-permute-done.7.refs_8_), channel_id=1, source_target_pairs={{0,1},{1,0},{2,3},{3,2},{4,5},{5,4},{6,7},{7,6},{8,9},{9,8},{10,11... | collective-permute-start | bytes 589832 | tf_op jit(solution)/shard_map/ppermute | solution.py:338
  35.9 8.0 %collective-permute-start.4 = (bf16[256,384]{1,0:T(8,128)(2,1)S(1)}, bf16[256,384]{1,0:T(8,128)(2,1)S(1)}, u32[]{:S(2)}, u32[]{:S(2)}) collective-permute-start(bf16[256,384]{1,0:T(8,128)(2,1)S(1)} %collective-permute-done.refs_1_), channel_id=1, source_target_pairs={{0,1},{1,0},{2,3},{3,2},{4,5},{5,4},{6,7},{7,6},{8,9},{9,8},{10,11... | collective-permute-start | bytes 589832 | tf_op jit(solution)/shard_map/ppermute | solution.py:338
  36.4 7.9 %collective-permute-start.5 = (bf16[256,384]{1,0:T(8,128)(2,1)S(1)}, bf16[256,384]{1,0:T(8,128)(2,1)S(1)}, u32[]{:S(2)}, u32[]{:S(2)}) collective-permute-start(bf16[256,384]{1,0:T(8,128)(2,1)S(1)} %collective-permute-done.1.refs_2_), channel_id=1, source_target_pairs={{0,1},{1,0},{2,3},{3,2},{4,5},{5,4},{6,7},{7,6},{8,9},{9,8},{10,11... | collective-permute-start | bytes 589832 | tf_op jit(solution)/shard_map/ppermute | solution.py:338
  37.3 7.1 %collective-permute-start.6 = (bf16[256,384]{1,0:T(8,128)(2,1)S(1)}, bf16[256,384]{1,0:T(8,128)(2,1)S(1)}, u32[]{:S(2)}, u32[]{:S(2)}) collective-permute-start(bf16[256,384]{1,0:T(8,128)(2,1)S(1)} %collective-permute-done.2.refs_3_), channel_id=1, source_target_pairs={{0,1},{1,0},{2,3},{3,2},{4,5},{5,4},{6,7},{7,6},{8,9},{9,8},{10,11... | collective-permute-start | bytes 589832 | tf_op jit(solution)/shard_map/ppermute | solution.py:338
  42.1 2.7 %collective-permute-start.12 = (bf16[256,384]{1,0:T(8,128)(2,1)S(1)}, bf16[256,384]{1,0:T(8,128)(2,1)S(1)}, u32[]{:S(2)}, u32[]{:S(2)}) collective-permute-start(bf16[256,384]{1,0:T(8,128)(2,1)S(1)} %collective-permute-done.8.refs_9_), channel_id=1, source_target_pairs={{0,1},{1,0},{2,3},{3,2},{4,5},{5,4},{6,7},{7,6},{8,9},{9,8},{10,11... | collective-permute-start | bytes 589832 | tf_op jit(solution)/shard_map/ppermute | solution.py:338
  43.8 1.4 collective-permute-start.13
  43.9 1.6 collective-permute-start.14
  72.0 10.8 %collective-permute-start.22 = (bf16[1024,384]{1,0:T(8,128)(2,1)}, bf16[1024,384]{1,0:T(8,128)(2,1)S(1)}, u32[]{:S(2)}, u32[]{:S(2)}) collective-permute-start(bf16[1024,384]{1,0:T(8,128)(2,1)} %get-tuple-element.64), channel_id=1, source_target_pairs={{0,1},{1,0},{2,3},{3,2},{4,5},{5,4},{6,7},{7,6},{8,9},{9,8},{10,11... | collective-permute-start | bytes 2359304 | tf_op jit(solution)/shard_map/ppermute | solution.py:338
  82.5 4.5 %collective-permute-start.21 = (bf16[1024,384]{1,0:T(8,128)(2,1)}, bf16[1024,384]{1,0:T(8,128)(2,1)S(1)}, u32[]{:S(2)}, u32[]{:S(2)}) collective-permute-start(bf16[1024,384]{1,0:T(8,128)(2,1)} %get-tuple-element.62), channel_id=1, source_target_pairs={{0,1},{1,0},{2,3},{3,2},{4,5},{5,4},{6,7},{7,6},{8,9},{9,8},{10,11... | collective-permute-start | bytes 2359304 | tf_op jit(solution)/shard_map/ppermute | solution.py:338
  83.0 20.5 %collective-permute-start.23 = (bf16[1024,384]{1,0:T(8,128)(2,1)S(1)}, bf16[1024,384]{1,0:T(8,128)(2,1)S(1)}, u32[]{:S(2)}, u32[]{:S(2)}) collective-permute-start(bf16[1024,384]{1,0:T(8,128)(2,1)S(1)} %add_convert_fusion), channel_id=1, source_target_pairs={{0,2},{2,0},{1,3},{3,1},{4,6},{6,4},{5,7},{7,5},{8,10},{10,8},{9,1... | collective-permute-start | bytes 2359304 | tf_op jit(solution)/shard_map/ppermute | solution.py:338
  83.6 37.1 %collective-permute-start.27 = (bf16[256,1536]{1,0:T(8,128)(2,1)S(1)}, bf16[256,1536]{1,0:T(8,128)(2,1)}, u32[]{:S(2)}, u32[]{:S(2)}) collective-permute-start(bf16[256,1536]{1,0:T(8,128)(2,1)S(1)} %bitcast.19), channel_id=1, source_target_pairs={{0,4},{4,8},{8,12},{12,0},{1,5},{5,9},{9,13},{13,1},{2,6},{6,10},{... | collective-permute-start | bytes 2359304 | tf_op jit(solution)/shard_map/ppermute | solution.py:338
  83.6 37.1 %collective-permute-start.28 = (bf16[256,1536]{1,0:T(8,128)(2,1)S(1)}, bf16[256,1536]{1,0:T(8,128)(2,1)}, u32[]{:S(2)}, u32[]{:S(2)}) collective-permute-start(bf16[256,1536]{1,0:T(8,128)(2,1)S(1)} %bitcast.20), channel_id=1, source_target_pairs={{0,8},{4,12},{8,0},{12,4},{1,9},{5,13},{9,1},{13,5},{2,10},{6,14},... | collective-permute-start | bytes 2359304 | tf_op jit(solution)/shard_map/ppermute | solution.py:338
  84.9 36.1 %collective-permute-start.29 = (bf16[256,1536]{1,0:T(8,128)(2,1)S(1)}, bf16[256,1536]{1,0:T(8,128)(2,1)}, u32[]{:S(2)}, u32[]{:S(2)}) collective-permute-start(bf16[256,1536]{1,0:T(8,128)(2,1)S(1)} %bitcast.21), channel_id=1, source_target_pairs={{0,12},{4,0},{8,4},{12,8},{1,13},{5,1},{9,5},{13,9},{2,14},{6,2},{... | collective-permute-start | bytes 2359304 | tf_op jit(solution)/shard_map/ppermute | solution.py:338
  125.9 17.2 %collective-permute-start.30 = (bf16[192,1536]{1,0:T(8,128)(2,1)}, bf16[192,1536]{1,0:T(8,128)(2,1)S(1)}, u32[]{:S(2)}, u32[]{:S(2)}) collective-permute-start(bf16[192,1536]{1,0:T(8,128)(2,1)} %get-tuple-element.71), channel_id=1, source_target_pairs={{0,1},{1,0},{2,3},{3,2},{4,5},{5,4},{6,7},{7,6},{8,9},{9,8},{10,11... | collective-permute-start | bytes 1769480 | tf_op jit(solution)/shard_map/ppermute | solution.py:338
  131.2 24.2 %copy-start.17 = (bf16[256,384]{1,0:T(8,128)(2,1)S(1)}, bf16[256,384]{1,0:T(8,128)(2,1)}, u32[]{:S(2)}) copy-start(bf16[256,384]{1,0:T(8,128)(2,1)} %get-tuple-element.66.d1) | copy-start | bytes 589828
  131.2 24.2 %copy-start.16 = (bf16[256,384]{1,0:T(8,128)(2,1)S(1)}, bf16[256,384]{1,0:T(8,128)(2,1)}, u32[]{:S(2)}) copy-start(bf16[256,384]{1,0:T(8,128)(2,1)} %get-tuple-element.67.d2) | copy-start | bytes 589828
  131.3 25.8 %copy-start.15 = (bf16[256,384]{1,0:T(8,128)(2,1)S(1)}, bf16[256,384]{1,0:T(8,128)(2,1)}, u32[]{:S(2)}) copy-start(bf16[256,384]{1,0:T(8,128)(2,1)} %get-tuple-element.68.d3) | copy-start | bytes 589828
  131.3 26.9 %copy-start.12 = (bf16[192,256]{1,0:T(8,128)(2,1)S(1)}, bf16[192,256]{1,0:T(8,128)(2,1)}, u32[]{:S(2)}) copy-start(bf16[192,256]{1,0:T(8,128)(2,1)} %get-tuple-element.60.d3) | copy-start | bytes 294916
  131.3 1.9 %collective-permute-start.34 = (bf16[96,1536]{1,0:T(8,128)(2,1)}, bf16[96,1536]{1,0:T(8,128)(2,1)S(1)}, u32[]{:S(2)}, u32[]{:S(2)}) collective-permute-start(bf16[96,1536]{1,0:T(8,128)(2,1)} %get-tuple-element.77), channel_id=1, source_target_pairs={{0,1},{1,0},{2,3},{3,2},{4,5},{5,4},{6,7},{7,6},{8,9},{9,8},{10,11... | collective-permute-start | bytes 884744 | tf_op jit(solution)/shard_map/ppermute | solution.py:338
  135.8 10.5 %collective-permute-start.35 = (bf16[96,384]{1,0:T(8,128)(2,1)}, bf16[96,384]{1,0:T(8,128)(2,1)S(1)}, u32[]{:S(2)}, u32[]{:S(2)}) collective-permute-start(bf16[96,384]{1,0:T(8,128)(2,1)} %get-tuple-element.79), channel_id=1, source_target_pairs={{0,32},{32,64},{64,96},{96,0},{1,33},{33,65},{65,97},{97,1},{2,34}... | collective-permute-start | bytes 221192 | tf_op jit(solution)/shard_map/ppermute | solution.py:338
  137.0 9.6 %collective-permute-start.36 = (bf16[96,384]{1,0:T(8,128)(2,1)}, bf16[96,384]{1,0:T(8,128)(2,1)S(1)}, u32[]{:S(2)}, u32[]{:S(2)}) collective-permute-start(bf16[96,384]{1,0:T(8,128)(2,1)} %get-tuple-element.80), channel_id=1, source_target_pairs={{0,64},{32,96},{64,0},{96,32},{1,65},{33,97},{65,1},{97,33},{2,66}... | collective-permute-start | bytes 221192 | tf_op jit(solution)/shard_map/ppermute | solution.py:338
  139.7 7.8 %collective-permute-start.37 = (bf16[96,384]{1,0:T(8,128)(2,1)}, bf16[96,384]{1,0:T(8,128)(2,1)S(1)}, u32[]{:S(2)}, u32[]{:S(2)}) collective-permute-start(bf16[96,384]{1,0:T(8,128)(2,1)} %get-tuple-element.81), channel_id=1, source_target_pairs={{0,96},{32,0},{64,32},{96,64},{1,97},{33,1},{65,33},{97,65},{2,98}... | collective-permute-start | bytes 221192 | tf_op jit(solution)/shard_map/ppermute | solution.py:338
  140.7 17.4 %collective-permute-start.18 = (bf16[192,256]{1,0:T(8,128)(2,1)S(1)}, bf16[192,256]{1,0:T(8,128)(2,1)S(1)}, u32[]{:S(2)}, u32[]{:S(2)}) collective-permute-start(bf16[192,256]{1,0:T(8,128)(2,1)S(1)} %copy-done.14), channel_id=1, source_target_pairs={{0,12},{4,0},{8,4},{12,8},{1,13},{5,1},{9,5},{13,9},{2,14},{6,2},{... | collective-permute-start | bytes 294920 | tf_op jit(solution)/shard_map/ppermute | solution.py:338
  143.1 27.3 %collective-permute-start.19 = (bf16[192,256]{1,0:T(8,128)(2,1)S(1)}, bf16[192,256]{1,0:T(8,128)(2,1)S(1)}, u32[]{:S(2)}, u32[]{:S(2)}) collective-permute-start(bf16[192,256]{1,0:T(8,128)(2,1)S(1)} %copy-done.13), channel_id=1, source_target_pairs={{0,8},{4,12},{8,0},{12,4},{1,9},{5,13},{9,1},{13,5},{2,10},{6,14},... | collective-permute-start | bytes 294920 | tf_op jit(solution)/shard_map/ppermute | solution.py:338
  146.2 9.2 %collective-permute-start.31 = (bf16[192,384]{1,0:T(8,128)(2,1)}, bf16[192,384]{1,0:T(8,128)(2,1)S(1)}, u32[]{:S(2)}, u32[]{:S(2)}) collective-permute-start(bf16[192,384]{1,0:T(8,128)(2,1)} %get-tuple-element.73), channel_id=1, source_target_pairs={{0,32},{32,64},{64,96},{96,0},{1,33},{33,65},{65,97},{97,1},{2,34}... | collective-permute-start | bytes 442376 | tf_op jit(solution)/shard_map/ppermute | solution.py:338
  146.7 8.8 %collective-permute-start.32 = (bf16[192,384]{1,0:T(8,128)(2,1)}, bf16[192,384]{1,0:T(8,128)(2,1)S(1)}, u32[]{:S(2)}, u32[]{:S(2)}) collective-permute-start(bf16[192,384]{1,0:T(8,128)(2,1)} %get-tuple-element.74), channel_id=1, source_target_pairs={{0,64},{32,96},{64,0},{96,32},{1,65},{33,97},{65,1},{97,33},{2,66}... | collective-permute-start | bytes 442376 | tf_op jit(solution)/shard_map/ppermute | solution.py:338
  147.4 9.7 %collective-permute-start.33 = (bf16[192,384]{1,0:T(8,128)(2,1)}, bf16[192,384]{1,0:T(8,128)(2,1)S(1)}, u32[]{:S(2)}, u32[]{:S(2)}) collective-permute-start(bf16[192,384]{1,0:T(8,128)(2,1)} %get-tuple-element.75), channel_id=1, source_target_pairs={{0,96},{32,0},{64,32},{96,64},{1,97},{33,1},{65,33},{97,65},{2,98}... | collective-permute-start | bytes 442376 | tf_op jit(solution)/shard_map/ppermute | solution.py:338
  155.4 15.0 %collective-permute-start.24 = (bf16[256,384]{1,0:T(8,128)(2,1)S(1)}, bf16[256,384]{1,0:T(8,128)(2,1)S(1)}, u32[]{:S(2)}, u32[]{:S(2)}) collective-permute-start(bf16[256,384]{1,0:T(8,128)(2,1)S(1)} %copy-done.17), channel_id=1, source_target_pairs={{0,12},{4,0},{8,4},{12,8},{1,13},{5,1},{9,5},{13,9},{2,14},{6,2},{... | collective-permute-start | bytes 589832 | tf_op jit(solution)/shard_map/ppermute | solution.py:338
  155.4 15.0 %collective-permute-start.25 = (bf16[256,384]{1,0:T(8,128)(2,1)S(1)}, bf16[256,384]{1,0:T(8,128)(2,1)S(1)}, u32[]{:S(2)}, u32[]{:S(2)}) collective-permute-start(bf16[256,384]{1,0:T(8,128)(2,1)S(1)} %copy-done.16), channel_id=1, source_target_pairs={{0,8},{4,12},{8,0},{12,4},{1,9},{5,13},{9,1},{13,5},{2,10},{6,14},... | collective-permute-start | bytes 589832 | tf_op jit(solution)/shard_map/ppermute | solution.py:338
  157.1 13.3 %collective-permute-start.26 = (bf16[256,384]{1,0:T(8,128)(2,1)S(1)}, bf16[256,384]{1,0:T(8,128)(2,1)S(1)}, u32[]{:S(2)}, u32[]{:S(2)}) collective-permute-start(bf16[256,384]{1,0:T(8,128)(2,1)S(1)} %copy-done.15), channel_id=1, source_target_pairs={{0,4},{4,8},{8,12},{12,0},{1,5},{5,9},{9,13},{13,1},{2,6},{6,10},{... | collective-permute-start | bytes 589832 | tf_op jit(solution)/shard_map/ppermute | solution.py:338
  158.1 12.2 %collective-permute-start.20 = (bf16[192,256]{1,0:T(8,128)(2,1)S(1)}, bf16[192,256]{1,0:T(8,128)(2,1)S(1)}, u32[]{:S(2)}, u32[]{:S(2)}) collective-permute-start(bf16[192,256]{1,0:T(8,128)(2,1)S(1)} %copy-done.12), channel_id=1, source_target_pairs={{0,4},{4,8},{8,12},{12,0},{1,5},{5,9},{9,13},{13,1},{2,6},{6,10},{... | collective-permute-start | bytes 294920 | tf_op jit(solution)/shard_map/ppermute | solution.py:338
  160.4 20.1 %all-to-all-start = ((bf16[32,12,288]{2,1,0:T(8,128)(2,1)}), bf16[32,12,288]{2,1,0:T(8,128)(2,1)S(1)}, u32[]{:S(2)}, u32[]{:S(2)}) async-start(bf16[32,12,288]{2,1,0:T(8,128)(2,1)} %reshape.36), calls=%async_computation | async-start | bytes 786432 | tf_op jit(solution)/shard_map/all_to_all | solution.py:375
  (27 other events, 138.6 us)

commit v2 on v0

v2 whole, which is shorter than its diff:
```python
import functools
import math

import jax
import jax.numpy as jnp
from jax import lax
from jax.experimental import pallas as pl
from jax.experimental.pallas import tpu as pltpu
from jax.sharding import Mesh, PartitionSpec as P

F32, BF16 = jnp.float32, jnp.bfloat16
D = 1536
H = 4
E = 192
HD = H * E
NB = 256
NQ = 4 * NB
NK = 16 * NB
KC = 512
SCALE = 1.0 / math.sqrt(E)
C2 = SCALE * math.log2(math.e)
ANY = pl.BlockSpec(memory_space=pl.ANY)
VM = pl.BlockSpec(memory_space=pltpu.VMEM)
SM = pl.BlockSpec(memory_space=pltpu.SMEM)
PARAMS = pltpu.CompilerParams(vmem_limit_bytes=58 * 2**20)
SMALL = pltpu.CompilerParams(vmem_limit_bytes=24 * 2**20)
sds = jax.ShapeDtypeStruct


def dot(a, b, dims=(((1,), (0,)), ((), ()))):
    return lax.dot_general(a, b, dims, preferred_element_type=F32)


def nt(a, b):
    return dot(a, b, (((1,), (1,)), ((), ())))


def call(body, name, us, ins, outs, out_specs, in_specs=None, scratch=(), params=PARAMS):
    return pl.pallas_call(
        body, in_specs=in_specs or [VM] * len(ins), out_specs=out_specs, out_shape=outs,
        scratch_shapes=list(scratch), compiler_params=params, name=name,
        cost_estimate=pl.CostEstimate(flops=2**20, bytes_accessed=int(us * 1e5), transcendentals=0),
    )(*ins)


KP = D // 4


def send_out(me, scr, outs, sem):
    cps = [pltpu.make_async_copy(scr.at[lax.rem(me + j, H)], outs[j], sem.at[j]) for j in range(4)]
    for c in cps:
        c.start()
    for c in cps:
        c.wait()


def loads(pairs, sem):
    cps = []
    for n, (a, b) in enumerate(pairs):
        for i in range(4):
            r = pl.ds(i * KP, KP)
            cps.append(pltpu.make_async_copy(a.at[r], b.at[r], sem.at[4 * n + i]))
    return cps


TT = (((0,), (1,)), ((), ()))


def projkv_body(me, x, wk, wv, o0, o1, o2, o3, wks, wvs, scr, sem, osem):
    cps = loads(((wk, wks), (wv, wvs)), sem)
    for i in range(4):
        cps[i].start()
        cps[4 + i].start()
    k = v = None
    for i in range(4):
        cps[i].wait()
        cps[4 + i].wait()
        r = pl.ds(i * KP, KP)
        xi = x[:, r]
        dk, dv = dot(wks[r, :], xi, TT), dot(wvs[r, :], xi, TT)
        k, v = (dk, dv) if i == 0 else (k + dk, v + dv)
    k, v = k.astype(BF16), v.astype(BF16)
    for h in range(H):
        scr[h] = jnp.concatenate([k[h * E:(h + 1) * E], v[h * E:(h + 1) * E]], 0).T
    send_out(me[0], scr, (o0, o1, o2, o3), osem)


def projkv(me, x, wk, wv):
    return call(
        projkv_body, "projkv", 5, (me, x, wk, wv), [sds((NB, 2 * E), BF16)] * 4, [ANY] * 4, [SM, VM, ANY, ANY],
        [pltpu.VMEM((D, HD), BF16), pltpu.VMEM((D, HD), BF16), pltpu.VMEM((H, NB, 2 * E), BF16),
         pltpu.SemaphoreType.DMA((8,)), pltpu.SemaphoreType.DMA((4,))])


def projq_body(me, x, wq, do, o0, o1, o2, o3, wqs, scr, sem, osem):
    cps = loads(((wq, wqs),), sem)
    for c in cps:
        c.start()
    q = None
    doT = do[...].T
    for i in range(4):
        cps[i].wait()
        r = pl.ds(i * KP, KP)
        dq = dot(wqs[r, :], x[:, r], TT)
        q = dq if i == 0 else q + dq
    q = q.astype(BF16)
    for h in range(H):
        scr[h, 0:E, :] = q[h * E:(h + 1) * E]
        scr[h, E:2 * E, :] = doT[h * E:(h + 1) * E]
    send_out(me[0], scr, (o0, o1, o2, o3), osem)


def projq(me, x, wq, do):
    return call(
        projq_body, "projq", 4, (me, x, wq, do), [sds((2 * E, NB), BF16)] * 4, [ANY] * 4, [SM, VM, ANY, VM],
        [pltpu.VMEM((D, HD), BF16), pltpu.VMEM((H, 2 * E, NB), BF16),
         pltpu.SemaphoreType.DMA((4,)), pltpu.SemaphoreType.DMA((4,))])


def pack_body(a, b, c, o):
    for i, p in enumerate((a, b, c)):
        o[i * NB:(i + 1) * NB, :] = p[...]


def pack(a, b, c):
    return call(pack_body, "pack", 1, (a, b, c), sds((3 * NB, 2 * E), BF16), VM, params=SMALL)


def attn_body(core, *refs):
    kv_in, qdo_in = refs[:8], refs[8:12]
    quarters = (refs[14], refs[15], refs[12], refs[13])
    dq_mine, dq_other = refs[16:18]
    dq_out = refs[18:22]
    kv, qdo, qT, doT, s_scr, p_scr, sem = refs[22:]
    cq = [pltpu.make_async_copy(qdo_in[i], qdo.at[:, pl.ds(NB * i, NB)], sem.at[8 + i]) for i in range(4)]
    ck, at = [], 0
    for i in range(8):
        n = NB if i % 2 == 0 else 3 * NB
        ck.append(pltpu.make_async_copy(kv_in[i], kv.at[pl.ds(at, n)], sem.at[i]))
        at += n
    for c in cq + ck:
        c.start()
    for c in cq:
        c.wait()
    zz = jnp.zeros((64, NQ), BF16)
    q, do = qdo[0:E, :], qdo[E:2 * E, :]
    qT[...] = jnp.concatenate([q, zz], 0)
    doT[...] = jnp.concatenate([zz, do], 0)
    m8 = jnp.full((8, NQ), -jnp.inf, F32)
    n = NK // KC
    for i in range(n):
        if i % 2 == 0:
            ck[i].wait()
            ck[i + 1].wait()
        r = pl.ds(i * KC, KC)
        s = dot(kv[r, 0:256], qT[...])
        s_scr[r, :] = s
        m8 = jnp.maximum(m8, jnp.max(s.reshape(KC // 8, 8, NQ), axis=0))
    mc = jnp.max(m8, axis=0, keepdims=True) * C2
    l8 = r8 = jnp.zeros((8, NQ), F32)
    for i in range(n):
        r = pl.ds(i * KC, KC)
        dp = dot(kv[r, 128:384], doT[...])
        p = jnp.exp2(s_scr[r, :] * C2 - mc)
        s_scr[r, :] = dp
        p_scr[r, :] = p.astype(BF16)
        l8 = l8 + jnp.sum(p.reshape(KC // 8, 8, NQ), axis=0)
        r8 = r8 + jnp.sum((p * dp).reshape(KC // 8, 8, NQ), axis=0)
    inv = 1.0 / jnp.sum(l8, axis=0, keepdims=True)
    delta = jnp.sum(r8, axis=0, keepdims=True) * inv
    qs = (q.astype(F32) * (inv * SCALE)).astype(BF16)
    dos = (do.astype(F32) * inv).astype(BF16)
    first = core[0] == 0
    half = n // 2
    acc = None
    for i in list(range(half, n)) + list(range(half)):
        r = pl.ds(i * KC, KC)
        p = p_scr[r, :]
        ds = (p.astype(F32) * (s_scr[r, :] - delta)).astype(BF16)
        dk, dv = nt(qs, ds), nt(dos, p)
        g = dot(kv[r, 0:256].T[:E], ds)
        acc = g if acc is None else acc + g
        at = (i % 2) * KC
        quarters[i // 2][0:E, at:at + KC] = dk.astype(BF16)
        quarters[i // 2][E:2 * E, at:at + KC] = dv.astype(BF16)
    dqT = (acc * (inv * SCALE)).astype(BF16)
    dq_mine[...] = jnp.where(first, dqT[:E // 2], dqT[E // 2:])
    dq_other[...] = jnp.where(first, dqT[E // 2:], dqT[:E // 2])
    for j in range(4):
        dq_out[j][...] = dqT[:, j * NB:(j + 1) * NB]


def attn(core, kvs, qdos):
    part = [sds((2 * E, NQ), BF16)] * 4 + [sds((E // 2, NQ), BF16)] * 2
    return call(
        attn_body, "attn", 1, (core, *kvs, *qdos), part + [sds((E, NB), BF16)] * 4,
        [VM] * 10, [SM] + [ANY] * 12,
        [pltpu.VMEM((NK, 2 * E), BF16), pltpu.VMEM((2 * E, NQ), BF16), pltpu.VMEM((256, NQ), BF16),
         pltpu.VMEM((256, NQ), BF16), pltpu.VMEM((NK, NQ), F32), pltpu.VMEM((NK, NQ), BF16),
         pltpu.SemaphoreType.DMA((12,))])


W = D // 4


def add_body(a, b, o):
    o[...] = (a[...].astype(F32) + b[...].astype(F32)).astype(BF16)


def add(a, b):
    return call(add_body, "add", 1, (a, b), sds(a.shape, BF16), VM, params=SMALL)


def comb_body(core, a, t, u, *refs):
    dqs, ps, mine, other = refs[:4], refs[4:8], refs[8], refs[9]
    d = (a[...].astype(F32) + t[...].astype(F32) + u[...].astype(F32)).astype(BF16)
    for j in range(4):
        ps[j][0:E, :] = dqs[j][...]
        ps[j][E:3 * E, :] = d[:, j * NB:(j + 1) * NB]
    first = core[0] == 0
    mine[...] = jnp.where(first, d[:E], d[E:])
    other[...] = jnp.where(first, d[E:], d[:E])


def comb(core, a, t, u, dqs):
    return call(comb_body, "comb", 1, (core, a, t, u, *dqs), [sds((3 * E, NB), BF16)] * 4 + [sds((E, NQ), BF16)] * 2,
                [VM] * 6, [SM] + [VM] * 7, params=SMALL)


def gkv_body(me, d0, d1, q0, q1, *refs):
    xs, outs, (g, xv, sem) = refs[:8], refs[8:12], refs[12:]
    cps = [pltpu.make_async_copy(x, xv.at[i], sem.at[i]) for i, x in enumerate(xs)]
    for c in cps:
        c.start()
    halves = [jnp.concatenate([d0[...], q0[...]], 0), jnp.concatenate([d1[...], q1[...]], 0)]
    acc = None
    for i in range(8):
        cps[i].wait()
        k = i % 4
        p = dot(halves[i // 4][:, k * NB:(k + 1) * NB], xv[i])
        acc = p if acc is None else acc + p
    g[...] = acc
    for j, o in enumerate(outs):
        at = pl.multiple_of(lax.rem(me[0] + j, 4) * W, 128)
        o[...] = g[:, pl.ds(at, W)].astype(BF16)


def gkv(me, d0, d1, q0, q1, xs):
    n = E + E // 2
    return call(gkv_body, "gkv", 4, (me, d0, d1, q0, q1, *xs), [sds((n, W), BF16)] * 4, [VM] * 4,
                [SM] + [VM] * 4 + [ANY] * 8,
                [pltpu.VMEM((n, D), F32), pltpu.VMEM((8, NB, D), BF16), pltpu.SemaphoreType.DMA((8,))])


def fin1_body(a, b, c, d, out):
    s = ((a[...].astype(F32) + b[...].astype(F32)) + (c[...].astype(F32) + d[...].astype(F32))).T
    for i in range(32):
        out[i] = s[12 * i:12 * i + 12, :].astype(BF16)


def fin1(a):
    return call(fin1_body, "fin1", 1, tuple(a), sds((32, 12, 288), BF16), VM, params=SMALL)


def fin2_body(s, gq_o, gk_o, gv_o):
    for x in range(4):
        for c in range(2):
            v = None
            for zl in range(2):
                for zh in range(2):
                    t = s[((zl * 4 + x) * 2 + zh) * 2 + c].astype(F32)
                    v = t if v is None else v + t
            (gk_o, gv_o)[c][:, x * E:(x + 1) * E] = v[:, :E]
            at = x * E + c * (E // 2)
            gq_o[:, at:at + E // 2] = v[:, E:]


def fin2(s):
    return call(fin2_body, "fin2", 1, (s,), [sds((12, HD), F32)] * 3, [VM] * 3, params=SMALL)


def back_body(count, me, *refs):
    ps, w_in = refs[:4], refs[4:4 + count]
    rest = refs[4 + count:]
    acc = None
    if count == 2:
        acc, rest = rest[0][...], rest[1:]
    out, d, ws, sem = rest
    cps = [pltpu.make_async_copy(w, ws.at[i], sem.at[i]) for i, w in enumerate(w_in)]
    for c in cps:
        c.start()
    for j, p in enumerate(ps):
        at = pl.ds(pl.multiple_of(lax.rem(me[0] + j, H) * E, E), E)
        for i in range(count):
            d[i, at, :] = p[i * E:(i + 1) * E, :]
    for i in range(count):
        x = d[i].T
        cps[i].wait()
        g = nt(x, ws[i])
        acc = g if acc is None else acc + g
    out[...] = acc.astype(out.dtype)


def back(me, ps, ws, *acc):
    n = len(ws)
    return call(functools.partial(back_body, n), "back", 2, (me, *ps, *ws, *acc),
                sds((NB, D), BF16), VM, [SM] + [VM] * 4 + [ANY] * n + [VM] * len(acc),
                [pltpu.VMEM((n, HD, NB), BF16), pltpu.VMEM((n, D, HD), BF16), pltpu.SemaphoreType.DMA((n,))], SMALL)


def ahead(x, axis, j, n):
    return lax.ppermute(x, axis, [(i, (i + j) % n) for i in range(n)])


def core_swap(x):
    return ahead(x, "c", 1, 2)


def around(pieces, axis, sign=1):
    return [pieces[0]] + [ahead(pieces[j], axis, (sign * j) % 4, 4) for j in (1, 2, 3)]


def after(x, y):
    return lax.optimization_barrier((x, y))[0]


def shards(normed, w_query, w_key, w_value, grad_context):
    rows = normed[0]
    cot = grad_context[0]
    mx = lax.axis_index("x").reshape(1)
    my = lax.axis_index("y").reshape(1)
    mc = lax.axis_index("c").reshape(1)
    barrier = lax.optimization_barrier
    kv = projkv(mx, rows, w_key, w_value)
    own0, far0, near0 = kv[0], ahead(kv[0], "zh", 1, 2), core_swap(kv[0])
    kv = around(kv, "x")
    qdo = projq(mx, rows, w_query, cot)
    kv, qdo, far0, near0 = barrier((tuple(kv[1:]), tuple(qdo), far0, near0))
    own = pack(*kv)
    far, near, qdo = barrier((ahead(own, "zh", 1, 2), core_swap(own), tuple(around(qdo, "x"))))
    diag, diag0, rows_n = core_swap(far), core_swap(after(far0, far)), core_swap(after(rows, far))
    x2_from = after(rows, diag)
    xs = [rows, ahead(after(rows, qdo), "x", 1, 4), ahead(x2_from, "x", 2, 4), ahead(after(rows, qdo), "x", 3, 4)]
    diag, diag0, rows_n = barrier((diag, diag0, rows_n))
    kvs = [own0, own, near0, near, far0, far, diag0, diag]
    parts = attn(mc, kvs, qdo)
    parts, x1, x3 = barrier((tuple(parts), xs[1], xs[3]))
    rsame, rother, lsame, lother, dq0, dq1, *dqT = parts
    t, t2 = barrier((core_swap(rother), core_swap(lother)))
    half = add(rsame, t)
    u = ahead(half, "zh", 1, 2)
    x1n, x3n, dqn = barrier(tuple(core_swap(after(v, half)) for v in (x1, x3, dq1)))
    x2n = core_swap(after(xs[2], x1n))
    u, t2, x2n, x1n, x3n, dqn = barrier((u, t2, x2n, x1n, x3n, dqn))
    *ps, dmine, dother = comb(mc, lsame, t2, u, dqT)
    ps = around(ps, "x", -1)
    s4 = gkv(my, dmine, core_swap(dother), dq0, dqn, [rows, x1, xs[2], x3, rows_n, x1n, x2n, x3n])
    s4, ps = barrier((tuple(s4), tuple(ps)))
    s4 = around(s4, "y")
    out = back(mx, ps, [w_query, w_key, w_value])
    s4, out = barrier((tuple(s4), out))
    d_normed = out.reshape(normed.shape)
    s = lax.all_to_all(fin1(s4), ("zl", "x", "zh", "c"), 0, 0, tiled=True)
    grad_q, grad_k, grad_v = fin2(s)
    return d_normed, grad_q, grad_k, grad_v


def solution(mesh):
    split_mesh = Mesh(mesh.devices.reshape(4, 2, 4, 2, 2), ("y", "zl", "x", "zh", "c"))
    dp, seq = ("y", "zl"), ("x", "zh", "c")
    rows = P(dp, seq, None)
    grads = P(dp + seq, None)
    return jax.shard_map(
        shards, mesh=split_mesh, in_specs=(rows, P(), P(), P(), rows),
        out_specs=(rows, grads, grads, grads), check_vma=False,
    )
```

time: 552 us -> 146 us (0.26)
  waiting for transfers between devices: 406 us -> 45.8 us
  matrix products: 86.1 us -> 0 us
  Pallas kernels: 0 us -> 43.3 us
  local copies, waits for them, and re-layouts: 44 us -> 5.11 us
  starting transfers between devices: 0.39 us -> 36.3 us
  blocking collectives: 0 us -> 14.7 us
  between operations: 13.9 us -> 0.92 us
    unnamed x6 -> x0, waiting for transfers between devices: 168 us -> none
    reduce_scatter x2 -> x0, waiting for transfers between devices: 133 us -> none  [the longest x1 88.3 us: shards(): lax.psum_scatter(dv_term.astype(jnp.bfloat16), 'seq', scatter_dimension=0...]
    all_gather x2 -> x0, waiting for transfers between devices: 105 us -> none  [the longest x1 59.8 us: shards(): lax.all_gather(key, 'seq', axis=0, tiled=True)]
    dot_general x12 -> x0, matrix products: 53.2 us -> none  [the longest x1 10.5 us: shards(): jnp.einsum('hqk,qhe->khe', prob_b, cotan3, preferred_element_type=jnp.flo...]
    ppermute x0 -> x30, waiting for transfers between devices: none -> 45.8 us  [ahead(): return lax.ppermute(x, axis, [(i, (i + j) % n) for i in range(n)])]
    pallas_call x0 -> x10, Pallas kernels: none -> 43.3 us  [call(): pl.pallas_call(body, in_specs=in_specs or [VM] * len(ins), out_specs=out_...]
    ppermute x0 -> x30, starting transfers between devices: none -> 36.3 us  [ahead(): return lax.ppermute(x, axis, [(i, (i + j) % n) for i in range(n)])]
    sub x2 -> x0, matrix products: 32.9 us -> none  [the longest x1 21.9 us: shards(): dscore = (probs * (dprob - delta) * scale).astype(jnp.bfloat16)]
  transfers between devices with their start and end apart: 5 -> 30, of which waited for: 5 -> 13; matrix products, arithmetic and copies ran while one was open for 14% -> 0% of each run, Pallas kernels for 0% -> 24%
where the time goes in v2:
time: 146 us
  waiting for transfers between devices  45.8 us (31%)
  Pallas kernels  43.3 us (30%)
  starting transfers between devices  36.3 us (25%)
  blocking collectives  14.7 us (10%)
  local copies, waits for them, and re-layouts  5.11 us (4%)
    ppermute x30, waiting for transfers between devices, ahead(): return lax.ppermute(x, axis, [(i, (i + j) % n) for i in range(n)])  45.8 us
    pallas_call x10, Pallas kernels, call(): pl.pallas_call(body, in_specs=in_specs or [VM] * len(ins), out_specs=out_...  43.3 us
    ppermute x30, starting transfers between devices, ahead(): return lax.ppermute(x, axis, [(i, (i + j) % n) for i in range(n)])  36.3 us
    all_to_all x1, blocking collectives, shards(): s = lax.all_to_all(fin1(s4), ('zl', 'x', 'zh', 'c'), 0, 0, tiled=True)  14.7 us
    unnamed x52, local copies, waits for them, and re-layouts  5.11 us
  transfers between devices with their start and end apart: 30, of which 13 were waited for; matrix products, arithmetic and copies ran while one was open for 0% of the time, Pallas kernels for 24%

profile of v2, /device:TPU:1, one launch (start us, length us, event | category | flops | bytes accessed | tf_op | source)
XLA Modules:
  0.0 146.1 jit_solution(7528225993669638163)
XLA Ops:
  0.6 5.8 %projkv.1 = (bf16[256,384]{1,0:T(8,128)(2,1)}, bf16[256,384]{1,0:T(8,128)(2,1)}, bf16[256,384]{1,0:T(8,128)(2,1)}, bf16[256,384]{1,0:T(8,128)(2,1)}) custom-call(s32[1]{0:T(128)} %bitcast.2.me, bf16[256,1536]{1,0:T(8,128)(2,1)} %bitcast.6, bf16[1536,768]{1,0:T(8,128)(2,1)} %refs_5_.1, bf16[1536,768]{1,0:T(8,128)(2,1)} %refs_6_.1), custom_call_target="tpu_custom_call" | custom-call | flops 1048576 | bytes 500000 | tf_op jit(solution)/shard_map/projkv/pallas_call | solution.py:39
  6.5 2.1 %collective-permute-start = (bf16[256,384]{1,0:T(8,128)(2,1)}, bf16[256,384]{1,0:T(8,128)(2,1)S(1)}, u32[]{:S(2)}, u32[]{:S(2)}) collective-permute-start(bf16[256,384]{1,0:T(8,128)(2,1)} %get-tuple-element.98), channel_id=1, source_target_pairs={{0,4},{4,8},{8,12},{12,0},{1,5},{5,9},{9,13},{13,1},{2,6},{6,10},{... | collective-permute-start | bytes 589832 | tf_op jit(solution)/shard_map/ppermute | solution.py:312
  8.6 2.4 %collective-permute-start.1 = (bf16[256,384]{1,0:T(8,128)(2,1)}, bf16[256,384]{1,0:T(8,128)(2,1)S(1)}, u32[]{:S(2)}, u32[]{:S(2)}) collective-permute-start(bf16[256,384]{1,0:T(8,128)(2,1)} %get-tuple-element.99), channel_id=1, source_target_pairs={{0,8},{4,12},{8,0},{12,4},{1,9},{5,13},{9,1},{13,5},{2,10},{6,14},... | collective-permute-start | bytes 589832 | tf_op jit(solution)/shard_map/ppermute | solution.py:312
  11.0 1.2 collective-permute-start.2
  12.2 1.5 %collective-permute-start.4 = (bf16[256,384]{1,0:T(8,128)(2,1)}, bf16[256,384]{1,0:T(8,128)(2,1)S(1)}, u32[]{:S(2)}, u32[]{:S(2)}) collective-permute-start(bf16[256,384]{1,0:T(8,128)(2,1)} %get-tuple-element.97.refs_0_), channel_id=1, source_target_pairs={{0,1},{1,0},{2,3},{3,2},{4,5},{5,4},{6,7},{7,6},{8,9},{9,8},{10,11... | collective-permute-start | bytes 589832 | tf_op jit(solution)/shard_map/ppermute | solution.py:312
  13.7 3.6 %collective-permute-start.3 = (bf16[256,384]{1,0:T(8,128)(2,1)}, bf16[256,384]{1,0:T(8,128)(2,1)}, u32[]{:S(2)}, u32[]{:S(2)}) collective-permute-start(bf16[256,384]{1,0:T(8,128)(2,1)} %get-tuple-element.97.refs_0_), channel_id=1, source_target_pairs={{0,2},{2,0},{1,3},{3,1},{4,6},{6,4},{5,7},{7,5},{8,10},{10,8},{9,1... | collective-permute-start | bytes 589832 | tf_op jit(solution)/shard_map/ppermute | solution.py:312
  17.3 5.2 %projq.1 = (bf16[384,256]{1,0:T(8,128)(2,1)}, bf16[384,256]{1,0:T(8,128)(2,1)}, bf16[384,256]{1,0:T(8,128)(2,1)}, bf16[384,256]{1,0:T(8,128)(2,1)}) custom-call(s32[1]{0:T(128)} %bitcast.2.me, bf16[256,1536]{1,0:T(8,128)(2,1)} %bitcast.7, bf16[1536,768]{1,0:T(8,128)(2,1)} %refs_4_.1, bf16[256,768]{1,0:T(8,128)(2,1)} %bitcast.14), custom_call_target="tpu_custom_call" | custom-call | flops 1048576 | bytes 400000 | tf_op jit(solution)/shard_map/projq/pallas_call | solution.py:39
  22.9 0.7 collective-permute-start.6
  23.6 3.0 %collective-permute-start.5 = (bf16[768,384]{1,0:T(8,128)(2,1)S(1)}, bf16[768,384]{1,0:T(8,128)(2,1)}, u32[]{:S(2)}, u32[]{:S(2)}) collective-permute-start(bf16[768,384]{1,0:T(8,128)(2,1)S(1)} %pack.1.refs_1_), channel_id=1, source_target_pairs={{0,2},{2,0},{1,3},{3,1},{4,6},{6,4},{5,7},{7,5},{8,10},{10,8},{9,1... | collective-permute-start | bytes 1769480 | tf_op jit(solution)/shard_map/ppermute | solution.py:312
  26.9 1.3 collective-permute-start.8
  28.2 1.3 collective-permute-start.9
  29.5 8.9 %collective-permute-done.7.refs_9_ = bf16[384,256]{1,0:T(8,128)(2,1)S(1)} collective-permute-done((bf16[384,256]{1,0:T(8,128)(2,1)}, bf16[384,256]{1,0:T(8,128)(2,1)S(1)}, u32[]{:S(2)}, u32[]{:S(2)}) %collective-permute-start.7) | collective-permute-done | bytes 196640 | tf_op jit(solution)/shard_map/ppermute | solution.py:312
  38.5 0.3 collective-permute-done.9.refs_11_
  39.5 0.6 collective-permute-done.5.refs_5_
  40.1 0.9 collective-permute-start.12
  41.0 2.3 %collective-permute-start.14 = (bf16[256,1536]{1,0:T(8,128)(2,1)S(1)}, bf16[256,1536]{1,0:T(8,128)(2,1)S(1)}, u32[]{:S(2)}, u32[]{:S(2)}) collective-permute-start(bf16[256,1536]{1,0:T(8,128)(2,1)S(1)} %bitcast.10), channel_id=1, source_target_pairs={{0,12},{4,0},{8,4},{12,8},{1,13},{5,1},{9,5},{13,9},{2,14},{6,2},{... | collective-permute-start | bytes 2359304 | tf_op jit(solution)/shard_map/ppermute | solution.py:312
  43.3 0.4 collective-permute-start.10
  43.8 2.1 %collective-permute-done.11.refs_6_ = bf16[256,384]{1,0:T(8,128)(2,1)} collective-permute-done((bf16[256,384]{1,0:T(8,128)(2,1)}, bf16[256,384]{1,0:T(8,128)(2,1)}, u32[]{:S(2)}, u32[]{:S(2)}) %collective-permute-start.11) | collective-permute-done | bytes 196640 | tf_op jit(solution)/shard_map/ppermute | solution.py:312
  45.9 19.3 %attn.1 = (bf16[384,1024]{1,0:T(8,128)(2,1)}, bf16[384,1024]{1,0:T(8,128)(2,1)}, bf16[384,1024]{1,0:T(8,128)(2,1)}, bf16[384,1024]{1,0:T(8,128)(2,1)}, bf16[96,1...) custom-call(s32[1]{0:T(128)} %bitcast.1.core, ...), custom_call_target="tpu_custom_call" | custom-call | flops 1048576 | bytes 100000 | tf_op jit(solution)/shard_map/attn/pallas_call | solution.py:39
  65.3 0.4 collective-permute-start.15
  65.9 2.0 %collective-permute-done.15.b = bf16[384,1024]{1,0:T(8,128)(2,1)S(1)} collective-permute-done((bf16[384,1024]{1,0:T(8,128)(2,1)}, bf16[384,1024]{1,0:T(8,128)(2,1)S(1)}, u32[]{:S(2)}, u32[]{:S(2)}) %collective-permute-start.15) | collective-permute-done | bytes 786464 | tf_op jit(solution)/shard_map/ppermute | solution.py:312
  67.9 1.1 collective-permute-done.16.t
  69.0 1.1 copy-done.5
  70.3 0.4 collective-permute-start.19
  70.9 1.2 collective-permute-start.18
  72.2 0.6 collective-permute-start.21
  72.8 2.0 %collective-permute-start.17 = (bf16[384,1024]{1,0:T(8,128)(2,1)S(1)}, bf16[384,1024]{1,0:T(8,128)(2,1)S(1)}, u32[]{:S(2)}, u32[]{:S(2)}) collective-permute-start(bf16[384,1024]{1,0:T(8,128)(2,1)S(1)} %add.1), channel_id=1, source_target_pairs={{0,2},{2,0},{1,3},{3,1},{4,6},{6,4},{5,7},{7,5},{8,10},{10,8},{9,1... | collective-permute-start | bytes 2359304 | tf_op jit(solution)/shard_map/ppermute | solution.py:312
  74.9 16.3 %collective-permute-done.18.refs_2_ = bf16[256,1536]{1,0:T(8,128)(2,1)S(1)} collective-permute-done((bf16[256,1536]{1,0:T(8,128)(2,1)S(1)}, bf16[256,1536]{1,0:T(8,128)(2,1)S(1)}, u32[]{:S(2)}, u32[]{:S(2)}) %collective-permute-start.18) | collective-permute-done | bytes 786464 | tf_op jit(solution)/shard_map/ppermute | solution.py:312
  91.2 1.2 collective-permute-start.22
  92.4 1.1 collective-permute-done.17.u
  93.5 0.9 collective-permute-done.22.refs_6_
  94.5 1.1 comb.1
  95.5 0.7 copy-done.6
  96.3 0.4 collective-permute-start.23
  96.7 2.9 %collective-permute-start.24 = (bf16[576,256]{1,0:T(8,128)(2,1)}, bf16[576,256]{1,0:T(8,128)(2,1)S(1)}, u32[]{:S(2)}, u32[]{:S(2)}) collective-permute-start(bf16[576,256]{1,0:T(8,128)(2,1)} %get-tuple-element.171), channel_id=1, source_target_pairs={{0,12},{4,0},{8,4},{12,8},{1,13},{5,1},{9,5},{13,9},{2,14},{6,2},{... | collective-permute-start | bytes 884744 | tf_op jit(solution)/shard_map/ppermute | solution.py:312
  99.6 0.6 collective-permute-start.25
  100.3 0.8 copy-done.19
  101.0 6.7 %gkv.1 = (bf16[288,384]{1,0:T(8,128)(2,1)}, bf16[288,384]{1,0:T(8,128)(2,1)}, bf16[288,384]{1,0:T(8,128)(2,1)}, bf16[288,384]{1,0:T(8,128)(2,1)}) custom-call(s32[1]{0:T(128)} %bitcast.me, bf16[192,1024]{1,0:T(8,128)(2,1)} %copy-done.6, bf16[192,1024]{1,0:T(8,128)(2,1)} %copy-done.19, bf16[96,1024]{1,0:T(8,128)(2,1)} %get-tuple-element.160.q0, ...), custom_call_target="tpu_custom_call" | custom-call | flops 1048576 | bytes 400000 | tf_op jit(solution)/shard_map/gkv/pallas_call | solution.py:39
  107.7 4.6 %collective-permute-done.24.refs_1_ = bf16[576,256]{1,0:T(8,128)(2,1)S(1)} collective-permute-done((bf16[576,256]{1,0:T(8,128)(2,1)}, bf16[576,256]{1,0:T(8,128)(2,1)S(1)}, u32[]{:S(2)}, u32[]{:S(2)}) %collective-permute-start.24) | collective-permute-done | bytes 294944 | tf_op jit(solution)/shard_map/ppermute | solution.py:312
  112.4 4.2 %collective-permute-done.26.refs_3_ = bf16[576,256]{1,0:T(8,128)(2,1)S(1)} collective-permute-done((bf16[576,256]{1,0:T(8,128)(2,1)S(1)}, bf16[576,256]{1,0:T(8,128)(2,1)S(1)}, u32[]{:S(2)}, u32[]{:S(2)}) %collective-permute-start.26) | collective-permute-done | bytes 294944 | tf_op jit(solution)/shard_map/ppermute | solution.py:312
  116.6 1.3 collective-permute-start.27
  117.8 2.6 %collective-permute-start.28 = (bf16[288,384]{1,0:T(8,128)(2,1)}, bf16[288,384]{1,0:T(8,128)(2,1)S(1)}, u32[]{:S(2)}, u32[]{:S(2)}) collective-permute-start(bf16[288,384]{1,0:T(8,128)(2,1)} %get-tuple-element.176), channel_id=1, source_target_pairs={{0,64},{32,96},{64,0},{96,32},{1,65},{33,97},{65,1},{97,33},{2,66}... | collective-permute-start | bytes 663560 | tf_op jit(solution)/shard_map/ppermute | solution.py:312
  120.5 1.1 collective-permute-start.29
  121.5 1.7 %copy-done.2 = bf16[1536,768]{1,0:T(8,128)(2,1)S(1)} copy-done((bf16[1536,768]{1,0:T(8,128)(2,1)S(1)}, bf16[1536,768]{1,0:T(8,128)(2,1)}, u32[]{:S(2)}) %copy-start.2) | copy-done | bytes 2359320
  123.2 4.0 %back.1 = bf16[256,1536]{1,0:T(8,128)(2,1)} custom-call(s32[1]{0:T(128)} %bitcast.2.me, bf16[576,256]{1,0:T(8,128)(2,1)S(1)} %get-tuple-element.178.refs_0_, bf16[576,256]{1,0:T(8,128)(2,1)S(1)} %collective-permute-done.24.refs_1_, bf16[576,256]{1,0:T(8,128)(2,1)S(1)} %collective-permute-done.25.refs_2_, ...), custom_call_target="tpu_custom_call" | custom-call | flops 1048576 | bytes 200000 | tf_op jit(solution)/shard_map/back/pallas_call | solution.py:39
  127.3 3.2 %collective-permute-done.28.c = bf16[288,384]{1,0:T(8,128)(2,1)S(1)} collective-permute-done((bf16[288,384]{1,0:T(8,128)(2,1)}, bf16[288,384]{1,0:T(8,128)(2,1)S(1)}, u32[]{:S(2)}, u32[]{:S(2)}) %collective-permute-start.28) | collective-permute-done | bytes 221216 | tf_op jit(solution)/shard_map/ppermute | solution.py:312
  130.7 14.7 %all_to_all.5.s = bf16[32,12,288]{2,1,0:T(8,128)(2,1)S(1)} all-to-all(bf16[32,12,288]{2,1,0:T(8,128)(2,1)S(1)} %fin1.1), channel_id=1, replica_groups=mesh['y'=4,'zl'=2,'x'=4,'zh'=2,'c'=2] {'zl','x','zh','c'}, dimensions={0} | all-to-all | bytes 442368 | tf_op jit(solution)/shard_map/all_to_all | solution.py:363
  145.4 0.8 fin2.1
  (75 shorter events, 2.4 us)
Async XLA Ops:
  6.5 16.1 %collective-permute-start = (bf16[256,384]{1,0:T(8,128)(2,1)}, bf16[256,384]{1,0:T(8,128)(2,1)S(1)}, u32[]{:S(2)}, u32[]{:S(2)}) collective-permute-start(bf16[256,384]{1,0:T(8,128)(2,1)} %get-tuple-element.98), channel_id=1, source_target_pairs={{0,4},{4,8},{8,12},{12,0},{1,5},{5,9},{9,13},{13,1},{2,6},{6,10},{... | collective-permute-start | bytes 589832 | tf_op jit(solution)/shard_map/ppermute | solution.py:312
  8.6 14.0 %collective-permute-start.1 = (bf16[256,384]{1,0:T(8,128)(2,1)}, bf16[256,384]{1,0:T(8,128)(2,1)S(1)}, u32[]{:S(2)}, u32[]{:S(2)}) collective-permute-start(bf16[256,384]{1,0:T(8,128)(2,1)} %get-tuple-element.99), channel_id=1, source_target_pairs={{0,8},{4,12},{8,0},{12,4},{1,9},{5,13},{9,1},{13,5},{2,10},{6,14},... | collective-permute-start | bytes 589832 | tf_op jit(solution)/shard_map/ppermute | solution.py:312
  11.0 11.6 %collective-permute-start.2 = (bf16[256,384]{1,0:T(8,128)(2,1)}, bf16[256,384]{1,0:T(8,128)(2,1)S(1)}, u32[]{:S(2)}, u32[]{:S(2)}) collective-permute-start(bf16[256,384]{1,0:T(8,128)(2,1)} %get-tuple-element.100), channel_id=1, source_target_pairs={{0,12},{4,0},{8,4},{12,8},{1,13},{5,1},{9,5},{13,9},{2,14},{6,2},{... | collective-permute-start | bytes 589832 | tf_op jit(solution)/shard_map/ppermute | solution.py:312
  12.2 10.4 %collective-permute-start.4 = (bf16[256,384]{1,0:T(8,128)(2,1)}, bf16[256,384]{1,0:T(8,128)(2,1)S(1)}, u32[]{:S(2)}, u32[]{:S(2)}) collective-permute-start(bf16[256,384]{1,0:T(8,128)(2,1)} %get-tuple-element.97.refs_0_), channel_id=1, source_target_pairs={{0,1},{1,0},{2,3},{3,2},{4,5},{5,4},{6,7},{7,6},{8,9},{9,8},{10,11... | collective-permute-start | bytes 589832 | tf_op jit(solution)/shard_map/ppermute | solution.py:312
  13.7 9.2 %collective-permute-start.3 = (bf16[256,384]{1,0:T(8,128)(2,1)}, bf16[256,384]{1,0:T(8,128)(2,1)}, u32[]{:S(2)}, u32[]{:S(2)}) collective-permute-start(bf16[256,384]{1,0:T(8,128)(2,1)} %get-tuple-element.97.refs_0_), channel_id=1, source_target_pairs={{0,2},{2,0},{1,3},{3,1},{4,6},{6,4},{5,7},{7,5},{8,10},{10,8},{9,1... | collective-permute-start | bytes 589832 | tf_op jit(solution)/shard_map/ppermute | solution.py:312
  17.3 22.8 %copy-start.12 = (bf16[1,256,1536]{2,1,0:T(8,128)(2,1)S(1)}, bf16[1,256,1536]{2,1,0:T(8,128)(2,1)}, u32[]{:S(2)}) copy-start(bf16[1,256,1536]{2,1,0:T(8,128)(2,1)} %param.5) | copy-start | bytes 2359300
  22.6 18.4 %copy-start.20 = (bf16[256,384]{1,0:T(8,128)(2,1)}, bf16[256,384]{1,0:T(8,128)(2,1)S(1)}, u32[]{:S(2)}) copy-start(bf16[256,384]{1,0:T(8,128)(2,1)S(1)} %collective-permute-done.4.refs_2_) | copy-start | bytes 589828
  22.9 23.0 %copy-start.3 = (bf16[768,384]{1,0:T(8,128)(2,1)}, bf16[768,384]{1,0:T(8,128)(2,1)S(1)}, u32[]{:S(2)}) copy-start(bf16[768,384]{1,0:T(8,128)(2,1)S(1)} %pack.1.refs_1_) | copy-start | bytes 1769476
  22.9 15.9 %collective-permute-start.6 = (bf16[768,384]{1,0:T(8,128)(2,1)S(1)}, bf16[768,384]{1,0:T(8,128)(2,1)S(1)}, u32[]{:S(2)}, u32[]{:S(2)}) collective-permute-start(bf16[768,384]{1,0:T(8,128)(2,1)S(1)} %pack.1.refs_1_), channel_id=1, source_target_pairs={{0,1},{1,0},{2,3},{3,2},{4,5},{5,4},{6,7},{7,6},{8,9},{9,8},{10,11... | collective-permute-start | bytes 1769480 | tf_op jit(solution)/shard_map/ppermute | solution.py:312
  23.6 16.5 %collective-permute-start.5 = (bf16[768,384]{1,0:T(8,128)(2,1)S(1)}, bf16[768,384]{1,0:T(8,128)(2,1)}, u32[]{:S(2)}, u32[]{:S(2)}) collective-permute-start(bf16[768,384]{1,0:T(8,128)(2,1)S(1)} %pack.1.refs_1_), channel_id=1, source_target_pairs={{0,2},{2,0},{1,3},{3,1},{4,6},{6,4},{5,7},{7,5},{8,10},{10,8},{9,1... | collective-permute-start | bytes 1769480 | tf_op jit(solution)/shard_map/ppermute | solution.py:312
  26.6 11.9 %collective-permute-start.7 = (bf16[384,256]{1,0:T(8,128)(2,1)}, bf16[384,256]{1,0:T(8,128)(2,1)S(1)}, u32[]{:S(2)}, u32[]{:S(2)}) collective-permute-start(bf16[384,256]{1,0:T(8,128)(2,1)} %get-tuple-element.110), channel_id=1, source_target_pairs={{0,4},{4,8},{8,12},{12,0},{1,5},{5,9},{9,13},{13,1},{2,6},{6,10},{... | collective-permute-start | bytes 589832 | tf_op jit(solution)/shard_map/ppermute | solution.py:312
  26.9 11.6 %collective-permute-start.8 = (bf16[384,256]{1,0:T(8,128)(2,1)}, bf16[384,256]{1,0:T(8,128)(2,1)S(1)}, u32[]{:S(2)}, u32[]{:S(2)}) collective-permute-start(bf16[384,256]{1,0:T(8,128)(2,1)} %get-tuple-element.111), channel_id=1, source_target_pairs={{0,8},{4,12},{8,0},{12,4},{1,9},{5,13},{9,1},{13,5},{2,10},{6,14},... | collective-permute-start | bytes 589832 | tf_op jit(solution)/shard_map/ppermute | solution.py:312
  28.2 10.6 %collective-permute-start.9 = (bf16[384,256]{1,0:T(8,128)(2,1)}, bf16[384,256]{1,0:T(8,128)(2,1)S(1)}, u32[]{:S(2)}, u32[]{:S(2)}) collective-permute-start(bf16[384,256]{1,0:T(8,128)(2,1)} %get-tuple-element.112), channel_id=1, source_target_pairs={{0,12},{4,0},{8,4},{12,8},{1,13},{5,1},{9,5},{13,9},{2,14},{6,2},{... | collective-permute-start | bytes 589832 | tf_op jit(solution)/shard_map/ppermute | solution.py:312
  39.5 6.4 %copy-start.18 = (bf16[768,384]{1,0:T(8,128)(2,1)}, bf16[768,384]{1,0:T(8,128)(2,1)S(1)}, u32[]{:S(2)}) copy-start(bf16[768,384]{1,0:T(8,128)(2,1)S(1)} %collective-permute-done.6.refs_3_) | copy-start | bytes 1769476
  40.1 5.8 %collective-permute-start.12 = (bf16[256,1536]{1,0:T(8,128)(2,1)S(1)}, bf16[256,1536]{1,0:T(8,128)(2,1)S(1)}, u32[]{:S(2)}, u32[]{:S(2)}) collective-permute-start(bf16[256,1536]{1,0:T(8,128)(2,1)S(1)} %bitcast.9), channel_id=1, source_target_pairs={{0,1},{1,0},{2,3},{3,2},{4,5},{5,4},{6,7},{7,6},{8,9},{9,8},{10,11... | collective-permute-start | bytes 2359304 | tf_op jit(solution)/shard_map/ppermute | solution.py:312
  41.0 24.3 %collective-permute-start.14 = (bf16[256,1536]{1,0:T(8,128)(2,1)S(1)}, bf16[256,1536]{1,0:T(8,128)(2,1)S(1)}, u32[]{:S(2)}, u32[]{:S(2)}) collective-permute-start(bf16[256,1536]{1,0:T(8,128)(2,1)S(1)} %bitcast.10), channel_id=1, source_target_pairs={{0,12},{4,0},{8,4},{12,8},{1,13},{5,1},{9,5},{13,9},{2,14},{6,2},{... | collective-permute-start | bytes 2359304 | tf_op jit(solution)/shard_map/ppermute | solution.py:312
  43.3 22.0 %collective-permute-start.13 = (bf16[256,1536]{1,0:T(8,128)(2,1)S(1)}, bf16[256,1536]{1,0:T(8,128)(2,1)}, u32[]{:S(2)}, u32[]{:S(2)}) collective-permute-start(bf16[256,1536]{1,0:T(8,128)(2,1)S(1)} %bitcast.11), channel_id=1, source_target_pairs={{0,4},{4,8},{8,12},{12,0},{1,5},{5,9},{9,13},{13,1},{2,6},{6,10},{... | collective-permute-start | bytes 2359304 | tf_op jit(solution)/shard_map/ppermute | solution.py:312
  43.3 2.6 %collective-permute-start.10 = (bf16[768,384]{1,0:T(8,128)(2,1)}, bf16[768,384]{1,0:T(8,128)(2,1)}, u32[]{:S(2)}, u32[]{:S(2)}) collective-permute-start(bf16[768,384]{1,0:T(8,128)(2,1)} %collective-permute-done.5.refs_5_), channel_id=1, source_target_pairs={{0,1},{1,0},{2,3},{3,2},{4,5},{5,4},{6,7},{7,6},{8,9},{9,8},{10,11... | collective-permute-start | bytes 1769480 | tf_op jit(solution)/shard_map/ppermute | solution.py:312
  43.6 2.3 %collective-permute-start.11 = (bf16[256,384]{1,0:T(8,128)(2,1)}, bf16[256,384]{1,0:T(8,128)(2,1)}, u32[]{:S(2)}, u32[]{:S(2)}) collective-permute-start(bf16[256,384]{1,0:T(8,128)(2,1)} %collective-permute-done.3.refs_4_), channel_id=1, source_target_pairs={{0,1},{1,0},{2,3},{3,2},{4,5},{5,4},{6,7},{7,6},{8,9},{9,8},{10,11... | collective-permute-start | bytes 589832 | tf_op jit(solution)/shard_map/ppermute | solution.py:312
  45.9 24.4 %copy-start.13 = (bf16[256,1536]{1,0:T(8,128)(2,1)}, bf16[256,1536]{1,0:T(8,128)(2,1)S(1)}, u32[]{:S(2)}) copy-start(bf16[256,1536]{1,0:T(8,128)(2,1)S(1)} %collective-permute-done.12.refs_4_) | copy-start | bytes 2359300
  65.2 29.2 %copy-start.4 = (bf16[384,1024]{1,0:T(8,128)(2,1)S(1)}, bf16[384,1024]{1,0:T(8,128)(2,1)}, u32[]{:S(2)}) copy-start(bf16[384,1024]{1,0:T(8,128)(2,1)} %get-tuple-element.135.a) | copy-start | bytes 2359300
  65.3 28.2 %copy-start.14 = (bf16[256,1536]{1,0:T(8,128)(2,1)}, bf16[256,1536]{1,0:T(8,128)(2,1)S(1)}, u32[]{:S(2)}) copy-start(bf16[256,1536]{1,0:T(8,128)(2,1)S(1)} %collective-permute-done.14.refs_3_) | copy-start | bytes 2359300
  65.3 2.6 %collective-permute-start.15 = (bf16[384,1024]{1,0:T(8,128)(2,1)}, bf16[384,1024]{1,0:T(8,128)(2,1)S(1)}, u32[]{:S(2)}, u32[]{:S(2)}) collective-permute-start(bf16[384,1024]{1,0:T(8,128)(2,1)} %get-tuple-element.137), channel_id=1, source_target_pairs={{0,1},{1,0},{2,3},{3,2},{4,5},{5,4},{6,7},{7,6},{8,9},{9,8},{10,11... | collective-permute-start | bytes 2359304 | tf_op jit(solution)/shard_map/ppermute | solution.py:312
  65.7 3.3 %collective-permute-start.16 = (bf16[384,1024]{1,0:T(8,128)(2,1)}, bf16[384,1024]{1,0:T(8,128)(2,1)S(1)}, u32[]{:S(2)}, u32[]{:S(2)}) collective-permute-start(bf16[384,1024]{1,0:T(8,128)(2,1)} %get-tuple-element.138), channel_id=1, source_target_pairs={{0,1},{1,0},{2,3},{3,2},{4,5},{5,4},{6,7},{7,6},{8,9},{9,8},{10,11... | collective-permute-start | bytes 2359304 | tf_op jit(solution)/shard_map/ppermute | solution.py:312
  70.1 24.3 %copy-start.8 = (bf16[192,256]{1,0:T(8,128)(2,1)S(1)}, bf16[192,256]{1,0:T(8,128)(2,1)}, u32[]{:S(2)}) copy-start(bf16[192,256]{1,0:T(8,128)(2,1)} %get-tuple-element.154.refs_0_) | copy-start | bytes 294916
  70.1 24.3 %copy-start.9 = (bf16[192,256]{1,0:T(8,128)(2,1)S(1)}, bf16[192,256]{1,0:T(8,128)(2,1)}, u32[]{:S(2)}) copy-start(bf16[192,256]{1,0:T(8,128)(2,1)} %get-tuple-element.155.refs_1_) | copy-start | bytes 294916
  70.1 24.3 %copy-start.10 = (bf16[192,256]{1,0:T(8,128)(2,1)S(1)}, bf16[192,256]{1,0:T(8,128)(2,1)}, u32[]{:S(2)}) copy-start(bf16[192,256]{1,0:T(8,128)(2,1)} %get-tuple-element.156.refs_2_) | copy-start | bytes 294916
  70.1 24.3 %copy-start.11 = (bf16[192,256]{1,0:T(8,128)(2,1)S(1)}, bf16[192,256]{1,0:T(8,128)(2,1)}, u32[]{:S(2)}) copy-start(bf16[192,256]{1,0:T(8,128)(2,1)} %get-tuple-element.157.refs_3_) | copy-start | bytes 294916
  70.3 4.5 %collective-permute-start.19 = (bf16[256,1536]{1,0:T(8,128)(2,1)}, bf16[256,1536]{1,0:T(8,128)(2,1)S(1)}, u32[]{:S(2)}, u32[]{:S(2)}) collective-permute-start(bf16[256,1536]{1,0:T(8,128)(2,1)} %collective-permute-done.13.refs_1_), channel_id=1, source_target_pairs={{0,1},{1,0},{2,3},{3,2},{4,5},{5,4},{6,7},{7,6},{8,9},{9,8},{10,11... | collective-permute-start | bytes 2359304 | tf_op jit(solution)/shard_map/ppermute | solution.py:312
  70.8 4.1 %collective-permute-start.20 = (bf16[256,1536]{1,0:T(8,128)(2,1)S(1)}, bf16[256,1536]{1,0:T(8,128)(2,1)S(1)}, u32[]{:S(2)}, u32[]{:S(2)}) collective-permute-start(bf16[256,1536]{1,0:T(8,128)(2,1)S(1)} %collective-permute-done.14.refs_3_), channel_id=1, source_target_pairs={{0,1},{1,0},{2,3},{3,2},{4,5},{5,4},{6,7},{7,6},{8,9},{9,8},{10,11... | collective-permute-start | bytes 2359304 | tf_op jit(solution)/shard_map/ppermute | solution.py:312
  70.9 20.3 %collective-permute-start.18 = (bf16[256,1536]{1,0:T(8,128)(2,1)S(1)}, bf16[256,1536]{1,0:T(8,128)(2,1)S(1)}, u32[]{:S(2)}, u32[]{:S(2)}) collective-permute-start(bf16[256,1536]{1,0:T(8,128)(2,1)S(1)} %bitcast.12), channel_id=1, source_target_pairs={{0,8},{4,12},{8,0},{12,4},{1,9},{5,13},{9,1},{13,5},{2,10},{6,14},... | collective-permute-start | bytes 2359304 | tf_op jit(solution)/shard_map/ppermute | solution.py:312
  72.2 2.7 %collective-permute-start.21 = (bf16[96,1024]{1,0:T(8,128)(2,1)S(1)}, bf16[96,1024]{1,0:T(8,128)(2,1)S(1)}, u32[]{:S(2)}, u32[]{:S(2)}) collective-permute-start(bf16[96,1024]{1,0:T(8,128)(2,1)S(1)} %copy-done.25), channel_id=1, source_target_pairs={{0,1},{1,0},{2,3},{3,2},{4,5},{5,4},{6,7},{7,6},{8,9},{9,8},{10,11... | collective-permute-start | bytes 589832 | tf_op jit(solution)/shard_map/ppermute | solution.py:312
  72.8 20.7 %collective-permute-start.17 = (bf16[384,1024]{1,0:T(8,128)(2,1)S(1)}, bf16[384,1024]{1,0:T(8,128)(2,1)S(1)}, u32[]{:S(2)}, u32[]{:S(2)}) collective-permute-start(bf16[384,1024]{1,0:T(8,128)(2,1)S(1)} %add.1), channel_id=1, source_target_pairs={{0,2},{2,0},{1,3},{3,1},{4,6},{6,4},{5,7},{7,5},{8,10},{10,8},{9,1... | collective-permute-start | bytes 2359304 | tf_op jit(solution)/shard_map/ppermute | solution.py:312
  74.8 25.4 %copy-start.24 = (bf16[96,1024]{1,0:T(8,128)(2,1)}, bf16[96,1024]{1,0:T(8,128)(2,1)S(1)}, u32[]{:S(2)}) copy-start(bf16[96,1024]{1,0:T(8,128)(2,1)S(1)} %collective-permute-done.21.q1) | copy-start | bytes 589828
  74.8 18.6 %copy-start.15 = (bf16[256,1536]{1,0:T(8,128)(2,1)}, bf16[256,1536]{1,0:T(8,128)(2,1)S(1)}, u32[]{:S(2)}) copy-start(bf16[256,1536]{1,0:T(8,128)(2,1)S(1)} %collective-permute-done.19.refs_5_) | copy-start | bytes 2359300
  74.9 18.6 %copy-start.16 = (bf16[256,1536]{1,0:T(8,128)(2,1)}, bf16[256,1536]{1,0:T(8,128)(2,1)S(1)}, u32[]{:S(2)}) copy-start(bf16[256,1536]{1,0:T(8,128)(2,1)S(1)} %collective-permute-done.20.refs_7_) | copy-start | bytes 2359300
  91.2 2.3 %copy-start.17 = (bf16[256,1536]{1,0:T(8,128)(2,1)}, bf16[256,1536]{1,0:T(8,128)(2,1)S(1)}, u32[]{:S(2)}) copy-start(bf16[256,1536]{1,0:T(8,128)(2,1)S(1)} %collective-permute-done.18.refs_2_) | copy-start | bytes 2359300
  91.2 3.2 %collective-permute-start.22 = (bf16[256,1536]{1,0:T(8,128)(2,1)S(1)}, bf16[256,1536]{1,0:T(8,128)(2,1)}, u32[]{:S(2)}, u32[]{:S(2)}) collective-permute-start(bf16[256,1536]{1,0:T(8,128)(2,1)S(1)} %collective-permute-done.18.refs_2_), channel_id=1, source_target_pairs={{0,1},{1,0},{2,3},{3,2},{4,5},{5,4},{6,7},{7,6},{8,9},{9,8},{10,11... | collective-permute-start | bytes 2359304 | tf_op jit(solution)/shard_map/ppermute | solution.py:312
  96.3 4.0 %collective-permute-start.23 = (bf16[192,1024]{1,0:T(8,128)(2,1)S(1)}, bf16[192,1024]{1,0:T(8,128)(2,1)S(1)}, u32[]{:S(2)}, u32[]{:S(2)}) collective-permute-start(bf16[192,1024]{1,0:T(8,128)(2,1)S(1)} %get-tuple-element.159), channel_id=1, source_target_pairs={{0,1},{1,0},{2,3},{3,2},{4,5},{5,4},{6,7},{7,6},{8,9},{9,8},{10,11... | collective-permute-start | bytes 1179656 | tf_op jit(solution)/shard_map/ppermute | solution.py:312
  96.7 15.7 %collective-permute-start.24 = (bf16[576,256]{1,0:T(8,128)(2,1)}, bf16[576,256]{1,0:T(8,128)(2,1)S(1)}, u32[]{:S(2)}, u32[]{:S(2)}) collective-permute-start(bf16[576,256]{1,0:T(8,128)(2,1)} %get-tuple-element.171), channel_id=1, source_target_pairs={{0,12},{4,0},{8,4},{12,8},{1,13},{5,1},{9,5},{13,9},{2,14},{6,2},{... | collective-permute-start | bytes 884744 | tf_op jit(solution)/shard_map/ppermute | solution.py:312
  99.6 12.8 %collective-permute-start.25 = (bf16[576,256]{1,0:T(8,128)(2,1)}, bf16[576,256]{1,0:T(8,128)(2,1)S(1)}, u32[]{:S(2)}, u32[]{:S(2)}) collective-permute-start(bf16[576,256]{1,0:T(8,128)(2,1)} %get-tuple-element.172), channel_id=1, source_target_pairs={{0,8},{4,12},{8,0},{12,4},{1,9},{5,13},{9,1},{13,5},{2,10},{6,14},... | collective-permute-start | bytes 884744 | tf_op jit(solution)/shard_map/ppermute | solution.py:312
  100.2 16.3 %collective-permute-start.26 = (bf16[576,256]{1,0:T(8,128)(2,1)S(1)}, bf16[576,256]{1,0:T(8,128)(2,1)S(1)}, u32[]{:S(2)}, u32[]{:S(2)}) collective-permute-start(bf16[576,256]{1,0:T(8,128)(2,1)S(1)} %get-tuple-element.173), channel_id=1, source_target_pairs={{0,4},{4,8},{8,12},{12,0},{1,5},{5,9},{9,13},{13,1},{2,6},{6,10},{... | collective-permute-start | bytes 884744 | tf_op jit(solution)/shard_map/ppermute | solution.py:312
  101.0 20.5 %copy-start = (bf16[1536,768]{1,0:T(8,128)(2,1)S(1)}, bf16[1536,768]{1,0:T(8,128)(2,1)}, u32[]{:S(2)}) copy-start(bf16[1536,768]{1,0:T(8,128)(2,1)} %refs_5_.1) | copy-start | bytes 7077892
  101.0 20.5 %copy-start.1 = (bf16[1536,768]{1,0:T(8,128)(2,1)S(1)}, bf16[1536,768]{1,0:T(8,128)(2,1)}, u32[]{:S(2)}) copy-start(bf16[1536,768]{1,0:T(8,128)(2,1)} %refs_6_.1) | copy-start | bytes 7077892
  116.6 10.7 %collective-permute-start.27 = (bf16[288,384]{1,0:T(8,128)(2,1)}, bf16[288,384]{1,0:T(8,128)(2,1)S(1)}, u32[]{:S(2)}, u32[]{:S(2)}) collective-permute-start(bf16[288,384]{1,0:T(8,128)(2,1)} %get-tuple-element.175), channel_id=1, source_target_pairs={{0,32},{32,64},{64,96},{96,0},{1,33},{33,65},{65,97},{97,1},{2,34}... | collective-permute-start | bytes 663560 | tf_op jit(solution)/shard_map/ppermute | solution.py:312
  117.8 12.6 %collective-permute-start.28 = (bf16[288,384]{1,0:T(8,128)(2,1)}, bf16[288,384]{1,0:T(8,128)(2,1)S(1)}, u32[]{:S(2)}, u32[]{:S(2)}) collective-permute-start(bf16[288,384]{1,0:T(8,128)(2,1)} %get-tuple-element.176), channel_id=1, source_target_pairs={{0,64},{32,96},{64,0},{96,32},{1,65},{33,97},{65,1},{97,33},{2,66}... | collective-permute-start | bytes 663560 | tf_op jit(solution)/shard_map/ppermute | solution.py:312
  120.5 10.0 %collective-permute-start.29 = (bf16[288,384]{1,0:T(8,128)(2,1)}, bf16[288,384]{1,0:T(8,128)(2,1)S(1)}, u32[]{:S(2)}, u32[]{:S(2)}) collective-permute-start(bf16[288,384]{1,0:T(8,128)(2,1)} %get-tuple-element.177), channel_id=1, source_target_pairs={{0,96},{32,0},{64,32},{96,64},{1,97},{33,1},{65,33},{97,65},{2,98}... | collective-permute-start | bytes 663560 | tf_op jit(solution)/shard_map/ppermute | solution.py:312
  123.2 7.3 %copy-start.7 = (bf16[288,384]{1,0:T(8,128)(2,1)S(1)}, bf16[288,384]{1,0:T(8,128)(2,1)}, u32[]{:S(2)}) copy-start(bf16[288,384]{1,0:T(8,128)(2,1)} %get-tuple-element.183.a) | copy-start | bytes 663556
  (8 other events, 8.5 us)

commit v3 on v2

--- a/solution.py
+++ b/solution.py
@@ -350,12 +350,13 @@
     half = add(rsame, t)
     u = ahead(half, "zh", 1, 2)
     x1n, x3n, dqn = barrier(tuple(core_swap(after(v, half)) for v in (x1, x3, dq1)))
-    x2n = core_swap(after(xs[2], x1n))
-    u, t2, x2n, x1n, x3n, dqn = barrier((u, t2, x2n, x1n, x3n, dqn))
+    u, t2, x1n, x3n, dqn = barrier((u, t2, x1n, x3n, dqn))
+    x2n = core_swap(after(xs[2], u))
     *ps, dmine, dother = comb(mc, lsame, t2, u, dqT)
     ps = around(ps, "x", -1)
     s4 = gkv(my, dmine, core_swap(dother), dq0, dqn, [rows, x1, xs[2], x3, rows_n, x1n, x2n, x3n])
-    s4, ps = barrier((tuple(s4), tuple(ps)))
+    s4, ps1, ps2 = barrier((tuple(s4), ps[1], ps[2]))
+    ps = [ps[0], ps1, ps2, ps[3]]
     s4 = around(s4, "y")
     out = back(mx, ps, [w_query, w_key, w_value])
     s4, out = barrier((tuple(s4), out))

time: 146 us -> 142 us (0.973)
  waiting for transfers between devices: 45.8 us -> 36.7 us
  blocking collectives: 14.7 us -> 22.1 us
  starting transfers between devices: 36.3 us -> 34.4 us
    ppermute x30, waiting for transfers between devices: 45.8 us -> 36.7 us  [ahead(): return lax.ppermute(x, axis, [(i, (i + j) % n) for i in range(n)])]
    all_to_all x1, blocking collectives: 14.7 us -> 22.1 us  [shards(): s = lax.all_to_all(fin1(s4), ('zl', 'x', 'zh', 'c'), 0, 0, tiled=True)]
    ppermute x30, starting transfers between devices: 36.3 us -> 34.4 us  [ahead(): return lax.ppermute(x, axis, [(i, (i + j) % n) for i in range(n)])]
  transfers between devices with their start and end apart: 30 -> 30, of which waited for: 13 -> 11; matrix products, arithmetic and copies ran while one was open for 0% -> 0% of each run, Pallas kernels for 24% -> 26%
where the time goes in v3:
time: 142 us
  Pallas kernels  43.3 us (30%)
  waiting for transfers between devices  36.7 us (26%)
  starting transfers between devices  34.4 us (24%)
  blocking collectives  22.1 us (16%)
  local copies, waits for them, and re-layouts  4.61 us (3%)
    pallas_call x10, Pallas kernels, call(): pl.pallas_call(body, in_specs=in_specs or [VM] * len(ins), out_specs=out_...  43.3 us
    ppermute x30, waiting for transfers between devices, ahead(): return lax.ppermute(x, axis, [(i, (i + j) % n) for i in range(n)])  36.7 us
    ppermute x30, starting transfers between devices, ahead(): return lax.ppermute(x, axis, [(i, (i + j) % n) for i in range(n)])  34.4 us
    all_to_all x1, blocking collectives, shards(): s = lax.all_to_all(fin1(s4), ('zl', 'x', 'zh', 'c'), 0, 0, tiled=True)  22.1 us
    unnamed x52, local copies, waits for them, and re-layouts  4.61 us
  transfers between devices with their start and end apart: 30, of which 11 were waited for; matrix products, arithmetic and copies ran while one was open for 0% of the time, Pallas kernels for 26%

profile of v3, /device:TPU:1, one launch (start us, length us, event | category | flops | bytes accessed | tf_op | source)
XLA Modules:
  0.0 142.1 jit_solution(11361826588587490477)
XLA Ops:
  0.6 5.8 %projkv.1 = (bf16[256,384]{1,0:T(8,128)(2,1)}, bf16[256,384]{1,0:T(8,128)(2,1)}, bf16[256,384]{1,0:T(8,128)(2,1)}, bf16[256,384]{1,0:T(8,128)(2,1)}) custom-call(s32[1]{0:T(128)} %bitcast.2.me, bf16[256,1536]{1,0:T(8,128)(2,1)} %bitcast.6, bf16[1536,768]{1,0:T(8,128)(2,1)} %refs_5_.1, bf16[1536,768]{1,0:T(8,128)(2,1)} %refs_6_.1), custom_call_target="tpu_custom_call" | custom-call | flops 1048576 | bytes 500000 | tf_op jit(solution)/shard_map/projkv/pallas_call | solution.py:39
  6.5 2.1 %collective-permute-start = (bf16[256,384]{1,0:T(8,128)(2,1)}, bf16[256,384]{1,0:T(8,128)(2,1)S(1)}, u32[]{:S(2)}, u32[]{:S(2)}) collective-permute-start(bf16[256,384]{1,0:T(8,128)(2,1)} %get-tuple-element.95), channel_id=1, source_target_pairs={{0,4},{4,8},{8,12},{12,0},{1,5},{5,9},{9,13},{13,1},{2,6},{6,10},{... | collective-permute-start | bytes 589832 | tf_op jit(solution)/shard_map/ppermute | solution.py:312
  8.6 2.4 %collective-permute-start.1 = (bf16[256,384]{1,0:T(8,128)(2,1)}, bf16[256,384]{1,0:T(8,128)(2,1)S(1)}, u32[]{:S(2)}, u32[]{:S(2)}) collective-permute-start(bf16[256,384]{1,0:T(8,128)(2,1)} %get-tuple-element.96), channel_id=1, source_target_pairs={{0,8},{4,12},{8,0},{12,4},{1,9},{5,13},{9,1},{13,5},{2,10},{6,14},... | collective-permute-start | bytes 589832 | tf_op jit(solution)/shard_map/ppermute | solution.py:312
  11.0 1.2 collective-permute-start.2
  12.2 3.6 %collective-permute-start.3 = (bf16[256,384]{1,0:T(8,128)(2,1)}, bf16[256,384]{1,0:T(8,128)(2,1)}, u32[]{:S(2)}, u32[]{:S(2)}) collective-permute-start(bf16[256,384]{1,0:T(8,128)(2,1)} %get-tuple-element.94.refs_0_), channel_id=1, source_target_pairs={{0,2},{2,0},{1,3},{3,1},{4,6},{6,4},{5,7},{7,5},{8,10},{10,8},{9,1... | collective-permute-start | bytes 589832 | tf_op jit(solution)/shard_map/ppermute | solution.py:312
  15.8 1.8 %collective-permute-start.4 = (bf16[256,384]{1,0:T(8,128)(2,1)}, bf16[256,384]{1,0:T(8,128)(2,1)S(1)}, u32[]{:S(2)}, u32[]{:S(2)}) collective-permute-start(bf16[256,384]{1,0:T(8,128)(2,1)} %get-tuple-element.94.refs_0_), channel_id=1, source_target_pairs={{0,1},{1,0},{2,3},{3,2},{4,5},{5,4},{6,7},{7,6},{8,9},{9,8},{10,11... | collective-permute-start | bytes 589832 | tf_op jit(solution)/shard_map/ppermute | solution.py:312
  17.6 5.2 %projq.1 = (bf16[384,256]{1,0:T(8,128)(2,1)}, bf16[384,256]{1,0:T(8,128)(2,1)}, bf16[384,256]{1,0:T(8,128)(2,1)}, bf16[384,256]{1,0:T(8,128)(2,1)}) custom-call(s32[1]{0:T(128)} %bitcast.2.me, bf16[256,1536]{1,0:T(8,128)(2,1)} %bitcast.7, bf16[1536,768]{1,0:T(8,128)(2,1)} %refs_4_.1, bf16[256,768]{1,0:T(8,128)(2,1)} %bitcast.14), custom_call_target="tpu_custom_call" | custom-call | flops 1048576 | bytes 400000 | tf_op jit(solution)/shard_map/projq/pallas_call | solution.py:39
  22.9 0.6 collective-permute-start.5
  23.5 1.8 %collective-permute-start.6 = (bf16[768,384]{1,0:T(8,128)(2,1)S(1)}, bf16[768,384]{1,0:T(8,128)(2,1)}, u32[]{:S(2)}, u32[]{:S(2)}) collective-permute-start(bf16[768,384]{1,0:T(8,128)(2,1)S(1)} %pack.1.refs_1_), channel_id=1, source_target_pairs={{0,1},{1,0},{2,3},{3,2},{4,5},{5,4},{6,7},{7,6},{8,9},{9,8},{10,11... | collective-permute-start | bytes 1769480 | tf_op jit(solution)/shard_map/ppermute | solution.py:312
  25.4 1.0 collective-permute-start.7
  26.4 2.1 %collective-permute-start.8 = (bf16[384,256]{1,0:T(8,128)(2,1)}, bf16[384,256]{1,0:T(8,128)(2,1)S(1)}, u32[]{:S(2)}, u32[]{:S(2)}) collective-permute-start(bf16[384,256]{1,0:T(8,128)(2,1)} %get-tuple-element.108), channel_id=1, source_target_pairs={{0,8},{4,12},{8,0},{12,4},{1,9},{5,13},{9,1},{13,5},{2,10},{6,14},... | collective-permute-start | bytes 589832 | tf_op jit(solution)/shard_map/ppermute | solution.py:312
  28.5 1.3 collective-permute-start.9
  29.8 3.5 %collective-permute-done.7.refs_9_ = bf16[384,256]{1,0:T(8,128)(2,1)S(1)} collective-permute-done((bf16[384,256]{1,0:T(8,128)(2,1)}, bf16[384,256]{1,0:T(8,128)(2,1)S(1)}, u32[]{:S(2)}, u32[]{:S(2)}) %collective-permute-start.7) | collective-permute-done | bytes 196640 | tf_op jit(solution)/shard_map/ppermute | solution.py:312
  33.3 4.7 %collective-permute-done.8.refs_10_ = bf16[384,256]{1,0:T(8,128)(2,1)S(1)} collective-permute-done((bf16[384,256]{1,0:T(8,128)(2,1)}, bf16[384,256]{1,0:T(8,128)(2,1)S(1)}, u32[]{:S(2)}, u32[]{:S(2)}) %collective-permute-start.8) | collective-permute-done | bytes 196640 | tf_op jit(solution)/shard_map/ppermute | solution.py:312
  38.0 1.5 %collective-permute-done.5.refs_5_ = bf16[768,384]{1,0:T(8,128)(2,1)S(1)} collective-permute-done((bf16[768,384]{1,0:T(8,128)(2,1)S(1)}, bf16[768,384]{1,0:T(8,128)(2,1)S(1)}, u32[]{:S(2)}, u32[]{:S(2)}) %collective-permute-start.5) | collective-permute-done | bytes 589856 | tf_op jit(solution)/shard_map/ppermute | solution.py:312
  39.5 0.9 collective-permute-start.12
  40.4 0.8 collective-permute-start.13
  41.2 1.9 %collective-permute-start.14 = (bf16[256,1536]{1,0:T(8,128)(2,1)S(1)}, bf16[256,1536]{1,0:T(8,128)(2,1)}, u32[]{:S(2)}, u32[]{:S(2)}) collective-permute-start(bf16[256,1536]{1,0:T(8,128)(2,1)S(1)} %bitcast.11), channel_id=1, source_target_pairs={{0,12},{4,0},{8,4},{12,8},{1,13},{5,1},{9,5},{13,9},{2,14},{6,2},{... | collective-permute-start | bytes 2359304 | tf_op jit(solution)/shard_map/ppermute | solution.py:312
  43.1 0.6 collective-permute-start.10
  43.7 2.1 %collective-permute-done.11.refs_6_ = bf16[256,384]{1,0:T(8,128)(2,1)} collective-permute-done((bf16[256,384]{1,0:T(8,128)(2,1)}, bf16[256,384]{1,0:T(8,128)(2,1)}, u32[]{:S(2)}, u32[]{:S(2)}) %collective-permute-start.11) | collective-permute-done | bytes 196640 | tf_op jit(solution)/shard_map/ppermute | solution.py:312
  45.9 19.2 %attn.1 = (bf16[384,1024]{1,0:T(8,128)(2,1)}, bf16[384,1024]{1,0:T(8,128)(2,1)}, bf16[384,1024]{1,0:T(8,128)(2,1)}, bf16[384,1024]{1,0:T(8,128)(2,1)}, bf16[96,1...) custom-call(s32[1]{0:T(128)} %bitcast.1.core, ...), custom_call_target="tpu_custom_call" | custom-call | flops 1048576 | bytes 100000 | tf_op jit(solution)/shard_map/attn/pallas_call | solution.py:39
  65.1 0.4 collective-permute-start.15
  65.7 2.0 %collective-permute-done.15.b = bf16[384,1024]{1,0:T(8,128)(2,1)S(1)} collective-permute-done((bf16[384,1024]{1,0:T(8,128)(2,1)}, bf16[384,1024]{1,0:T(8,128)(2,1)S(1)}, u32[]{:S(2)}, u32[]{:S(2)}) %collective-permute-start.15) | collective-permute-done | bytes 786464 | tf_op jit(solution)/shard_map/ppermute | solution.py:312
  67.7 1.1 collective-permute-done.16.t
  68.8 1.1 copy-done.5
  70.2 0.4 collective-permute-start.18
  70.8 0.5 collective-permute-start.17
  71.3 1.1 collective-permute-start.22
  72.4 0.9 collective-permute-start.20
  73.3 1.1 collective-permute-done.20.q1
  74.4 16.9 %collective-permute-done.17.u = bf16[384,1024]{1,0:T(8,128)(2,1)S(1)} collective-permute-done((bf16[384,1024]{1,0:T(8,128)(2,1)S(1)}, bf16[384,1024]{1,0:T(8,128)(2,1)S(1)}, u32[]{:S(2)}, u32[]{:S(2)}) %collective-permute-start.17) | collective-permute-done | bytes 786464 | tf_op jit(solution)/shard_map/ppermute | solution.py:312
  91.5 1.5 %collective-permute-start.23 = (bf16[256,1536]{1,0:T(8,128)(2,1)}, bf16[256,1536]{1,0:T(8,128)(2,1)S(1)}, u32[]{:S(2)}, u32[]{:S(2)}) collective-permute-start(bf16[256,1536]{1,0:T(8,128)(2,1)} %collective-permute-done.22.refs_2_), channel_id=1, source_target_pairs={{0,1},{1,0},{2,3},{3,2},{4,5},{5,4},{6,7},{7,6},{8,9},{9,8},{10,11... | collective-permute-start | bytes 2359304 | tf_op jit(solution)/shard_map/ppermute | solution.py:312
  93.0 1.1 comb.1
  94.1 0.8 copy-done.6
  94.9 1.4 %collective-permute-start.24 = (bf16[576,256]{1,0:T(8,128)(2,1)}, bf16[576,256]{1,0:T(8,128)(2,1)S(1)}, u32[]{:S(2)}, u32[]{:S(2)}) collective-permute-start(bf16[576,256]{1,0:T(8,128)(2,1)} %get-tuple-element.166), channel_id=1, source_target_pairs={{0,12},{4,0},{8,4},{12,8},{1,13},{5,1},{9,5},{13,9},{2,14},{6,2},{... | collective-permute-start | bytes 884744 | tf_op jit(solution)/shard_map/ppermute | solution.py:312
  96.3 0.6 collective-permute-start.25
  96.9 0.7 copy-done.19
  97.9 6.7 %gkv.1 = (bf16[288,384]{1,0:T(8,128)(2,1)}, bf16[288,384]{1,0:T(8,128)(2,1)}, bf16[288,384]{1,0:T(8,128)(2,1)}, bf16[288,384]{1,0:T(8,128)(2,1)}) custom-call(s32[1]{0:T(128)} %bitcast.me, bf16[192,1024]{1,0:T(8,128)(2,1)} %copy-done.6, bf16[192,1024]{1,0:T(8,128)(2,1)} %copy-done.19, bf16[96,1024]{1,0:T(8,128)(2,1)} %get-tuple-element.155.q0, ...), custom_call_target="tpu_custom_call" | custom-call | flops 1048576 | bytes 400000 | tf_op jit(solution)/shard_map/gkv/pallas_call | solution.py:39
  104.6 1.2 collective-permute-done.25.refs_2_
  105.8 1.3 collective-permute-start.26
  107.2 2.6 %collective-permute-start.27 = (bf16[288,384]{1,0:T(8,128)(2,1)}, bf16[288,384]{1,0:T(8,128)(2,1)S(1)}, u32[]{:S(2)}, u32[]{:S(2)}) collective-permute-start(bf16[288,384]{1,0:T(8,128)(2,1)} %get-tuple-element.170), channel_id=1, source_target_pairs={{0,64},{32,96},{64,0},{96,32},{1,65},{33,97},{65,1},{97,33},{2,66}... | collective-permute-start | bytes 663560 | tf_op jit(solution)/shard_map/ppermute | solution.py:312
  109.8 1.1 collective-permute-start.28
  110.8 2.4 %collective-permute-done.29.refs_3_ = bf16[576,256]{1,0:T(8,128)(2,1)S(1)} collective-permute-done((bf16[576,256]{1,0:T(8,128)(2,1)S(1)}, bf16[576,256]{1,0:T(8,128)(2,1)S(1)}, u32[]{:S(2)}, u32[]{:S(2)}) %collective-permute-start.29) | collective-permute-done | bytes 294944 | tf_op jit(solution)/shard_map/ppermute | solution.py:312
  113.3 1.7 %copy-done.2 = bf16[1536,768]{1,0:T(8,128)(2,1)S(1)} copy-done((bf16[1536,768]{1,0:T(8,128)(2,1)S(1)}, bf16[1536,768]{1,0:T(8,128)(2,1)}, u32[]{:S(2)}) %copy-start.2) | copy-done | bytes 2359320
  114.9 4.0 %back.1 = bf16[256,1536]{1,0:T(8,128)(2,1)} custom-call(s32[1]{0:T(128)} %bitcast.2.me, bf16[576,256]{1,0:T(8,128)(2,1)S(1)} %get-tuple-element.172.refs_0_, bf16[576,256]{1,0:T(8,128)(2,1)S(1)} %collective-permute-done.24.refs_1_, bf16[576,256]{1,0:T(8,128)(2,1)S(1)} %collective-permute-done.25.refs_2_, ...), custom_call_target="tpu_custom_call" | custom-call | flops 1048576 | bytes 200000 | tf_op jit(solution)/shard_map/back/pallas_call | solution.py:39
  119.0 0.2 fin1.1
  119.3 22.1 %all_to_all.5.s = bf16[32,12,288]{2,1,0:T(8,128)(2,1)S(1)} all-to-all(bf16[32,12,288]{2,1,0:T(8,128)(2,1)S(1)} %fin1.1), channel_id=1, replica_groups=mesh['y'=4,'zl'=2,'x'=4,'zh'=2,'c'=2] {'zl','x','zh','c'}, dimensions={0} | all-to-all | bytes 442368 | tf_op jit(solution)/shard_map/all_to_all | solution.py:364
  141.4 0.8 fin2.1
  (75 shorter events, 1.3 us)
Async XLA Ops:
  6.5 16.3 %collective-permute-start = (bf16[256,384]{1,0:T(8,128)(2,1)}, bf16[256,384]{1,0:T(8,128)(2,1)S(1)}, u32[]{:S(2)}, u32[]{:S(2)}) collective-permute-start(bf16[256,384]{1,0:T(8,128)(2,1)} %get-tuple-element.95), channel_id=1, source_target_pairs={{0,4},{4,8},{8,12},{12,0},{1,5},{5,9},{9,13},{13,1},{2,6},{6,10},{... | collective-permute-start | bytes 589832 | tf_op jit(solution)/shard_map/ppermute | solution.py:312
  8.6 14.2 %collective-permute-start.1 = (bf16[256,384]{1,0:T(8,128)(2,1)}, bf16[256,384]{1,0:T(8,128)(2,1)S(1)}, u32[]{:S(2)}, u32[]{:S(2)}) collective-permute-start(bf16[256,384]{1,0:T(8,128)(2,1)} %get-tuple-element.96), channel_id=1, source_target_pairs={{0,8},{4,12},{8,0},{12,4},{1,9},{5,13},{9,1},{13,5},{2,10},{6,14},... | collective-permute-start | bytes 589832 | tf_op jit(solution)/shard_map/ppermute | solution.py:312
  11.0 11.8 %collective-permute-start.2 = (bf16[256,384]{1,0:T(8,128)(2,1)}, bf16[256,384]{1,0:T(8,128)(2,1)S(1)}, u32[]{:S(2)}, u32[]{:S(2)}) collective-permute-start(bf16[256,384]{1,0:T(8,128)(2,1)} %get-tuple-element.97), channel_id=1, source_target_pairs={{0,12},{4,0},{8,4},{12,8},{1,13},{5,1},{9,5},{13,9},{2,14},{6,2},{... | collective-permute-start | bytes 589832 | tf_op jit(solution)/shard_map/ppermute | solution.py:312
  12.2 10.6 %collective-permute-start.3 = (bf16[256,384]{1,0:T(8,128)(2,1)}, bf16[256,384]{1,0:T(8,128)(2,1)}, u32[]{:S(2)}, u32[]{:S(2)}) collective-permute-start(bf16[256,384]{1,0:T(8,128)(2,1)} %get-tuple-element.94.refs_0_), channel_id=1, source_target_pairs={{0,2},{2,0},{1,3},{3,1},{4,6},{6,4},{5,7},{7,5},{8,10},{10,8},{9,1... | collective-permute-start | bytes 589832 | tf_op jit(solution)/shard_map/ppermute | solution.py:312
  15.8 7.1 %collective-permute-start.4 = (bf16[256,384]{1,0:T(8,128)(2,1)}, bf16[256,384]{1,0:T(8,128)(2,1)S(1)}, u32[]{:S(2)}, u32[]{:S(2)}) collective-permute-start(bf16[256,384]{1,0:T(8,128)(2,1)} %get-tuple-element.94.refs_0_), channel_id=1, source_target_pairs={{0,1},{1,0},{2,3},{3,2},{4,5},{5,4},{6,7},{7,6},{8,9},{9,8},{10,11... | collective-permute-start | bytes 589832 | tf_op jit(solution)/shard_map/ppermute | solution.py:312
  17.6 21.9 %copy-start.12 = (bf16[1,256,1536]{2,1,0:T(8,128)(2,1)S(1)}, bf16[1,256,1536]{2,1,0:T(8,128)(2,1)}, u32[]{:S(2)}) copy-start(bf16[1,256,1536]{2,1,0:T(8,128)(2,1)} %param.5) | copy-start | bytes 2359300
  22.8 18.3 %copy-start.20 = (bf16[256,384]{1,0:T(8,128)(2,1)}, bf16[256,384]{1,0:T(8,128)(2,1)S(1)}, u32[]{:S(2)}) copy-start(bf16[256,384]{1,0:T(8,128)(2,1)S(1)} %collective-permute-done.4.refs_2_) | copy-start | bytes 589828
  22.9 22.9 %copy-start.3 = (bf16[768,384]{1,0:T(8,128)(2,1)}, bf16[768,384]{1,0:T(8,128)(2,1)S(1)}, u32[]{:S(2)}) copy-start(bf16[768,384]{1,0:T(8,128)(2,1)S(1)} %pack.1.refs_1_) | copy-start | bytes 1769476
  22.9 16.5 %collective-permute-start.5 = (bf16[768,384]{1,0:T(8,128)(2,1)S(1)}, bf16[768,384]{1,0:T(8,128)(2,1)S(1)}, u32[]{:S(2)}, u32[]{:S(2)}) collective-permute-start(bf16[768,384]{1,0:T(8,128)(2,1)S(1)} %pack.1.refs_1_), channel_id=1, source_target_pairs={{0,2},{2,0},{1,3},{3,1},{4,6},{6,4},{5,7},{7,5},{8,10},{10,8},{9,1... | collective-permute-start | bytes 1769480 | tf_op jit(solution)/shard_map/ppermute | solution.py:312
  23.5 16.0 %collective-permute-start.6 = (bf16[768,384]{1,0:T(8,128)(2,1)S(1)}, bf16[768,384]{1,0:T(8,128)(2,1)}, u32[]{:S(2)}, u32[]{:S(2)}) collective-permute-start(bf16[768,384]{1,0:T(8,128)(2,1)S(1)} %pack.1.refs_1_), channel_id=1, source_target_pairs={{0,1},{1,0},{2,3},{3,2},{4,5},{5,4},{6,7},{7,6},{8,9},{9,8},{10,11... | collective-permute-start | bytes 1769480 | tf_op jit(solution)/shard_map/ppermute | solution.py:312
  25.4 8.0 %collective-permute-start.7 = (bf16[384,256]{1,0:T(8,128)(2,1)}, bf16[384,256]{1,0:T(8,128)(2,1)S(1)}, u32[]{:S(2)}, u32[]{:S(2)}) collective-permute-start(bf16[384,256]{1,0:T(8,128)(2,1)} %get-tuple-element.107), channel_id=1, source_target_pairs={{0,4},{4,8},{8,12},{12,0},{1,5},{5,9},{9,13},{13,1},{2,6},{6,10},{... | collective-permute-start | bytes 589832 | tf_op jit(solution)/shard_map/ppermute | solution.py:312
  26.4 11.6 %collective-permute-start.8 = (bf16[384,256]{1,0:T(8,128)(2,1)}, bf16[384,256]{1,0:T(8,128)(2,1)S(1)}, u32[]{:S(2)}, u32[]{:S(2)}) collective-permute-start(bf16[384,256]{1,0:T(8,128)(2,1)} %get-tuple-element.108), channel_id=1, source_target_pairs={{0,8},{4,12},{8,0},{12,4},{1,9},{5,13},{9,1},{13,5},{2,10},{6,14},... | collective-permute-start | bytes 589832 | tf_op jit(solution)/shard_map/ppermute | solution.py:312
  28.5 9.5 %collective-permute-start.9 = (bf16[384,256]{1,0:T(8,128)(2,1)}, bf16[384,256]{1,0:T(8,128)(2,1)S(1)}, u32[]{:S(2)}, u32[]{:S(2)}) collective-permute-start(bf16[384,256]{1,0:T(8,128)(2,1)} %get-tuple-element.109), channel_id=1, source_target_pairs={{0,12},{4,0},{8,4},{12,8},{1,13},{5,1},{9,5},{13,9},{2,14},{6,2},{... | collective-permute-start | bytes 589832 | tf_op jit(solution)/shard_map/ppermute | solution.py:312
  33.3 6.2 %copy-start.21 = (bf16[384,256]{1,0:T(8,128)(2,1)}, bf16[384,256]{1,0:T(8,128)(2,1)S(1)}, u32[]{:S(2)}) copy-start(bf16[384,256]{1,0:T(8,128)(2,1)S(1)} %collective-permute-done.7.refs_9_) | copy-start | bytes 589828
  39.5 6.4 %copy-start.18 = (bf16[768,384]{1,0:T(8,128)(2,1)}, bf16[768,384]{1,0:T(8,128)(2,1)S(1)}, u32[]{:S(2)}) copy-start(bf16[768,384]{1,0:T(8,128)(2,1)S(1)} %collective-permute-done.5.refs_5_) | copy-start | bytes 1769476
  39.5 6.3 %collective-permute-start.12 = (bf16[256,1536]{1,0:T(8,128)(2,1)S(1)}, bf16[256,1536]{1,0:T(8,128)(2,1)S(1)}, u32[]{:S(2)}, u32[]{:S(2)}) collective-permute-start(bf16[256,1536]{1,0:T(8,128)(2,1)S(1)} %bitcast.9), channel_id=1, source_target_pairs={{0,1},{1,0},{2,3},{3,2},{4,5},{5,4},{6,7},{7,6},{8,9},{9,8},{10,11... | collective-permute-start | bytes 2359304 | tf_op jit(solution)/shard_map/ppermute | solution.py:312
  40.4 24.7 %collective-permute-start.13 = (bf16[256,1536]{1,0:T(8,128)(2,1)S(1)}, bf16[256,1536]{1,0:T(8,128)(2,1)S(1)}, u32[]{:S(2)}, u32[]{:S(2)}) collective-permute-start(bf16[256,1536]{1,0:T(8,128)(2,1)S(1)} %bitcast.10), channel_id=1, source_target_pairs={{0,4},{4,8},{8,12},{12,0},{1,5},{5,9},{9,13},{13,1},{2,6},{6,10},{... | collective-permute-start | bytes 2359304 | tf_op jit(solution)/shard_map/ppermute | solution.py:312
  41.2 24.0 %collective-permute-start.14 = (bf16[256,1536]{1,0:T(8,128)(2,1)S(1)}, bf16[256,1536]{1,0:T(8,128)(2,1)}, u32[]{:S(2)}, u32[]{:S(2)}) collective-permute-start(bf16[256,1536]{1,0:T(8,128)(2,1)S(1)} %bitcast.11), channel_id=1, source_target_pairs={{0,12},{4,0},{8,4},{12,8},{1,13},{5,1},{9,5},{13,9},{2,14},{6,2},{... | collective-permute-start | bytes 2359304 | tf_op jit(solution)/shard_map/ppermute | solution.py:312
  43.1 2.8 %collective-permute-start.10 = (bf16[768,384]{1,0:T(8,128)(2,1)S(1)}, bf16[768,384]{1,0:T(8,128)(2,1)}, u32[]{:S(2)}, u32[]{:S(2)}) collective-permute-start(bf16[768,384]{1,0:T(8,128)(2,1)S(1)} %collective-permute-done.5.refs_5_), channel_id=1, source_target_pairs={{0,1},{1,0},{2,3},{3,2},{4,5},{5,4},{6,7},{7,6},{8,9},{9,8},{10,11... | collective-permute-start | bytes 1769480 | tf_op jit(solution)/shard_map/ppermute | solution.py:312
  43.7 2.1 %collective-permute-start.11 = (bf16[256,384]{1,0:T(8,128)(2,1)}, bf16[256,384]{1,0:T(8,128)(2,1)}, u32[]{:S(2)}, u32[]{:S(2)}) collective-permute-start(bf16[256,384]{1,0:T(8,128)(2,1)} %collective-permute-done.3.refs_4_), channel_id=1, source_target_pairs={{0,1},{1,0},{2,3},{3,2},{4,5},{5,4},{6,7},{7,6},{8,9},{9,8},{10,11... | collective-permute-start | bytes 589832 | tf_op jit(solution)/shard_map/ppermute | solution.py:312
  45.8 24.4 %copy-start.13 = (bf16[256,1536]{1,0:T(8,128)(2,1)}, bf16[256,1536]{1,0:T(8,128)(2,1)S(1)}, u32[]{:S(2)}) copy-start(bf16[256,1536]{1,0:T(8,128)(2,1)S(1)} %collective-permute-done.12.refs_4_) | copy-start | bytes 2359300
  65.1 27.9 %copy-start.4 = (bf16[384,1024]{1,0:T(8,128)(2,1)S(1)}, bf16[384,1024]{1,0:T(8,128)(2,1)}, u32[]{:S(2)}) copy-start(bf16[384,1024]{1,0:T(8,128)(2,1)} %get-tuple-element.132.a) | copy-start | bytes 2359300
  65.1 26.3 %copy-start.14 = (bf16[256,1536]{1,0:T(8,128)(2,1)}, bf16[256,1536]{1,0:T(8,128)(2,1)S(1)}, u32[]{:S(2)}) copy-start(bf16[256,1536]{1,0:T(8,128)(2,1)S(1)} %collective-permute-done.13.refs_1_) | copy-start | bytes 2359300
  65.1 2.6 %collective-permute-start.15 = (bf16[384,1024]{1,0:T(8,128)(2,1)}, bf16[384,1024]{1,0:T(8,128)(2,1)S(1)}, u32[]{:S(2)}, u32[]{:S(2)}) collective-permute-start(bf16[384,1024]{1,0:T(8,128)(2,1)} %get-tuple-element.134), channel_id=1, source_target_pairs={{0,1},{1,0},{2,3},{3,2},{4,5},{5,4},{6,7},{7,6},{8,9},{9,8},{10,11... | collective-permute-start | bytes 2359304 | tf_op jit(solution)/shard_map/ppermute | solution.py:312
  65.5 3.3 %collective-permute-start.16 = (bf16[384,1024]{1,0:T(8,128)(2,1)}, bf16[384,1024]{1,0:T(8,128)(2,1)S(1)}, u32[]{:S(2)}, u32[]{:S(2)}) collective-permute-start(bf16[384,1024]{1,0:T(8,128)(2,1)} %get-tuple-element.135), channel_id=1, source_target_pairs={{0,1},{1,0},{2,3},{3,2},{4,5},{5,4},{6,7},{7,6},{8,9},{9,8},{10,11... | collective-permute-start | bytes 2359304 | tf_op jit(solution)/shard_map/ppermute | solution.py:312
  70.0 23.0 %copy-start.8 = (bf16[192,256]{1,0:T(8,128)(2,1)S(1)}, bf16[192,256]{1,0:T(8,128)(2,1)}, u32[]{:S(2)}) copy-start(bf16[192,256]{1,0:T(8,128)(2,1)} %get-tuple-element.149.refs_0_) | copy-start | bytes 294916
  70.0 23.0 %copy-start.9 = (bf16[192,256]{1,0:T(8,128)(2,1)S(1)}, bf16[192,256]{1,0:T(8,128)(2,1)}, u32[]{:S(2)}) copy-start(bf16[192,256]{1,0:T(8,128)(2,1)} %get-tuple-element.150.refs_1_) | copy-start | bytes 294916
  70.0 23.0 %copy-start.10 = (bf16[192,256]{1,0:T(8,128)(2,1)S(1)}, bf16[192,256]{1,0:T(8,128)(2,1)}, u32[]{:S(2)}) copy-start(bf16[192,256]{1,0:T(8,128)(2,1)} %get-tuple-element.151.refs_2_) | copy-start | bytes 294916
  70.0 23.0 %copy-start.11 = (bf16[192,256]{1,0:T(8,128)(2,1)S(1)}, bf16[192,256]{1,0:T(8,128)(2,1)}, u32[]{:S(2)}) copy-start(bf16[192,256]{1,0:T(8,128)(2,1)} %get-tuple-element.152.refs_3_) | copy-start | bytes 294916
  70.2 4.1 %collective-permute-start.18 = (bf16[256,1536]{1,0:T(8,128)(2,1)S(1)}, bf16[256,1536]{1,0:T(8,128)(2,1)S(1)}, u32[]{:S(2)}, u32[]{:S(2)}) collective-permute-start(bf16[256,1536]{1,0:T(8,128)(2,1)S(1)} %collective-permute-done.13.refs_1_), channel_id=1, source_target_pairs={{0,1},{1,0},{2,3},{3,2},{4,5},{5,4},{6,7},{7,6},{8,9},{9,8},{10,11... | collective-permute-start | bytes 2359304 | tf_op jit(solution)/shard_map/ppermute | solution.py:312
  70.6 3.8 %collective-permute-start.19 = (bf16[256,1536]{1,0:T(8,128)(2,1)}, bf16[256,1536]{1,0:T(8,128)(2,1)S(1)}, u32[]{:S(2)}, u32[]{:S(2)}) collective-permute-start(bf16[256,1536]{1,0:T(8,128)(2,1)} %collective-permute-done.14.refs_3_), channel_id=1, source_target_pairs={{0,1},{1,0},{2,3},{3,2},{4,5},{5,4},{6,7},{7,6},{8,9},{9,8},{10,11... | collective-permute-start | bytes 2359304 | tf_op jit(solution)/shard_map/ppermute | solution.py:312
  70.8 20.5 %collective-permute-start.17 = (bf16[384,1024]{1,0:T(8,128)(2,1)S(1)}, bf16[384,1024]{1,0:T(8,128)(2,1)S(1)}, u32[]{:S(2)}, u32[]{:S(2)}) collective-permute-start(bf16[384,1024]{1,0:T(8,128)(2,1)S(1)} %add.1), channel_id=1, source_target_pairs={{0,2},{2,0},{1,3},{3,1},{4,6},{6,4},{5,7},{7,5},{8,10},{10,8},{9,1... | collective-permute-start | bytes 2359304 | tf_op jit(solution)/shard_map/ppermute | solution.py:312
  71.3 20.1 %collective-permute-start.22 = (bf16[256,1536]{1,0:T(8,128)(2,1)S(1)}, bf16[256,1536]{1,0:T(8,128)(2,1)}, u32[]{:S(2)}, u32[]{:S(2)}) collective-permute-start(bf16[256,1536]{1,0:T(8,128)(2,1)S(1)} %bitcast.12), channel_id=1, source_target_pairs={{0,8},{4,12},{8,0},{12,4},{1,9},{5,13},{9,1},{13,5},{2,10},{6,14},... | collective-permute-start | bytes 2359304 | tf_op jit(solution)/shard_map/ppermute | solution.py:312
  72.4 2.0 %collective-permute-start.20 = (bf16[96,1024]{1,0:T(8,128)(2,1)S(1)}, bf16[96,1024]{1,0:T(8,128)(2,1)S(1)}, u32[]{:S(2)}, u32[]{:S(2)}) collective-permute-start(bf16[96,1024]{1,0:T(8,128)(2,1)S(1)} %copy-done.25), channel_id=1, source_target_pairs={{0,1},{1,0},{2,3},{3,2},{4,5},{5,4},{6,7},{7,6},{8,9},{9,8},{10,11... | collective-permute-start | bytes 589832 | tf_op jit(solution)/shard_map/ppermute | solution.py:312
  74.3 22.6 %copy-start.24 = (bf16[96,1024]{1,0:T(8,128)(2,1)}, bf16[96,1024]{1,0:T(8,128)(2,1)S(1)}, u32[]{:S(2)}) copy-start(bf16[96,1024]{1,0:T(8,128)(2,1)S(1)} %collective-permute-done.20.q1) | copy-start | bytes 589828
  74.3 17.1 %copy-start.15 = (bf16[256,1536]{1,0:T(8,128)(2,1)}, bf16[256,1536]{1,0:T(8,128)(2,1)S(1)}, u32[]{:S(2)}) copy-start(bf16[256,1536]{1,0:T(8,128)(2,1)S(1)} %collective-permute-done.18.refs_5_) | copy-start | bytes 2359300
  74.3 17.1 %copy-start.16 = (bf16[256,1536]{1,0:T(8,128)(2,1)}, bf16[256,1536]{1,0:T(8,128)(2,1)S(1)}, u32[]{:S(2)}) copy-start(bf16[256,1536]{1,0:T(8,128)(2,1)S(1)} %collective-permute-done.19.refs_7_) | copy-start | bytes 2359300
  91.5 5.5 %collective-permute-start.23 = (bf16[256,1536]{1,0:T(8,128)(2,1)}, bf16[256,1536]{1,0:T(8,128)(2,1)S(1)}, u32[]{:S(2)}, u32[]{:S(2)}) collective-permute-start(bf16[256,1536]{1,0:T(8,128)(2,1)} %collective-permute-done.22.refs_2_), channel_id=1, source_target_pairs={{0,1},{1,0},{2,3},{3,2},{4,5},{5,4},{6,7},{7,6},{8,9},{9,8},{10,11... | collective-permute-start | bytes 2359304 | tf_op jit(solution)/shard_map/ppermute | solution.py:312
  94.8 2.1 %collective-permute-start.21 = (bf16[192,1024]{1,0:T(8,128)(2,1)S(1)}, bf16[192,1024]{1,0:T(8,128)(2,1)S(1)}, u32[]{:S(2)}, u32[]{:S(2)}) collective-permute-start(bf16[192,1024]{1,0:T(8,128)(2,1)S(1)} %get-tuple-element.154), channel_id=1, source_target_pairs={{0,1},{1,0},{2,3},{3,2},{4,5},{5,4},{6,7},{7,6},{8,9},{9,8},{10,11... | collective-permute-start | bytes 1179656 | tf_op jit(solution)/shard_map/ppermute | solution.py:312
  94.9 9.8 %collective-permute-start.24 = (bf16[576,256]{1,0:T(8,128)(2,1)}, bf16[576,256]{1,0:T(8,128)(2,1)S(1)}, u32[]{:S(2)}, u32[]{:S(2)}) collective-permute-start(bf16[576,256]{1,0:T(8,128)(2,1)} %get-tuple-element.166), channel_id=1, source_target_pairs={{0,12},{4,0},{8,4},{12,8},{1,13},{5,1},{9,5},{13,9},{2,14},{6,2},{... | collective-permute-start | bytes 884744 | tf_op jit(solution)/shard_map/ppermute | solution.py:312
  96.3 9.5 %collective-permute-start.25 = (bf16[576,256]{1,0:T(8,128)(2,1)}, bf16[576,256]{1,0:T(8,128)(2,1)S(1)}, u32[]{:S(2)}, u32[]{:S(2)}) collective-permute-start(bf16[576,256]{1,0:T(8,128)(2,1)} %get-tuple-element.167), channel_id=1, source_target_pairs={{0,8},{4,12},{8,0},{12,4},{1,9},{5,13},{9,1},{13,5},{2,10},{6,14},... | collective-permute-start | bytes 884744 | tf_op jit(solution)/shard_map/ppermute | solution.py:312
  96.9 16.4 %collective-permute-start.29 = (bf16[576,256]{1,0:T(8,128)(2,1)S(1)}, bf16[576,256]{1,0:T(8,128)(2,1)S(1)}, u32[]{:S(2)}, u32[]{:S(2)}) collective-permute-start(bf16[576,256]{1,0:T(8,128)(2,1)S(1)} %get-tuple-element.175), channel_id=1, source_target_pairs={{0,4},{4,8},{8,12},{12,0},{1,5},{5,9},{9,13},{13,1},{2,6},{6,10},{... | collective-permute-start | bytes 884744 | tf_op jit(solution)/shard_map/ppermute | solution.py:312
  97.9 15.4 %copy-start = (bf16[1536,768]{1,0:T(8,128)(2,1)S(1)}, bf16[1536,768]{1,0:T(8,128)(2,1)}, u32[]{:S(2)}) copy-start(bf16[1536,768]{1,0:T(8,128)(2,1)} %refs_5_.1) | copy-start | bytes 7077892
  97.9 15.4 %copy-start.1 = (bf16[1536,768]{1,0:T(8,128)(2,1)S(1)}, bf16[1536,768]{1,0:T(8,128)(2,1)}, u32[]{:S(2)}) copy-start(bf16[1536,768]{1,0:T(8,128)(2,1)} %refs_6_.1) | copy-start | bytes 7077892
  105.8 13.1 %collective-permute-start.26 = (bf16[288,384]{1,0:T(8,128)(2,1)}, bf16[288,384]{1,0:T(8,128)(2,1)S(1)}, u32[]{:S(2)}, u32[]{:S(2)}) collective-permute-start(bf16[288,384]{1,0:T(8,128)(2,1)} %get-tuple-element.169), channel_id=1, source_target_pairs={{0,32},{32,64},{64,96},{96,0},{1,33},{33,65},{65,97},{97,1},{2,34}... | collective-permute-start | bytes 663560 | tf_op jit(solution)/shard_map/ppermute | solution.py:312
  107.2 11.8 %collective-permute-start.27 = (bf16[288,384]{1,0:T(8,128)(2,1)}, bf16[288,384]{1,0:T(8,128)(2,1)S(1)}, u32[]{:S(2)}, u32[]{:S(2)}) collective-permute-start(bf16[288,384]{1,0:T(8,128)(2,1)} %get-tuple-element.170), channel_id=1, source_target_pairs={{0,64},{32,96},{64,0},{96,32},{1,65},{33,97},{65,1},{97,33},{2,66}... | collective-permute-start | bytes 663560 | tf_op jit(solution)/shard_map/ppermute | solution.py:312
  109.8 9.2 %collective-permute-start.28 = (bf16[288,384]{1,0:T(8,128)(2,1)}, bf16[288,384]{1,0:T(8,128)(2,1)S(1)}, u32[]{:S(2)}, u32[]{:S(2)}) collective-permute-start(bf16[288,384]{1,0:T(8,128)(2,1)} %get-tuple-element.171), channel_id=1, source_target_pairs={{0,96},{32,0},{64,32},{96,64},{1,97},{33,1},{65,33},{97,65},{2,98}... | collective-permute-start | bytes 663560 | tf_op jit(solution)/shard_map/ppermute | solution.py:312
  114.9 4.1 %copy-start.7 = (bf16[288,384]{1,0:T(8,128)(2,1)S(1)}, bf16[288,384]{1,0:T(8,128)(2,1)}, u32[]{:S(2)}) copy-start(bf16[288,384]{1,0:T(8,128)(2,1)} %get-tuple-element.177.a) | copy-start | bytes 663556
  (8 other events, 10.6 us)

commit v4 on v3

--- a/solution.py
+++ b/solution.py
@@ -66,11 +66,14 @@
 TT = (((0,), (1,)), ((), ()))
 
 
-def projkv_body(me, x, wk, wv, o0, o1, o2, o3, wks, wvs, scr, sem, osem):
+def projkv_body(me, x_in, wk, wv, o0, o1, o2, o3, x, wks, wvs, scr, sem, osem, xsem):
+    cx = pltpu.make_async_copy(x_in, x, xsem.at[0])
+    cx.start()
     cps = loads(((wk, wks), (wv, wvs)), sem)
     for i in range(4):
         cps[i].start()
         cps[4 + i].start()
+    cx.wait()
     k = v = None
     for i in range(4):
         cps[i].wait()
@@ -87,9 +90,10 @@
 
 def projkv(me, x, wk, wv):
     return call(
-        projkv_body, "projkv", 5, (me, x, wk, wv), [sds((NB, 2 * E), BF16)] * 4, [ANY] * 4, [SM, VM, ANY, ANY],
-        [pltpu.VMEM((D, HD), BF16), pltpu.VMEM((D, HD), BF16), pltpu.VMEM((H, NB, 2 * E), BF16),
-         pltpu.SemaphoreType.DMA((8,)), pltpu.SemaphoreType.DMA((4,))])
+        projkv_body, "projkv", 5, (me, x, wk, wv), [sds((NB, 2 * E), BF16)] * 4, [ANY] * 4, [SM, ANY, ANY, ANY],
+        [pltpu.VMEM((NB, D), BF16), pltpu.VMEM((D, HD), BF16), pltpu.VMEM((D, HD), BF16),
+         pltpu.VMEM((H, NB, 2 * E), BF16),
+         pltpu.SemaphoreType.DMA((8,)), pltpu.SemaphoreType.DMA((4,)), pltpu.SemaphoreType.DMA((1,))])
 
 
 def projq_body(me, x, wq, do, o0, o1, o2, o3, wqs, scr, sem, osem):
@@ -355,8 +359,8 @@
     *ps, dmine, dother = comb(mc, lsame, t2, u, dqT)
     ps = around(ps, "x", -1)
     s4 = gkv(my, dmine, core_swap(dother), dq0, dqn, [rows, x1, xs[2], x3, rows_n, x1n, x2n, x3n])
-    s4, ps1, ps2 = barrier((tuple(s4), ps[1], ps[2]))
-    ps = [ps[0], ps1, ps2, ps[3]]
+    s4, ps2 = barrier((tuple(s4), ps[2]))
+    ps = [ps[0], ps[1], ps2, ps[3]]
     s4 = around(s4, "y")
     out = back(mx, ps, [w_query, w_key, w_value])
     s4, out = barrier((tuple(s4), out))

time: 142 us -> 138 us (0.972)
  blocking collectives: 22.1 us -> 18.5 us
  waiting for transfers between devices: 36.7 us -> 35 us
    all_to_all x1, blocking collectives: 22.1 us -> 18.5 us  [shards(): s = lax.all_to_all(fin1(s4), ('zl', 'x', 'zh', 'c'), 0, 0, tiled=True)]
    ppermute x30, waiting for transfers between devices: 36.7 us -> 35 us  [ahead(): return lax.ppermute(x, axis, [(i, (i + j) % n) for i in range(n)])]
where the time goes in v4:
time: 138 us; the launch traced here: 137 us
  Pallas kernels  43 us (31%)
  starting transfers between devices  35.1 us (25%)
  waiting for transfers between devices  35 us (25%)
  blocking collectives  18.5 us (13%)
  local copies, waits for them, and re-layouts  4.61 us (3%)
    pallas_call x10, Pallas kernels, call(): pl.pallas_call(body, in_specs=in_specs or [VM] * len(ins), out_specs=out_...  43 us
    ppermute x30, starting transfers between devices, ahead(): return lax.ppermute(x, axis, [(i, (i + j) % n) for i in range(n)])  35.1 us
    ppermute x30, waiting for transfers between devices, ahead(): return lax.ppermute(x, axis, [(i, (i + j) % n) for i in range(n)])  35 us
    all_to_all x1, blocking collectives, shards(): s = lax.all_to_all(fin1(s4), ('zl', 'x', 'zh', 'c'), 0, 0, tiled=True)  18.5 us
    unnamed x52, local copies, waits for them, and re-layouts  4.61 us
  transfers between devices with their start and end apart: 30, of which 11 were waited for; matrix products, arithmetic and copies ran while one was open for 0% of the time, Pallas kernels for 26%

profile of v4, /device:TPU:1, one launch (start us, length us, event | category | flops | bytes accessed | tf_op | source)
XLA Modules:
  0.0 137.2 jit_solution(8022504160030639288)
XLA Ops:
  0.6 5.6 %projkv.1 = (bf16[256,384]{1,0:T(8,128)(2,1)}, bf16[256,384]{1,0:T(8,128)(2,1)}, bf16[256,384]{1,0:T(8,128)(2,1)}, bf16[256,384]{1,0:T(8,128)(2,1)}) custom-call(s32[1]{0:T(128)} %bitcast.2.me, bf16[256,1536]{1,0:T(8,128)(2,1)} %bitcast.6, bf16[1536,768]{1,0:T(8,128)(2,1)} %refs_5_.1, bf16[1536,768]{1,0:T(8,128)(2,1)} %refs_6_.1), custom_call_target="tpu_custom_call" | custom-call | flops 1048576 | bytes 500000 | tf_op jit(solution)/shard_map/projkv/pallas_call | solution.py:39
  6.2 2.1 %collective-permute-start = (bf16[256,384]{1,0:T(8,128)(2,1)}, bf16[256,384]{1,0:T(8,128)(2,1)S(1)}, u32[]{:S(2)}, u32[]{:S(2)}) collective-permute-start(bf16[256,384]{1,0:T(8,128)(2,1)} %get-tuple-element.94), channel_id=1, source_target_pairs={{0,4},{4,8},{8,12},{12,0},{1,5},{5,9},{9,13},{13,1},{2,6},{6,10},{... | collective-permute-start | bytes 589832 | tf_op jit(solution)/shard_map/ppermute | solution.py:316
  8.3 2.5 %collective-permute-start.1 = (bf16[256,384]{1,0:T(8,128)(2,1)}, bf16[256,384]{1,0:T(8,128)(2,1)S(1)}, u32[]{:S(2)}, u32[]{:S(2)}) collective-permute-start(bf16[256,384]{1,0:T(8,128)(2,1)} %get-tuple-element.95), channel_id=1, source_target_pairs={{0,8},{4,12},{8,0},{12,4},{1,9},{5,13},{9,1},{13,5},{2,10},{6,14},... | collective-permute-start | bytes 589832 | tf_op jit(solution)/shard_map/ppermute | solution.py:316
  10.8 1.2 collective-permute-start.2
  11.9 3.6 %collective-permute-start.3 = (bf16[256,384]{1,0:T(8,128)(2,1)}, bf16[256,384]{1,0:T(8,128)(2,1)}, u32[]{:S(2)}, u32[]{:S(2)}) collective-permute-start(bf16[256,384]{1,0:T(8,128)(2,1)} %get-tuple-element.93.refs_0_), channel_id=1, source_target_pairs={{0,2},{2,0},{1,3},{3,1},{4,6},{6,4},{5,7},{7,5},{8,10},{10,8},{9,1... | collective-permute-start | bytes 589832 | tf_op jit(solution)/shard_map/ppermute | solution.py:316
  15.5 1.8 %collective-permute-start.4 = (bf16[256,384]{1,0:T(8,128)(2,1)}, bf16[256,384]{1,0:T(8,128)(2,1)S(1)}, u32[]{:S(2)}, u32[]{:S(2)}) collective-permute-start(bf16[256,384]{1,0:T(8,128)(2,1)} %get-tuple-element.93.refs_0_), channel_id=1, source_target_pairs={{0,1},{1,0},{2,3},{3,2},{4,5},{5,4},{6,7},{7,6},{8,9},{9,8},{10,11... | collective-permute-start | bytes 589832 | tf_op jit(solution)/shard_map/ppermute | solution.py:316
  17.3 5.2 %projq.1 = (bf16[384,256]{1,0:T(8,128)(2,1)}, bf16[384,256]{1,0:T(8,128)(2,1)}, bf16[384,256]{1,0:T(8,128)(2,1)}, bf16[384,256]{1,0:T(8,128)(2,1)}) custom-call(s32[1]{0:T(128)} %bitcast.2.me, bf16[256,1536]{1,0:T(8,128)(2,1)} %bitcast.7, bf16[1536,768]{1,0:T(8,128)(2,1)} %refs_4_.1, bf16[256,768]{1,0:T(8,128)(2,1)} %bitcast.14), custom_call_target="tpu_custom_call" | custom-call | flops 1048576 | bytes 400000 | tf_op jit(solution)/shard_map/projq/pallas_call | solution.py:39
  22.7 0.6 collective-permute-start.5
  23.3 1.8 %collective-permute-start.6 = (bf16[768,384]{1,0:T(8,128)(2,1)S(1)}, bf16[768,384]{1,0:T(8,128)(2,1)}, u32[]{:S(2)}, u32[]{:S(2)}) collective-permute-start(bf16[768,384]{1,0:T(8,128)(2,1)S(1)} %pack.1.refs_1_), channel_id=1, source_target_pairs={{0,1},{1,0},{2,3},{3,2},{4,5},{5,4},{6,7},{7,6},{8,9},{9,8},{10,11... | collective-permute-start | bytes 1769480 | tf_op jit(solution)/shard_map/ppermute | solution.py:316
  25.1 1.0 collective-permute-start.7
  26.2 2.1 %collective-permute-start.8 = (bf16[384,256]{1,0:T(8,128)(2,1)}, bf16[384,256]{1,0:T(8,128)(2,1)S(1)}, u32[]{:S(2)}, u32[]{:S(2)}) collective-permute-start(bf16[384,256]{1,0:T(8,128)(2,1)} %get-tuple-element.107), channel_id=1, source_target_pairs={{0,8},{4,12},{8,0},{12,4},{1,9},{5,13},{9,1},{13,5},{2,10},{6,14},... | collective-permute-start | bytes 589832 | tf_op jit(solution)/shard_map/ppermute | solution.py:316
  28.3 1.3 collective-permute-start.9
  29.5 3.5 %collective-permute-done.7.refs_9_ = bf16[384,256]{1,0:T(8,128)(2,1)S(1)} collective-permute-done((bf16[384,256]{1,0:T(8,128)(2,1)}, bf16[384,256]{1,0:T(8,128)(2,1)S(1)}, u32[]{:S(2)}, u32[]{:S(2)}) %collective-permute-start.7) | collective-permute-done | bytes 196640 | tf_op jit(solution)/shard_map/ppermute | solution.py:316
  33.1 4.7 %collective-permute-done.8.refs_10_ = bf16[384,256]{1,0:T(8,128)(2,1)S(1)} collective-permute-done((bf16[384,256]{1,0:T(8,128)(2,1)}, bf16[384,256]{1,0:T(8,128)(2,1)S(1)}, u32[]{:S(2)}, u32[]{:S(2)}) %collective-permute-start.8) | collective-permute-done | bytes 196640 | tf_op jit(solution)/shard_map/ppermute | solution.py:316
  37.8 1.5 %collective-permute-done.5.refs_5_ = bf16[768,384]{1,0:T(8,128)(2,1)S(1)} collective-permute-done((bf16[768,384]{1,0:T(8,128)(2,1)S(1)}, bf16[768,384]{1,0:T(8,128)(2,1)S(1)}, u32[]{:S(2)}, u32[]{:S(2)}) %collective-permute-start.5) | collective-permute-done | bytes 589856 | tf_op jit(solution)/shard_map/ppermute | solution.py:316
  39.3 0.9 collective-permute-start.12
  40.1 0.8 collective-permute-start.13
  40.9 1.9 %collective-permute-start.14 = (bf16[256,1536]{1,0:T(8,128)(2,1)S(1)}, bf16[256,1536]{1,0:T(8,128)(2,1)}, u32[]{:S(2)}, u32[]{:S(2)}) collective-permute-start(bf16[256,1536]{1,0:T(8,128)(2,1)S(1)} %bitcast.11), channel_id=1, source_target_pairs={{0,12},{4,0},{8,4},{12,8},{1,13},{5,1},{9,5},{13,9},{2,14},{6,2},{... | collective-permute-start | bytes 2359304 | tf_op jit(solution)/shard_map/ppermute | solution.py:316
  42.8 0.6 collective-permute-start.10
  43.5 2.1 %collective-permute-done.11.refs_6_ = bf16[256,384]{1,0:T(8,128)(2,1)} collective-permute-done((bf16[256,384]{1,0:T(8,128)(2,1)}, bf16[256,384]{1,0:T(8,128)(2,1)}, u32[]{:S(2)}, u32[]{:S(2)}) %collective-permute-start.11) | collective-permute-done | bytes 196640 | tf_op jit(solution)/shard_map/ppermute | solution.py:316
  45.6 19.2 %attn.1 = (bf16[384,1024]{1,0:T(8,128)(2,1)}, bf16[384,1024]{1,0:T(8,128)(2,1)}, bf16[384,1024]{1,0:T(8,128)(2,1)}, bf16[384,1024]{1,0:T(8,128)(2,1)}, bf16[96,1...) custom-call(s32[1]{0:T(128)} %bitcast.1.core, ...), custom_call_target="tpu_custom_call" | custom-call | flops 1048576 | bytes 100000 | tf_op jit(solution)/shard_map/attn/pallas_call | solution.py:39
  64.9 0.4 collective-permute-start.15
  65.5 2.0 %collective-permute-done.15.b = bf16[384,1024]{1,0:T(8,128)(2,1)S(1)} collective-permute-done((bf16[384,1024]{1,0:T(8,128)(2,1)}, bf16[384,1024]{1,0:T(8,128)(2,1)S(1)}, u32[]{:S(2)}, u32[]{:S(2)}) %collective-permute-start.15) | collective-permute-done | bytes 786464 | tf_op jit(solution)/shard_map/ppermute | solution.py:316
  67.5 1.1 collective-permute-done.16.t
  68.6 1.1 copy-done.5
  69.9 0.4 collective-permute-start.18
  70.5 0.5 collective-permute-start.17
  71.1 1.0 collective-permute-start.22
  72.1 0.9 collective-permute-start.20
  73.0 1.1 collective-permute-done.20.q1
  74.1 16.9 %collective-permute-done.17.u = bf16[384,1024]{1,0:T(8,128)(2,1)S(1)} collective-permute-done((bf16[384,1024]{1,0:T(8,128)(2,1)S(1)}, bf16[384,1024]{1,0:T(8,128)(2,1)S(1)}, u32[]{:S(2)}, u32[]{:S(2)}) %collective-permute-start.17) | collective-permute-done | bytes 786464 | tf_op jit(solution)/shard_map/ppermute | solution.py:316
  91.2 1.5 %collective-permute-start.23 = (bf16[256,1536]{1,0:T(8,128)(2,1)}, bf16[256,1536]{1,0:T(8,128)(2,1)S(1)}, u32[]{:S(2)}, u32[]{:S(2)}) collective-permute-start(bf16[256,1536]{1,0:T(8,128)(2,1)} %collective-permute-done.22.refs_2_), channel_id=1, source_target_pairs={{0,1},{1,0},{2,3},{3,2},{4,5},{5,4},{6,7},{7,6},{8,9},{9,8},{10,11... | collective-permute-start | bytes 2359304 | tf_op jit(solution)/shard_map/ppermute | solution.py:316
  92.7 1.1 comb.1
  93.8 0.8 copy-done.6
  94.6 1.0 collective-permute-start.24
  95.7 1.6 %collective-permute-start.28 = (bf16[576,256]{1,0:T(8,128)(2,1)}, bf16[576,256]{1,0:T(8,128)(2,1)S(1)}, u32[]{:S(2)}, u32[]{:S(2)}) collective-permute-start(bf16[576,256]{1,0:T(8,128)(2,1)} %get-tuple-element.171), channel_id=1, source_target_pairs={{0,12},{4,0},{8,4},{12,8},{1,13},{5,1},{9,5},{13,9},{2,14},{6,2},{... | collective-permute-start | bytes 884744 | tf_op jit(solution)/shard_map/ppermute | solution.py:316
  97.3 0.7 copy-done.19
  98.3 6.7 %gkv.1 = (bf16[288,384]{1,0:T(8,128)(2,1)}, bf16[288,384]{1,0:T(8,128)(2,1)}, bf16[288,384]{1,0:T(8,128)(2,1)}, bf16[288,384]{1,0:T(8,128)(2,1)}) custom-call(s32[1]{0:T(128)} %bitcast.me, bf16[192,1024]{1,0:T(8,128)(2,1)} %copy-done.6, bf16[192,1024]{1,0:T(8,128)(2,1)} %copy-done.19, bf16[96,1024]{1,0:T(8,128)(2,1)} %get-tuple-element.154.q0, ...), custom_call_target="tpu_custom_call" | custom-call | flops 1048576 | bytes 400000 | tf_op jit(solution)/shard_map/gkv/pallas_call | solution.py:39
  105.0 1.4 collective-permute-start.25
  106.4 2.6 %collective-permute-start.26 = (bf16[288,384]{1,0:T(8,128)(2,1)}, bf16[288,384]{1,0:T(8,128)(2,1)S(1)}, u32[]{:S(2)}, u32[]{:S(2)}) collective-permute-start(bf16[288,384]{1,0:T(8,128)(2,1)} %get-tuple-element.168), channel_id=1, source_target_pairs={{0,64},{32,96},{64,0},{96,32},{1,65},{33,97},{65,1},{97,33},{2,66}... | collective-permute-start | bytes 663560 | tf_op jit(solution)/shard_map/ppermute | solution.py:316
  109.0 1.1 collective-permute-start.27
  110.0 1.5 %collective-permute-done.29.refs_3_ = bf16[576,256]{1,0:T(8,128)(2,1)S(1)} collective-permute-done((bf16[576,256]{1,0:T(8,128)(2,1)S(1)}, bf16[576,256]{1,0:T(8,128)(2,1)S(1)}, u32[]{:S(2)}, u32[]{:S(2)}) %collective-permute-start.29) | collective-permute-done | bytes 294944 | tf_op jit(solution)/shard_map/ppermute | solution.py:316
  111.6 1.7 %copy-done.2 = bf16[1536,768]{1,0:T(8,128)(2,1)S(1)} copy-done((bf16[1536,768]{1,0:T(8,128)(2,1)S(1)}, bf16[1536,768]{1,0:T(8,128)(2,1)}, u32[]{:S(2)}) %copy-start.2) | copy-done | bytes 2359320
  113.3 4.0 %back.1 = bf16[256,1536]{1,0:T(8,128)(2,1)} custom-call(s32[1]{0:T(128)} %bitcast.2.me, bf16[576,256]{1,0:T(8,128)(2,1)S(1)} %get-tuple-element.170.refs_0_, bf16[576,256]{1,0:T(8,128)(2,1)S(1)} %collective-permute-done.28.refs_1_, bf16[576,256]{1,0:T(8,128)(2,1)S(1)} %collective-permute-done.24.refs_2_, ...), custom_call_target="tpu_custom_call" | custom-call | flops 1048576 | bytes 200000 | tf_op jit(solution)/shard_map/back/pallas_call | solution.py:39
  117.3 0.4 collective-permute-done.26.c
  117.7 0.2 fin1.1
  117.9 18.5 %all_to_all.5.s = bf16[32,12,288]{2,1,0:T(8,128)(2,1)S(1)} all-to-all(bf16[32,12,288]{2,1,0:T(8,128)(2,1)S(1)} %fin1.1), channel_id=1, replica_groups=mesh['y'=4,'zl'=2,'x'=4,'zh'=2,'c'=2] {'zl','x','zh','c'}, dimensions={0} | all-to-all | bytes 442368 | tf_op jit(solution)/shard_map/all_to_all | solution.py:368
  136.5 0.8 fin2.1
  (75 shorter events, 1.3 us)
Async XLA Ops:
  6.2 16.3 %collective-permute-start = (bf16[256,384]{1,0:T(8,128)(2,1)}, bf16[256,384]{1,0:T(8,128)(2,1)S(1)}, u32[]{:S(2)}, u32[]{:S(2)}) collective-permute-start(bf16[256,384]{1,0:T(8,128)(2,1)} %get-tuple-element.94), channel_id=1, source_target_pairs={{0,4},{4,8},{8,12},{12,0},{1,5},{5,9},{9,13},{13,1},{2,6},{6,10},{... | collective-permute-start | bytes 589832 | tf_op jit(solution)/shard_map/ppermute | solution.py:316
  8.3 14.2 %collective-permute-start.1 = (bf16[256,384]{1,0:T(8,128)(2,1)}, bf16[256,384]{1,0:T(8,128)(2,1)S(1)}, u32[]{:S(2)}, u32[]{:S(2)}) collective-permute-start(bf16[256,384]{1,0:T(8,128)(2,1)} %get-tuple-element.95), channel_id=1, source_target_pairs={{0,8},{4,12},{8,0},{12,4},{1,9},{5,13},{9,1},{13,5},{2,10},{6,14},... | collective-permute-start | bytes 589832 | tf_op jit(solution)/shard_map/ppermute | solution.py:316
  10.8 11.8 %collective-permute-start.2 = (bf16[256,384]{1,0:T(8,128)(2,1)}, bf16[256,384]{1,0:T(8,128)(2,1)S(1)}, u32[]{:S(2)}, u32[]{:S(2)}) collective-permute-start(bf16[256,384]{1,0:T(8,128)(2,1)} %get-tuple-element.96), channel_id=1, source_target_pairs={{0,12},{4,0},{8,4},{12,8},{1,13},{5,1},{9,5},{13,9},{2,14},{6,2},{... | collective-permute-start | bytes 589832 | tf_op jit(solution)/shard_map/ppermute | solution.py:316
  11.9 10.6 %collective-permute-start.3 = (bf16[256,384]{1,0:T(8,128)(2,1)}, bf16[256,384]{1,0:T(8,128)(2,1)}, u32[]{:S(2)}, u32[]{:S(2)}) collective-permute-start(bf16[256,384]{1,0:T(8,128)(2,1)} %get-tuple-element.93.refs_0_), channel_id=1, source_target_pairs={{0,2},{2,0},{1,3},{3,1},{4,6},{6,4},{5,7},{7,5},{8,10},{10,8},{9,1... | collective-permute-start | bytes 589832 | tf_op jit(solution)/shard_map/ppermute | solution.py:316
  15.5 7.1 %collective-permute-start.4 = (bf16[256,384]{1,0:T(8,128)(2,1)}, bf16[256,384]{1,0:T(8,128)(2,1)S(1)}, u32[]{:S(2)}, u32[]{:S(2)}) collective-permute-start(bf16[256,384]{1,0:T(8,128)(2,1)} %get-tuple-element.93.refs_0_), channel_id=1, source_target_pairs={{0,1},{1,0},{2,3},{3,2},{4,5},{5,4},{6,7},{7,6},{8,9},{9,8},{10,11... | collective-permute-start | bytes 589832 | tf_op jit(solution)/shard_map/ppermute | solution.py:316
  17.3 21.9 %copy-start.12 = (bf16[1,256,1536]{2,1,0:T(8,128)(2,1)S(1)}, bf16[1,256,1536]{2,1,0:T(8,128)(2,1)}, u32[]{:S(2)}) copy-start(bf16[1,256,1536]{2,1,0:T(8,128)(2,1)} %param.5) | copy-start | bytes 2359300
  22.6 18.3 %copy-start.20 = (bf16[256,384]{1,0:T(8,128)(2,1)}, bf16[256,384]{1,0:T(8,128)(2,1)S(1)}, u32[]{:S(2)}) copy-start(bf16[256,384]{1,0:T(8,128)(2,1)S(1)} %collective-permute-done.4.refs_2_) | copy-start | bytes 589828
  22.7 22.9 %copy-start.3 = (bf16[768,384]{1,0:T(8,128)(2,1)}, bf16[768,384]{1,0:T(8,128)(2,1)S(1)}, u32[]{:S(2)}) copy-start(bf16[768,384]{1,0:T(8,128)(2,1)S(1)} %pack.1.refs_1_) | copy-start | bytes 1769476
  22.7 16.5 %collective-permute-start.5 = (bf16[768,384]{1,0:T(8,128)(2,1)S(1)}, bf16[768,384]{1,0:T(8,128)(2,1)S(1)}, u32[]{:S(2)}, u32[]{:S(2)}) collective-permute-start(bf16[768,384]{1,0:T(8,128)(2,1)S(1)} %pack.1.refs_1_), channel_id=1, source_target_pairs={{0,2},{2,0},{1,3},{3,1},{4,6},{6,4},{5,7},{7,5},{8,10},{10,8},{9,1... | collective-permute-start | bytes 1769480 | tf_op jit(solution)/shard_map/ppermute | solution.py:316
  23.3 16.0 %collective-permute-start.6 = (bf16[768,384]{1,0:T(8,128)(2,1)S(1)}, bf16[768,384]{1,0:T(8,128)(2,1)}, u32[]{:S(2)}, u32[]{:S(2)}) collective-permute-start(bf16[768,384]{1,0:T(8,128)(2,1)S(1)} %pack.1.refs_1_), channel_id=1, source_target_pairs={{0,1},{1,0},{2,3},{3,2},{4,5},{5,4},{6,7},{7,6},{8,9},{9,8},{10,11... | collective-permute-start | bytes 1769480 | tf_op jit(solution)/shard_map/ppermute | solution.py:316
  25.1 8.0 %collective-permute-start.7 = (bf16[384,256]{1,0:T(8,128)(2,1)}, bf16[384,256]{1,0:T(8,128)(2,1)S(1)}, u32[]{:S(2)}, u32[]{:S(2)}) collective-permute-start(bf16[384,256]{1,0:T(8,128)(2,1)} %get-tuple-element.106), channel_id=1, source_target_pairs={{0,4},{4,8},{8,12},{12,0},{1,5},{5,9},{9,13},{13,1},{2,6},{6,10},{... | collective-permute-start | bytes 589832 | tf_op jit(solution)/shard_map/ppermute | solution.py:316
  26.2 11.6 %collective-permute-start.8 = (bf16[384,256]{1,0:T(8,128)(2,1)}, bf16[384,256]{1,0:T(8,128)(2,1)S(1)}, u32[]{:S(2)}, u32[]{:S(2)}) collective-permute-start(bf16[384,256]{1,0:T(8,128)(2,1)} %get-tuple-element.107), channel_id=1, source_target_pairs={{0,8},{4,12},{8,0},{12,4},{1,9},{5,13},{9,1},{13,5},{2,10},{6,14},... | collective-permute-start | bytes 589832 | tf_op jit(solution)/shard_map/ppermute | solution.py:316
  28.3 9.5 %collective-permute-start.9 = (bf16[384,256]{1,0:T(8,128)(2,1)}, bf16[384,256]{1,0:T(8,128)(2,1)S(1)}, u32[]{:S(2)}, u32[]{:S(2)}) collective-permute-start(bf16[384,256]{1,0:T(8,128)(2,1)} %get-tuple-element.108), channel_id=1, source_target_pairs={{0,12},{4,0},{8,4},{12,8},{1,13},{5,1},{9,5},{13,9},{2,14},{6,2},{... | collective-permute-start | bytes 589832 | tf_op jit(solution)/shard_map/ppermute | solution.py:316
  33.1 6.2 %copy-start.21 = (bf16[384,256]{1,0:T(8,128)(2,1)}, bf16[384,256]{1,0:T(8,128)(2,1)S(1)}, u32[]{:S(2)}) copy-start(bf16[384,256]{1,0:T(8,128)(2,1)S(1)} %collective-permute-done.7.refs_9_) | copy-start | bytes 589828
  39.2 6.4 %copy-start.18 = (bf16[768,384]{1,0:T(8,128)(2,1)}, bf16[768,384]{1,0:T(8,128)(2,1)S(1)}, u32[]{:S(2)}) copy-start(bf16[768,384]{1,0:T(8,128)(2,1)S(1)} %collective-permute-done.5.refs_5_) | copy-start | bytes 1769476
  39.3 6.3 %collective-permute-start.12 = (bf16[256,1536]{1,0:T(8,128)(2,1)S(1)}, bf16[256,1536]{1,0:T(8,128)(2,1)S(1)}, u32[]{:S(2)}, u32[]{:S(2)}) collective-permute-start(bf16[256,1536]{1,0:T(8,128)(2,1)S(1)} %bitcast.9), channel_id=1, source_target_pairs={{0,1},{1,0},{2,3},{3,2},{4,5},{5,4},{6,7},{7,6},{8,9},{9,8},{10,11... | collective-permute-start | bytes 2359304 | tf_op jit(solution)/shard_map/ppermute | solution.py:316
  40.1 24.7 %collective-permute-start.13 = (bf16[256,1536]{1,0:T(8,128)(2,1)S(1)}, bf16[256,1536]{1,0:T(8,128)(2,1)S(1)}, u32[]{:S(2)}, u32[]{:S(2)}) collective-permute-start(bf16[256,1536]{1,0:T(8,128)(2,1)S(1)} %bitcast.10), channel_id=1, source_target_pairs={{0,4},{4,8},{8,12},{12,0},{1,5},{5,9},{9,13},{13,1},{2,6},{6,10},{... | collective-permute-start | bytes 2359304 | tf_op jit(solution)/shard_map/ppermute | solution.py:316
  40.9 24.0 %collective-permute-start.14 = (bf16[256,1536]{1,0:T(8,128)(2,1)S(1)}, bf16[256,1536]{1,0:T(8,128)(2,1)}, u32[]{:S(2)}, u32[]{:S(2)}) collective-permute-start(bf16[256,1536]{1,0:T(8,128)(2,1)S(1)} %bitcast.11), channel_id=1, source_target_pairs={{0,12},{4,0},{8,4},{12,8},{1,13},{5,1},{9,5},{13,9},{2,14},{6,2},{... | collective-permute-start | bytes 2359304 | tf_op jit(solution)/shard_map/ppermute | solution.py:316
  42.8 2.8 %collective-permute-start.10 = (bf16[768,384]{1,0:T(8,128)(2,1)S(1)}, bf16[768,384]{1,0:T(8,128)(2,1)}, u32[]{:S(2)}, u32[]{:S(2)}) collective-permute-start(bf16[768,384]{1,0:T(8,128)(2,1)S(1)} %collective-permute-done.5.refs_5_), channel_id=1, source_target_pairs={{0,1},{1,0},{2,3},{3,2},{4,5},{5,4},{6,7},{7,6},{8,9},{9,8},{10,11... | collective-permute-start | bytes 1769480 | tf_op jit(solution)/shard_map/ppermute | solution.py:316
  43.5 2.1 %collective-permute-start.11 = (bf16[256,384]{1,0:T(8,128)(2,1)}, bf16[256,384]{1,0:T(8,128)(2,1)}, u32[]{:S(2)}, u32[]{:S(2)}) collective-permute-start(bf16[256,384]{1,0:T(8,128)(2,1)} %collective-permute-done.3.refs_4_), channel_id=1, source_target_pairs={{0,1},{1,0},{2,3},{3,2},{4,5},{5,4},{6,7},{7,6},{8,9},{9,8},{10,11... | collective-permute-start | bytes 589832 | tf_op jit(solution)/shard_map/ppermute | solution.py:316
  45.6 24.4 %copy-start.13 = (bf16[256,1536]{1,0:T(8,128)(2,1)}, bf16[256,1536]{1,0:T(8,128)(2,1)S(1)}, u32[]{:S(2)}) copy-start(bf16[256,1536]{1,0:T(8,128)(2,1)S(1)} %collective-permute-done.12.refs_4_) | copy-start | bytes 2359300
  64.8 27.9 %copy-start.4 = (bf16[384,1024]{1,0:T(8,128)(2,1)S(1)}, bf16[384,1024]{1,0:T(8,128)(2,1)}, u32[]{:S(2)}) copy-start(bf16[384,1024]{1,0:T(8,128)(2,1)} %get-tuple-element.131.a) | copy-start | bytes 2359300
  64.9 26.3 %copy-start.14 = (bf16[256,1536]{1,0:T(8,128)(2,1)}, bf16[256,1536]{1,0:T(8,128)(2,1)S(1)}, u32[]{:S(2)}) copy-start(bf16[256,1536]{1,0:T(8,128)(2,1)S(1)} %collective-permute-done.13.refs_1_) | copy-start | bytes 2359300
  64.9 2.6 %collective-permute-start.15 = (bf16[384,1024]{1,0:T(8,128)(2,1)}, bf16[384,1024]{1,0:T(8,128)(2,1)S(1)}, u32[]{:S(2)}, u32[]{:S(2)}) collective-permute-start(bf16[384,1024]{1,0:T(8,128)(2,1)} %get-tuple-element.133), channel_id=1, source_target_pairs={{0,1},{1,0},{2,3},{3,2},{4,5},{5,4},{6,7},{7,6},{8,9},{9,8},{10,11... | collective-permute-start | bytes 2359304 | tf_op jit(solution)/shard_map/ppermute | solution.py:316
  65.3 3.3 %collective-permute-start.16 = (bf16[384,1024]{1,0:T(8,128)(2,1)}, bf16[384,1024]{1,0:T(8,128)(2,1)S(1)}, u32[]{:S(2)}, u32[]{:S(2)}) collective-permute-start(bf16[384,1024]{1,0:T(8,128)(2,1)} %get-tuple-element.134), channel_id=1, source_target_pairs={{0,1},{1,0},{2,3},{3,2},{4,5},{5,4},{6,7},{7,6},{8,9},{9,8},{10,11... | collective-permute-start | bytes 2359304 | tf_op jit(solution)/shard_map/ppermute | solution.py:316
  69.7 23.0 %copy-start.8 = (bf16[192,256]{1,0:T(8,128)(2,1)S(1)}, bf16[192,256]{1,0:T(8,128)(2,1)}, u32[]{:S(2)}) copy-start(bf16[192,256]{1,0:T(8,128)(2,1)} %get-tuple-element.148.refs_0_) | copy-start | bytes 294916
  69.7 23.0 %copy-start.9 = (bf16[192,256]{1,0:T(8,128)(2,1)S(1)}, bf16[192,256]{1,0:T(8,128)(2,1)}, u32[]{:S(2)}) copy-start(bf16[192,256]{1,0:T(8,128)(2,1)} %get-tuple-element.149.refs_1_) | copy-start | bytes 294916
  69.7 23.0 %copy-start.10 = (bf16[192,256]{1,0:T(8,128)(2,1)S(1)}, bf16[192,256]{1,0:T(8,128)(2,1)}, u32[]{:S(2)}) copy-start(bf16[192,256]{1,0:T(8,128)(2,1)} %get-tuple-element.150.refs_2_) | copy-start | bytes 294916
  69.7 23.0 %copy-start.11 = (bf16[192,256]{1,0:T(8,128)(2,1)S(1)}, bf16[192,256]{1,0:T(8,128)(2,1)}, u32[]{:S(2)}) copy-start(bf16[192,256]{1,0:T(8,128)(2,1)} %get-tuple-element.151.refs_3_) | copy-start | bytes 294916
  69.9 4.2 %collective-permute-start.18 = (bf16[256,1536]{1,0:T(8,128)(2,1)S(1)}, bf16[256,1536]{1,0:T(8,128)(2,1)S(1)}, u32[]{:S(2)}, u32[]{:S(2)}) collective-permute-start(bf16[256,1536]{1,0:T(8,128)(2,1)S(1)} %collective-permute-done.13.refs_1_), channel_id=1, source_target_pairs={{0,1},{1,0},{2,3},{3,2},{4,5},{5,4},{6,7},{7,6},{8,9},{9,8},{10,11... | collective-permute-start | bytes 2359304 | tf_op jit(solution)/shard_map/ppermute | solution.py:316
  70.3 3.8 %collective-permute-start.19 = (bf16[256,1536]{1,0:T(8,128)(2,1)}, bf16[256,1536]{1,0:T(8,128)(2,1)S(1)}, u32[]{:S(2)}, u32[]{:S(2)}) collective-permute-start(bf16[256,1536]{1,0:T(8,128)(2,1)} %collective-permute-done.14.refs_3_), channel_id=1, source_target_pairs={{0,1},{1,0},{2,3},{3,2},{4,5},{5,4},{6,7},{7,6},{8,9},{9,8},{10,11... | collective-permute-start | bytes 2359304 | tf_op jit(solution)/shard_map/ppermute | solution.py:316
  70.5 20.5 %collective-permute-start.17 = (bf16[384,1024]{1,0:T(8,128)(2,1)S(1)}, bf16[384,1024]{1,0:T(8,128)(2,1)S(1)}, u32[]{:S(2)}, u32[]{:S(2)}) collective-permute-start(bf16[384,1024]{1,0:T(8,128)(2,1)S(1)} %add.1), channel_id=1, source_target_pairs={{0,2},{2,0},{1,3},{3,1},{4,6},{6,4},{5,7},{7,5},{8,10},{10,8},{9,1... | collective-permute-start | bytes 2359304 | tf_op jit(solution)/shard_map/ppermute | solution.py:316
  71.1 20.1 %collective-permute-start.22 = (bf16[256,1536]{1,0:T(8,128)(2,1)S(1)}, bf16[256,1536]{1,0:T(8,128)(2,1)}, u32[]{:S(2)}, u32[]{:S(2)}) collective-permute-start(bf16[256,1536]{1,0:T(8,128)(2,1)S(1)} %bitcast.12), channel_id=1, source_target_pairs={{0,8},{4,12},{8,0},{12,4},{1,9},{5,13},{9,1},{13,5},{2,10},{6,14},... | collective-permute-start | bytes 2359304 | tf_op jit(solution)/shard_map/ppermute | solution.py:316
  72.1 2.0 %collective-permute-start.20 = (bf16[96,1024]{1,0:T(8,128)(2,1)S(1)}, bf16[96,1024]{1,0:T(8,128)(2,1)S(1)}, u32[]{:S(2)}, u32[]{:S(2)}) collective-permute-start(bf16[96,1024]{1,0:T(8,128)(2,1)S(1)} %copy-done.25), channel_id=1, source_target_pairs={{0,1},{1,0},{2,3},{3,2},{4,5},{5,4},{6,7},{7,6},{8,9},{9,8},{10,11... | collective-permute-start | bytes 589832 | tf_op jit(solution)/shard_map/ppermute | solution.py:316
  74.1 23.2 %copy-start.24 = (bf16[96,1024]{1,0:T(8,128)(2,1)}, bf16[96,1024]{1,0:T(8,128)(2,1)S(1)}, u32[]{:S(2)}) copy-start(bf16[96,1024]{1,0:T(8,128)(2,1)S(1)} %collective-permute-done.20.q1) | copy-start | bytes 589828
  74.1 17.1 %copy-start.15 = (bf16[256,1536]{1,0:T(8,128)(2,1)}, bf16[256,1536]{1,0:T(8,128)(2,1)S(1)}, u32[]{:S(2)}) copy-start(bf16[256,1536]{1,0:T(8,128)(2,1)S(1)} %collective-permute-done.18.refs_5_) | copy-start | bytes 2359300
  74.1 17.1 %copy-start.16 = (bf16[256,1536]{1,0:T(8,128)(2,1)}, bf16[256,1536]{1,0:T(8,128)(2,1)S(1)}, u32[]{:S(2)}) copy-start(bf16[256,1536]{1,0:T(8,128)(2,1)S(1)} %collective-permute-done.19.refs_7_) | copy-start | bytes 2359300
  91.2 6.1 %collective-permute-start.23 = (bf16[256,1536]{1,0:T(8,128)(2,1)}, bf16[256,1536]{1,0:T(8,128)(2,1)S(1)}, u32[]{:S(2)}, u32[]{:S(2)}) collective-permute-start(bf16[256,1536]{1,0:T(8,128)(2,1)} %collective-permute-done.22.refs_2_), channel_id=1, source_target_pairs={{0,1},{1,0},{2,3},{3,2},{4,5},{5,4},{6,7},{7,6},{8,9},{9,8},{10,11... | collective-permute-start | bytes 2359304 | tf_op jit(solution)/shard_map/ppermute | solution.py:316
  94.6 2.7 %collective-permute-start.21 = (bf16[192,1024]{1,0:T(8,128)(2,1)S(1)}, bf16[192,1024]{1,0:T(8,128)(2,1)S(1)}, u32[]{:S(2)}, u32[]{:S(2)}) collective-permute-start(bf16[192,1024]{1,0:T(8,128)(2,1)S(1)} %get-tuple-element.153), channel_id=1, source_target_pairs={{0,1},{1,0},{2,3},{3,2},{4,5},{5,4},{6,7},{7,6},{8,9},{9,8},{10,11... | collective-permute-start | bytes 1179656 | tf_op jit(solution)/shard_map/ppermute | solution.py:316
  94.6 10.4 %collective-permute-start.24 = (bf16[576,256]{1,0:T(8,128)(2,1)}, bf16[576,256]{1,0:T(8,128)(2,1)S(1)}, u32[]{:S(2)}, u32[]{:S(2)}) collective-permute-start(bf16[576,256]{1,0:T(8,128)(2,1)} %get-tuple-element.165), channel_id=1, source_target_pairs={{0,8},{4,12},{8,0},{12,4},{1,9},{5,13},{9,1},{13,5},{2,10},{6,14},... | collective-permute-start | bytes 884744 | tf_op jit(solution)/shard_map/ppermute | solution.py:316
  95.7 14.4 %collective-permute-start.28 = (bf16[576,256]{1,0:T(8,128)(2,1)}, bf16[576,256]{1,0:T(8,128)(2,1)S(1)}, u32[]{:S(2)}, u32[]{:S(2)}) collective-permute-start(bf16[576,256]{1,0:T(8,128)(2,1)} %get-tuple-element.171), channel_id=1, source_target_pairs={{0,12},{4,0},{8,4},{12,8},{1,13},{5,1},{9,5},{13,9},{2,14},{6,2},{... | collective-permute-start | bytes 884744 | tf_op jit(solution)/shard_map/ppermute | solution.py:316
  97.3 14.3 %collective-permute-start.29 = (bf16[576,256]{1,0:T(8,128)(2,1)S(1)}, bf16[576,256]{1,0:T(8,128)(2,1)S(1)}, u32[]{:S(2)}, u32[]{:S(2)}) collective-permute-start(bf16[576,256]{1,0:T(8,128)(2,1)S(1)} %get-tuple-element.173), channel_id=1, source_target_pairs={{0,4},{4,8},{8,12},{12,0},{1,5},{5,9},{9,13},{13,1},{2,6},{6,10},{... | collective-permute-start | bytes 884744 | tf_op jit(solution)/shard_map/ppermute | solution.py:316
  98.3 13.3 %copy-start = (bf16[1536,768]{1,0:T(8,128)(2,1)S(1)}, bf16[1536,768]{1,0:T(8,128)(2,1)}, u32[]{:S(2)}) copy-start(bf16[1536,768]{1,0:T(8,128)(2,1)} %refs_5_.1) | copy-start | bytes 7077892
  98.3 13.3 %copy-start.1 = (bf16[1536,768]{1,0:T(8,128)(2,1)S(1)}, bf16[1536,768]{1,0:T(8,128)(2,1)}, u32[]{:S(2)}) copy-start(bf16[1536,768]{1,0:T(8,128)(2,1)} %refs_6_.1) | copy-start | bytes 7077892
  105.0 12.3 %collective-permute-start.25 = (bf16[288,384]{1,0:T(8,128)(2,1)}, bf16[288,384]{1,0:T(8,128)(2,1)S(1)}, u32[]{:S(2)}, u32[]{:S(2)}) collective-permute-start(bf16[288,384]{1,0:T(8,128)(2,1)} %get-tuple-element.167), channel_id=1, source_target_pairs={{0,32},{32,64},{64,96},{96,0},{1,33},{33,65},{65,97},{97,1},{2,34}... | collective-permute-start | bytes 663560 | tf_op jit(solution)/shard_map/ppermute | solution.py:316
  106.4 11.3 %collective-permute-start.26 = (bf16[288,384]{1,0:T(8,128)(2,1)}, bf16[288,384]{1,0:T(8,128)(2,1)S(1)}, u32[]{:S(2)}, u32[]{:S(2)}) collective-permute-start(bf16[288,384]{1,0:T(8,128)(2,1)} %get-tuple-element.168), channel_id=1, source_target_pairs={{0,64},{32,96},{64,0},{96,32},{1,65},{33,97},{65,1},{97,33},{2,66}... | collective-permute-start | bytes 663560 | tf_op jit(solution)/shard_map/ppermute | solution.py:316
  109.0 8.7 %collective-permute-start.27 = (bf16[288,384]{1,0:T(8,128)(2,1)}, bf16[288,384]{1,0:T(8,128)(2,1)S(1)}, u32[]{:S(2)}, u32[]{:S(2)}) collective-permute-start(bf16[288,384]{1,0:T(8,128)(2,1)} %get-tuple-element.169), channel_id=1, source_target_pairs={{0,96},{32,0},{64,32},{96,64},{1,97},{33,1},{65,33},{97,65},{2,98}... | collective-permute-start | bytes 663560 | tf_op jit(solution)/shard_map/ppermute | solution.py:316
  113.3 4.5 %copy-start.7 = (bf16[288,384]{1,0:T(8,128)(2,1)S(1)}, bf16[288,384]{1,0:T(8,128)(2,1)}, u32[]{:S(2)}) copy-start(bf16[288,384]{1,0:T(8,128)(2,1)} %get-tuple-element.175.a) | copy-start | bytes 663556
  (8 other events, 10.6 us)
